TPU v7x, 32 devices: a whole 2x2x4 slice. The times are simulated.
32 devices in a mesh: az: 4 (over y, x), rad: 8 (over z, core).
Axes of the slice: x: 2, y: 2, z: 4, core: 2. Of those that a mesh axis runs over, the one named last changes fastest.
Arguments:
- source_field: float32 [4096, 32, 128], P('az', 'rad'), may hold values from -6 to 6
- helmholtz: float32 [32], replicated, may hold values from 0.01 to 0.05
- azimuth_coef: float32 [32], replicated, may hold values from 0.2 to 0.5
- vertical_coef: float32 [32], replicated, may hold values from 1 to 4
- radial_coef: float32 [32], replicated, may hold values from 0.5 to 5
Outputs:
- pressure: float32 [4096, 32, 128], P('az', 'rad')
All inputs are finite; a program needn't handle non-finite values.
Results may differ from a plain program's by a relative error of at most 0.00012.
Values sent between devices are 32-bit elements; how exact they have to be, the bound alone decides.
No kernel may reach another device: no remote copies, remote signals or barrier semaphores. Data moves between devices by JAX's collectives and lax.ppermute only.
A program may use at most 128 MiB of HBM per device.

v0:
```python
import math

import jax
import jax.numpy as jnp
from jax import lax
from jax.sharding import PartitionSpec as P


def partner_2(block, axis, distance):
    count = lax.axis_size(axis)
    route = []
    for low in range(count):
        high = low | 1 << distance
        if high != low and high < count:
            route += [(low, high), (high, low)]
    return lax.ppermute(block, axis, route)


def cosine_matrix(depth):
    row_ids = jnp.arange(depth, dtype=jnp.int32)
    phases = (2 * row_ids[:, None] + 1) * row_ids[None, :] % (4 * depth)
    angles = math.pi / (2 * depth) * phases.astype(jnp.float32)
    scales = jnp.where(row_ids == 0, math.sqrt(1.0 / depth), math.sqrt(2.0 / depth)).astype(
        jnp.float32
    )
    return jnp.cos(angles) * scales[None, :]


def contract(pattern, matrix, values):
    return jnp.einsum(pattern, matrix, values, precision=lax.Precision.HIGHEST)


def dft_table(points, orient):
    row_ids = jnp.arange(points, dtype=jnp.int32)
    phases = row_ids[:, None] * row_ids[None, :] % points
    angles = orient * 2.0 * math.pi / points * phases.astype(jnp.float32)
    return (jnp.cos(angles), jnp.sin(angles))


def apply_table(cosine, sine, real_part, imag_part, pattern):
    new_real = contract(pattern, cosine, real_part) - contract(pattern, sine, imag_part)
    new_imag = contract(pattern, cosine, imag_part) + contract(pattern, sine, real_part)
    return (new_real, new_imag)


def complex_dft(real_part, imag_part, orient):
    length = real_part.shape[0]
    trailing = real_part.shape[1:]
    bit_count = length.bit_length() - 1
    outer_size = 2 ** (bit_count // 2)
    inner_size = length // outer_size
    shaped_real = real_part.reshape((outer_size, inner_size) + trailing)
    shaped_imag = imag_part.reshape((outer_size, inner_size) + trailing)
    outer_cos, outer_sin = dft_table(outer_size, orient)
    first_real, first_imag = apply_table(
        outer_cos, outer_sin, shaped_real, shaped_imag, "pu,pq...->uq..."
    )
    outer_ids = jnp.arange(outer_size, dtype=jnp.int32)[:, None]
    inner_ids = jnp.arange(inner_size, dtype=jnp.int32)[None, :]
    twist = orient * 2.0 * math.pi / length * (outer_ids * inner_ids % length).astype(jnp.float32)
    twist = twist.reshape((outer_size, inner_size) + (1,) * len(trailing))
    twist_cos = jnp.cos(twist)
    twist_sin = jnp.sin(twist)
    middle_real = first_real * twist_cos - first_imag * twist_sin
    middle_imag = first_real * twist_sin + first_imag * twist_cos
    inner_cos, inner_sin = dft_table(inner_size, orient)
    last_real, last_imag = apply_table(
        inner_cos, inner_sin, middle_real, middle_imag, "qv,uq...->vu..."
    )
    return (last_real.reshape((length,) + trailing), last_imag.reshape((length,) + trailing))


def rotate(stacked, angles):
    cosine = jnp.cos(angles)
    sine = jnp.sin(angles)
    return jnp.stack(
        [stacked[0] * cosine - stacked[1] * sine, stacked[0] * sine + stacked[1] * cosine]
    )


def combine(own_part, partner, digit):
    return jnp.where(digit == 0, own_part + partner, partner - own_part)


def pair_real(values, bit_index):
    return partner_2(values, "az", bit_index)


def pair_complex(values, bit_index):
    return partner_2(values, "az", bit_index)


def from_below(values, stride, filler):
    block = jnp.full(values.shape[:-2] + (stride,) + values.shape[-1:], filler, values.dtype)
    return jnp.concatenate([block, values[..., :-stride, :]], axis=-2)


def from_above(values, stride, filler):
    block = jnp.full(values.shape[:-2] + (stride,) + values.shape[-1:], filler, values.dtype)
    return jnp.concatenate([values[..., stride:, :], block], axis=-2)


def mode_solve(stacked, mode_ids, total_az, helmholtz, azimuth_coef, vertical_coef, radial_coef):
    total_rad = stacked.shape[2]
    depth = stacked.shape[3]
    azim_eig = 2.0 - 2.0 * jnp.cos(2.0 * math.pi / total_az * mode_ids.astype(jnp.float32))
    level_ids = jnp.arange(depth, dtype=jnp.int32)
    vert_eig = 2.0 - 2.0 * jnp.cos(math.pi / depth * level_ids.astype(jnp.float32))
    radius = jnp.arange(total_rad, dtype=jnp.int32)
    coupling = jnp.where(radius < total_rad - 1, radial_coef, jnp.zeros_like(radial_coef))
    previous = jnp.concatenate([jnp.zeros((1,), jnp.float32), coupling[:-1]])
    diagonal = (
        (helmholtz + coupling + previous)[None, :, None]
        + azim_eig[:, None, None] * azimuth_coef[None, :, None]
        + vert_eig[None, None, :] * vertical_coef[None, :, None]
    )
    lower = jnp.broadcast_to((-previous)[None, :, None], diagonal.shape)
    upper = jnp.broadcast_to((-coupling)[None, :, None], diagonal.shape)
    right_side = stacked
    for level in range((total_rad - 1).bit_length()):
        stride = 2**level
        lower_factor = -lower / from_below(diagonal, stride, 1.0)
        upper_factor = -upper / from_above(diagonal, stride, 1.0)
        new_diagonal = (
            diagonal
            + lower_factor * from_below(upper, stride, 0.0)
            + upper_factor * from_above(lower, stride, 0.0)
        )
        right_side = (
            right_side
            + lower_factor * from_below(right_side, stride, 0.0)
            + upper_factor * from_above(right_side, stride, 0.0)
        )
        lower = lower_factor * from_below(lower, stride, 0.0)
        upper = upper_factor * from_above(upper, stride, 0.0)
        diagonal = new_diagonal
    return right_side / diagonal


def on_device(source_field, helmholtz, azimuth_coef, vertical_coef, radial_coef):
    local_len, rad_local, depth = source_field.shape
    az_count = lax.axis_size("az")
    az_index = lax.axis_index("az")
    rad_index = lax.axis_index("rad")
    total_az = local_len * az_count
    basis = cosine_matrix(depth)
    layered = jnp.matmul(source_field, basis, precision=lax.Precision.HIGHEST)
    bit_count = az_count.bit_length() - 1
    top_bit = bit_count - 1
    digit = az_index // 2**top_bit % 2
    mixed = combine(layered, pair_real(layered, top_bit), digit)
    lower_part = az_index % 2**top_bit
    angles = -2.0 * math.pi / az_count * (lower_part * digit).astype(jnp.float32)
    stacked = jnp.stack([mixed * jnp.cos(angles), mixed * jnp.sin(angles)])
    section = 1
    bit_index = bit_count - 1 - section
    digit = az_index // 2**bit_index % 2
    stacked = combine(stacked, pair_complex(stacked, bit_index), digit)
    own_mode = jnp.zeros((), jnp.int32)
    for place in range(bit_count):
        own_mode = own_mode + az_index // 2**place % 2 * 2 ** (bit_count - 1 - place)
    positions = jnp.arange(local_len, dtype=jnp.int32)
    phases = (positions * own_mode % total_az).astype(jnp.float32)
    stacked = rotate(stacked, (-2.0 * math.pi / total_az * phases)[:, None, None])
    spec_real, spec_imag = complex_dft(stacked[0], stacked[1], -1.0)
    modes = lax.all_to_all(
        jnp.stack([spec_real, spec_imag]), "rad", split_axis=1, concat_axis=2, tiled=True
    )
    group = modes.shape[1]
    mode_ids = own_mode + az_count * (rad_index * group + jnp.arange(group, dtype=jnp.int32))
    solved = mode_solve(
        modes, mode_ids, total_az, helmholtz, azimuth_coef, vertical_coef, radial_coef
    )
    returned = lax.all_to_all(solved, "rad", split_axis=2, concat_axis=1, tiled=True)
    back_real, back_imag = complex_dft(returned[0], returned[1], 1.0)
    stacked = rotate(
        jnp.stack([back_real, back_imag]), (2.0 * math.pi / total_az * phases)[:, None, None]
    )
    section = 1
    bit_index = bit_count - 1 - section
    digit = az_index // 2**bit_index % 2
    stacked = combine(stacked, pair_complex(stacked, bit_index), digit)
    digit = az_index // 2**top_bit % 2
    lower_part = az_index % 2**top_bit
    angles = 2.0 * math.pi / az_count * (lower_part * digit).astype(jnp.float32)
    real_only = stacked[0] * jnp.cos(angles) - stacked[1] * jnp.sin(angles)
    slab = combine(real_only, pair_real(real_only, top_bit), digit) * (1.0 / total_az)
    return jnp.matmul(slab, basis.T, precision=lax.Precision.HIGHEST)


def solution(mesh):
    in_specs = (P("az", "rad", None), P(), P(), P(), P())
    out_specs = P("az", "rad", None)
    return jax.shard_map(
        on_device, mesh=mesh, in_specs=in_specs, out_specs=out_specs, check_vma=False
    )
```

profile of v0, /device:TPU:0, one launch (start us, length us, event | category | flops | bytes accessed | tf_op | source)
XLA Modules:
  0.0 652.6 jit_solution(18217309531003166243)
XLA Ops:
  0.0 1.6 copy-done
  1.6 3.5 fusion.65
  5.1 3.0 collective-permute-start
  8.3 45.8 %collective-permute-done = f32[1024,4,128]{0,2,1:T(8,128)} collective-permute-done((f32[1024,4,128]{0,2,1:T(8,128)}, f32[1024,4,128]{0,2,1:T(8,128)}, u32[]{:S(2)}, u32[]{:S(2)}) %collective-permute-start) | collective-permute-done | bytes 2097184 | tf_op jit(solution)/shard_map/ppermute | solution.py:16
  54.1 2.9 multiply_bitcast_fusion.1
  57.1 2.8 pad_maximum_fusion
  60.3 1.7 collective-permute-start.1
  64.2 2.6 broadcast_multiply_fusion.1
  66.8 2.4 fusion.251
  69.2 2.5 fusion.252
  71.6 80.7 %collective-permute-done.1 = f32[2,1024,4,128]{1,3,2,0:T(8,128)} collective-permute-done((f32[2,1024,4,128]{1,3,2,0:T(8,128)}, f32[2,1024,4,128]{1,3,2,0:T(8,128)}, u32[]{:S(2)}, u32[]{:S(2)}) %collective-permute-start.1) | collective-permute-done | bytes 4194336 | tf_op jit(solution)/shard_map/ppermute | solution.py:16
  152.4 3.2 subtract_select_fusion.1
  155.5 2.3 fusion.243
  157.9 2.9 copy.94
  160.8 3.1 copy.96
  163.8 3.2 multiply_subtract_fusion.3
  167.0 3.7 fusion.35
  170.7 3.7 fusion.33
  174.4 3.7 fusion.41
  178.1 4.6 multiply_subtract_fusion.2
  182.7 3.7 fusion.27
  186.4 3.7 fusion.25
  190.1 3.9 fusion.47
  194.0 1.2 copy.104
  195.2 3.7 fusion.50
  200.5 4.7 copy.108
  205.2 4.8 all-to-all-start
  212.8 4.0 pad_multiply_fusion.4
  227.3 3.4 multiply_add_fusion.6
  230.7 73.4 %all-to-all-done = f32[2,1024,4,128]{3,2,0,1:T(4,128)} async-done(((f32[2,1024,4,128]{3,2,0,1:T(4,128)}), f32[2,1024,4,128]{3,2,0,1:T(4,128)}, u32[]{:S(2)}, u32[]{:S(2)}) %all-to-all-start) | async-done | bytes 4194336 | tf_op jit(solution)/shard_map/all_to_all | solution.py:166
  304.1 3.0 copy.109
  307.6 4.2 fusion.242
  311.9 5.9 multiply_add_fusion.3
  317.8 4.5 fusion.241
  322.3 5.8 multiply_add_fusion.2
  328.1 3.8 fusion.240
  332.0 5.6 multiply_add_fusion.1
  337.6 3.4 fusion.239
  341.0 5.2 multiply_add_fusion
  349.0 1.7 add_divide_fusion
  350.7 2.3 copy.111
  353.0 4.8 all-to-all-start.1
  357.9 93.7 %all-to-all-done.1 = f32[2,128,32,128]{3,1,0,2:T(8,128)} async-done(((f32[2,128,32,128]{3,1,0,2:T(8,128)}), f32[2,128,32,128]{3,1,0,2:T(8,128)}, u32[]{:S(2)}, u32[]{:S(2)}) %all-to-all-start.1) | async-done | bytes 4194336 | tf_op jit(solution)/shard_map/all_to_all | solution.py:174
  451.6 2.5 copy.112
  454.7 3.7 fusion.19
  458.4 3.7 fusion.17
  462.3 3.7 fusion.53
  466.0 4.4 multiply_subtract_fusion.1
  470.4 3.7 fusion.11
  474.1 5.0 fusion.9
  479.0 4.1 fusion.59
  483.1 2.5 copy.121
  485.7 2.9 copy.122
  488.6 5.3 fusion.62
  495.2 2.0 copy.126
  497.1 3.0 multiply_subtract_fusion
  500.1 2.7 pad_maximum_fusion.2
  502.8 1.5 collective-permute-start.2
  504.4 90.8 %collective-permute-done.2 = f32[2,1024,4,128]{1,3,2,0:T(8,128)} collective-permute-done((f32[2,1024,4,128]{1,3,2,0:T(8,128)}, f32[2,1024,4,128]{1,3,2,0:T(8,128)}, u32[]{:S(2)}, u32[]{:S(2)}) %collective-permute-start.2) | collective-permute-done | bytes 4194336 | tf_op jit(solution)/shard_map/ppermute | solution.py:16
  595.2 3.8 subtract_select_fusion
  599.6 1.6 collective-permute-start.3
  601.1 44.8 %collective-permute-done.3 = f32[1024,4,128]{0,2,1:T(8,128)S(1)} collective-permute-done((f32[1024,4,128]{0,2,1:T(8,128)S(1)}, f32[1024,4,128]{0,2,1:T(8,128)S(1)}, u32[]{:S(2)}, u32[]{:S(2)}) %collective-permute-start.3) | collective-permute-done | bytes 2097184 | tf_op jit(solution)/shard_map/ppermute | solution.py:16
  645.9 3.8 fusion.4
  649.7 2.7 copy.130
  (119 shorter events, 23.2 us)
Async XLA Ops:
  0.0 1.6 copy-start
  0.0 5.1 copy-start.27
  1.6 3.5 copy-start.29
  5.1 48.9 %collective-permute-start = (f32[1024,4,128]{0,2,1:T(8,128)}, f32[1024,4,128]{0,2,1:T(8,128)}, u32[]{:S(2)}, u32[]{:S(2)}) collective-permute-start(f32[1024,4,128]{0,2,1:T(8,128)} %fusion.65), channel_id=1, source_target_pairs={{0,16},{16,0},{8,24},{24,8},{1,17},{17,1},{9,25},{25,9},{2,18},{18... | collective-permute-start | bytes 6291464 | tf_op jit(solution)/shard_map/ppermute | solution.py:16
  57.0 2.8 copy-start.5
  57.0 3.3 copy-start.7
  57.0 5.0 copy-start.31
  57.0 5.0 copy-start.32
  57.0 5.9 copy-start.33
  57.1 5.9 copy-start.34
  60.3 92.1 %collective-permute-start.1 = (f32[2,1024,4,128]{1,3,2,0:T(8,128)}, f32[2,1024,4,128]{1,3,2,0:T(8,128)}, u32[]{:S(2)}, u32[]{:S(2)}) collective-permute-start(f32[2,1024,4,128]{1,3,2,0:T(8,128)} %pad_maximum_fusion), channel_id=1, source_target_pairs={{0,8},{8,0},{16,24},{24,16},{1,9},{9,1},{17,25},{25,17},{2,10},{10... | collective-permute-start | bytes 12582920 | tf_op jit(solution)/shard_map/ppermute | solution.py:16
  64.2 2.6 copy-start.16
  64.2 2.6 copy-start.18
  69.2 83.2 %copy-start.6 = (f32[1,1024,4,128]{1,3,2,0:T(8,128)S(1)}, f32[1,1024,4,128]{1,3,2,0:T(8,128)}, u32[]{:S(2)}) copy-start(f32[1,1024,4,128]{1,3,2,0:T(8,128)} %copy-done.5) | copy-start | bytes 6291460
  69.2 83.2 %copy-start.8 = (f32[1,1024,4,128]{1,3,2,0:T(8,128)S(1)}, f32[1,1024,4,128]{1,3,2,0:T(8,128)}, u32[]{:S(2)}) copy-start(f32[1,1024,4,128]{1,3,2,0:T(8,128)} %copy-done.7) | copy-start | bytes 6291460
  205.2 98.9 %all-to-all-start = ((f32[2,1024,4,128]{3,2,0,1:T(4,128)}), f32[2,1024,4,128]{3,2,0,1:T(4,128)}, u32[]{:S(2)}, u32[]{:S(2)}) async-start(f32[2,1024,4,128]{3,2,0,1:T(4,128)} %copy.108), calls=%async_computation | async-start | bytes 8388608 | tf_op jit(solution)/shard_map/all_to_all | solution.py:166
  210.0 1.6 copy-start.17
  210.0 2.2 copy-start.19
  210.0 2.8 copy-start.26
  212.8 4.0 copy-start.24
  212.8 4.0 copy-start.25
  216.8 1.6 copy-start.2
  216.8 2.1 copy-start.4
  220.9 1.4 copy-start.9
  221.5 1.8 copy-start.11
  224.6 1.4 copy-start.13
  225.8 1.3 copy-start.15
  307.6 4.3 copy-start.20
  317.8 4.5 copy-start.3
  328.1 3.8 copy-start.10
  337.6 3.4 copy-start.14
  346.1 1.6 copy-start.21
  346.1 2.2 copy-start.22
  346.2 2.8 copy-start.23
  353.0 98.6 %all-to-all-start.1 = ((f32[2,128,32,128]{3,1,0,2:T(8,128)}), f32[2,128,32,128]{3,1,0,2:T(8,128)}, u32[]{:S(2)}, u32[]{:S(2)}) async-start(f32[2,128,32,128]{3,1,0,2:T(8,128)} %copy.111), calls=%async_computation.1 | async-start | bytes 8388608 | tf_op jit(solution)/shard_map/all_to_all | solution.py:174
  500.1 2.7 copy-start.12
  502.8 92.4 %collective-permute-start.2 = (f32[2,1024,4,128]{1,3,2,0:T(8,128)}, f32[2,1024,4,128]{1,3,2,0:T(8,128)}, u32[]{:S(2)}, u32[]{:S(2)}) collective-permute-start(f32[2,1024,4,128]{1,3,2,0:T(8,128)} %pad_maximum_fusion.2), channel_id=1, source_target_pairs={{0,8},{8,0},{16,24},{24,16},{1,9},{9,1},{17,25},{25,17},{2,10},{10... | collective-permute-start | bytes 12582920 | tf_op jit(solution)/shard_map/ppermute | solution.py:16
  599.1 46.8 %copy-start.28 = (f32[128]{0:T(128)S(1)}, f32[128]{0:T(128)}, u32[]{:S(2)}) copy-start(f32[128]{0:T(128)} %copy-done.27) | copy-start | bytes 1540
  599.1 46.8 %copy-start.30 = (s32[128]{0:T(128)S(1)}, s32[128]{0:T(128)}, u32[]{:S(2)}) copy-start(s32[128]{0:T(128)} %copy-done.29) | copy-start | bytes 1540
  599.6 46.3 %collective-permute-start.3 = (f32[1024,4,128]{0,2,1:T(8,128)S(1)}, f32[1024,4,128]{0,2,1:T(8,128)S(1)}, u32[]{:S(2)}, u32[]{:S(2)}) collective-permute-start(f32[1024,4,128]{0,2,1:T(8,128)S(1)} %fusion.1), channel_id=1, source_target_pairs={{0,16},{16,0},{8,24},{24,8},{1,17},{17,1},{9,25},{25,9},{2,18},{18... | collective-permute-start | bytes 6291464 | tf_op jit(solution)/shard_map/ppermute | solution.py:16
  645.9 6.5 copy-start.1
where the time goes:
time: 659 us; the launch traced here: 653 us
  waiting for transfers between devices  429 us (65%)
  matrix products  71.5 us (11%)
  local copies, waits for them, and re-layouts  69.8 us (11%)
  other arithmetic  63.6 us (10%)
  starting transfers between devices  17.3 us (3%)
    ppermute x4, waiting for transfers between devices, partner_2(): return lax.ppermute(block, axis, route)  262 us
    all_to_all x1, waiting for transfers between devices, on_device(): lax.all_to_all(solved, 'rad', split_axis=2, concat_axis=1, tiled=True)  93.7 us
    all_to_all x1, waiting for transfers between devices, on_device(): lax.all_to_all(jnp.stack([spec_real, spec_imag]), 'rad', split_axis=1, co...  73.4 us
    dot_general x16, matrix products, contract(): return jnp.einsum(pattern, matrix, values, precision=lax.Precision.HIGHEST)  64.1 us
    add x4, other arithmetic, mode_solve(): right_side + lower_factor * from_below(right_side, stride, 0.0)  22.5 us
    slice x15, local copies, waits for them, and re-layouts, from_below(): return jnp.concatenate([block, values[..., :-stride, :]], axis=-2)  21.3 us
  transfers between devices with their start and end apart: 6, of which 6 were waited for; matrix products, arithmetic and copies ran while one was open for 4% of the time, Pallas kernels for 0%

commit v1 on v0

v1 whole, which is shorter than its diff:
```python
import functools
import math

import jax
import jax.numpy as jnp
import ml_dtypes
import numpy as np
from jax import lax
from jax.experimental import pallas as pl
from jax.experimental.pallas import tpu as pltpu
from jax.sharding import PartitionSpec as P

F32 = jnp.float32
BF16 = jnp.bfloat16
CELLS = 4
SLABS = 4
LANES = 128
VMEM_LIMIT = 56 * 2**20


def two_halves(table):
    high = table.astype(np.float32).astype(ml_dtypes.bfloat16)
    low = (table - high.astype(np.float64)).astype(np.float32).astype(ml_dtypes.bfloat16)
    return high, low


def cosine_basis(depth):
    rows = np.arange(depth)
    phases = (2 * rows[:, None] + 1) * rows[None, :] % (4 * depth)
    scales = np.where(rows == 0, math.sqrt(1.0 / depth), math.sqrt(2.0 / depth))
    return np.cos(math.pi / (2 * depth) * phases) * scales[None, :]


def wide_basis(basis):
    high, low = two_halves(basis)
    top = np.concatenate([high, low], axis=1)
    bottom = np.concatenate([high, np.zeros_like(high)], axis=1)
    return np.concatenate([top, bottom], axis=0)


def slab_tables(length):
    quarter = length // 8
    half = quarter // 2
    offsets = np.arange(quarter) + 0.5
    stage = np.zeros((4, 2 * quarter, 2 * quarter))
    modes = np.zeros((4, 2 * quarter), np.int64)

    def angle(mode):
        return 2 * np.pi * (mode[:, None] * offsets[None, :] % length) / length

    def scale(mode):
        single = (mode == 0) | (mode == length // 2)
        return np.where(single, np.sqrt(1 / length), np.sqrt(2 / length))[:, None]

    steps = np.arange(half)
    for first, mode, column, wave in (
        (0, 8 * steps, 0, np.cos),
        (half, 8 * steps + 4, quarter, np.cos),
        (quarter, 8 * (steps + 1), 0, np.sin),
        (quarter + half, 8 * steps + 4, quarter, np.sin),
    ):
        stage[0, first : first + half, column : column + quarter] = scale(mode) * wave(angle(mode))
        modes[0, first : first + half] = mode
    for slot in (1, 2, 3):
        mode = slot + 8 * np.arange(quarter)
        cosine, sine = scale(mode) * np.cos(angle(mode)), scale(mode) * np.sin(angle(mode))
        stage[slot] = np.block([[cosine, sine], [sine, -cosine]])
        modes[slot] = np.concatenate([mode, mode])
    modes = modes.reshape(-1)
    parity = np.tile(np.repeat([1, -1], quarter), 4)
    single = (modes == 0) | (modes == length // 2)
    size = np.where(single, np.sqrt(1 / length), np.sqrt(2 / length))
    ends = size * np.where(parity > 0, np.cos(np.pi * modes / length), np.sin(np.pi * modes / length))
    eigen = 2.0 - 2.0 * np.cos(2 * np.pi * modes / length)
    return stage, eigen, ends, parity


def spread(column):
    return np.broadcast_to(column[..., None], column.shape + (LANES,)).astype(np.float32)


def split(values):
    high = values.astype(BF16)
    low = (values - high.astype(F32)).astype(BF16)
    return high, low


def dot(left, right):
    return jnp.dot(left, right, preferred_element_type=F32)


def times_basis(values, wide):
    high, low = split(values)
    both = dot(jnp.concatenate([high, low], axis=1), wide)
    depth = values.shape[1]
    return both[:, :depth] + both[:, depth:]


class Radial:
    def __init__(self, helmholtz, azimuth, vertical, radial, total):
        self.refs = (helmholtz, azimuth, vertical, radial)
        self.total = total

    def coupling(self, cell):
        cell = jnp.asarray(cell, jnp.int32)
        return jnp.where(cell < self.total - 1, self.refs[3][cell], 0.0)

    def previous(self, cell):
        cell = jnp.asarray(cell, jnp.int32)
        return jnp.where(cell > 0, self.refs[3][jnp.maximum(cell - 1, 0)], 0.0)

    def diagonal(self, cell, lam, mu):
        base = self.refs[0][cell] + self.coupling(cell) + self.previous(cell)
        return lam * self.refs[1][cell] + (mu * self.refs[2][cell] + base)


def inverse(values):
    return pl.reciprocal(values, approx=False)


def solve_block(radial, first, lam, mu, right, add_first=None, add_last=None):
    rows = []
    factor = values = None
    for place in range(CELLS):
        cell = first + place
        diagonal = radial.diagonal(cell, lam, mu)
        if place == 0 and add_first is not None:
            diagonal = diagonal - add_first
        if place == CELLS - 1 and add_last is not None:
            diagonal = diagonal - add_last
        if place > 0:
            before = radial.previous(cell)
            pivot = inverse(diagonal - before * factor)
            values = (right[place] + before * values) * pivot
        else:
            pivot = inverse(diagonal)
            values = right[place] * pivot
        factor = radial.coupling(cell) * pivot
        rows.append((values, factor))
    answer = [rows[-1][0]]
    for values, factor in rows[-2::-1]:
        answer.insert(0, values + factor * answer[0])
    return answer


def block_ports(radial, first, lam, mu):
    diagonals = [radial.diagonal(first + place, lam, mu) for place in range(CELLS)]
    pivot = inverse(diagonals[0])
    forward = [pivot]
    for place in range(1, CELLS):
        before = radial.previous(first + place)
        pivot = inverse(diagonals[place] - before * before * pivot)
        forward.append(pivot)
    last = forward[-1]
    cross = last
    for place in range(CELLS - 2, -1, -1):
        cross = radial.coupling(first + place) * forward[place] * cross
    backward = inverse(diagonals[-1])
    for place in range(CELLS - 2, -1, -1):
        after = radial.coupling(first + place)
        backward = inverse(diagonals[place] - after * after * backward)
    entry, leave = radial.previous(first), radial.coupling(first + CELLS - 1)
    return backward * entry, cross * leave, cross * entry, last * leave


def chip_ports(radial, first, lam, mu):
    b1, g1, b2, g2 = block_ports(radial, first, lam, mu)
    c1, h1, c2, h2 = block_ports(radial, first + CELLS, lam, mu)
    mid = inverse(1.0 - g2 * c1)
    low = c1 * b2 * mid
    high = h1 * mid
    whole = (
        b1 + g1 * low,
        g1 * high,
        c2 * (b2 + g2 * low),
        h2 + c2 * g2 * high,
    )
    return (b1, g1, b2, g2), (c1, h1, c2, h2), mid, whole


def forward_kernel(total, source, wide, stage_high, stage_low, lam, mu, *rest):
    radial = Radial(*rest[:4], total)
    spectrum, keep, send, high, low = rest[4:]
    length = source.shape[0]
    quarter = length // 8
    root = math.sqrt(0.5)
    core = lax.rem(lax.axis_index("rad"), 2)
    first = lax.axis_index("rad") * CELLS
    for cell in range(CELLS):
        x = [source[n * quarter : (n + 1) * quarter, cell, :] for n in range(8)]
        s = [x[n] + x[n + 4] for n in range(4)]
        d = [x[n] - x[n + 4] for n in range(4)]
        even, odd = s[0] + s[2], s[1] + s[3]
        minus, plus = root * (d[1] - d[3]), root * (d[1] + d[3])
        parts = (
            even + odd,
            even - odd,
            d[0] + minus,
            -plus - d[2],
            s[0] - s[2],
            s[3] - s[1],
            d[0] - minus,
            d[2] - plus,
        )
        for place, part in enumerate(parts):
            one, two = split(times_basis(part, wide[...]))
            slot, half = place // 2, place % 2
            rows = slice(half * quarter, (half + 1) * quarter)
            columns = slice(cell * LANES, (cell + 1) * LANES)
            high[slot, rows, columns] = one
            low[slot, rows, columns] = two
    for slot in range(4):
        result = (
            dot(stage_high[slot], high[slot])
            + dot(stage_high[slot], low[slot])
            + dot(stage_low[slot], high[slot])
        )
        for cell in range(CELLS):
            spectrum[cell, slot * 2 * quarter : (slot + 1) * 2 * quarter, :] = result[
                :, cell * LANES : (cell + 1) * LANES
            ]
    chunk = 32
    half = length // 2
    level = mu[...][:1]

    def step(index, _):
        ends = []
        for part in range(2):
            rows = pl.ds(pl.multiple_of(part * half + index * chunk, chunk), chunk)
            right = [spectrum[cell, rows, :] for cell in range(CELLS)]
            answer = solve_block(radial, first, lam[rows, :], level, right)
            ends.append((answer[0], answer[-1]))
        rows = pl.ds(pl.multiple_of(index * chunk, chunk), chunk)
        for place in range(2):
            keep[place, rows, :] = jnp.where(core == 0, ends[0][place], ends[1][place])
            send[place, rows, :] = jnp.where(core == 0, ends[1][place], ends[0][place])
        return 0

    lax.fori_loop(0, half // chunk, step, 0)


def pair_ports_kernel(total, lam, mu, *rest):
    radial = Radial(*rest[:4], total)
    (out,) = rest[4:]
    half = out.shape[1]
    core = lax.rem(lax.axis_index("rad"), 2)
    first = lax.axis_index("rad") // 2 * (2 * CELLS)
    level = mu[...][:1]
    chunk = 32

    def step(index, _):
        rows = pl.ds(pl.multiple_of(index * chunk, chunk), chunk)
        spot = pl.ds(pl.multiple_of(core * half + index * chunk, chunk), chunk)
        (b1, g1, b2, g2), (c1, h1, c2, h2), mid, _whole = chip_ports(
            radial, first, lam[spot, :], level
        )
        for place, value in enumerate((g1, b2, g2, c1, h1, c2, mid)):
            out[place, rows, :] = value
        return 0

    lax.fori_loop(0, half // chunk, step, 0)


def merge_kernel(chips, keep, got, ports, *rest):
    outs, whole = rest[:-1], rest[-1]
    half = keep.shape[1]
    core = lax.rem(lax.axis_index("rad"), 2)
    chip = lax.axis_index("rad") // 2
    chunk = 32

    def step(index, _):
        rows = pl.ds(pl.multiple_of(index * chunk, chunk), chunk)
        g1, b2, g2, c1, h1, c2, mid = (ports[place, rows, :] for place in range(7))
        mine = [keep[place, rows, :] for place in range(2)]
        other = [got[place, rows, :] for place in range(2)]
        low = [jnp.where(core == 0, m, o) for m, o in zip(mine, other)]
        high = [jnp.where(core == 0, o, m) for m, o in zip(mine, other)]
        upper = (high[0] + c1 * low[1]) * mid
        whole[0, rows, :] = low[0] + g1 * upper
        whole[1, rows, :] = high[1] + c2 * (low[1] + g2 * upper)
        return 0

    lax.fori_loop(0, half // chunk, step, 0)
    piece = half // chips
    for distance, out in enumerate(outs):
        target = lax.rem(chip + distance, chips)
        out[...] = whole[:, pl.ds(pl.multiple_of(target * piece, piece), piece), :]


def chain_ports_kernel(total, chips, lam, mu, *rest):
    radial = Radial(*rest[:4], total)
    (out,) = rest[4:]
    length = lam.shape[0]
    half = length // 2
    piece = half // chips
    core = lax.rem(lax.axis_index("rad"), 2)
    chip = lax.axis_index("rad") // 2
    level = mu[...][:1]
    chunk = min(64, piece)

    def step(index, _):
        rows = pl.ds(pl.multiple_of(index * chunk, chunk), chunk)
        start = core * half + chip * piece + index * chunk
        values = lam[pl.ds(pl.multiple_of(start, chunk), chunk), :]

        def link(place, carry):
            _one, _two, _mid, (b1, g1, b2, g2) = chip_ports(
                radial, place * (2 * CELLS), values, level
            )
            pivot = inverse(1.0 - b1 * carry)
            out[place, 0, rows, :] = b1
            out[place, 1, rows, :] = b2
            out[place, 2, rows, :] = pivot
            out[place, 3, rows, :] = g1 * pivot
            out[place, 4, rows, :] = carry
            return g2 + b2 * carry * g1 * pivot

        lax.fori_loop(0, chips, link, jnp.zeros((chunk, LANES), F32))
        return 0

    lax.fori_loop(0, piece // chunk, step, 0)


def chain_kernel(chips, ports, *rest):
    pieces, outs = rest[:chips], rest[chips : 2 * chips]
    ends, sides, before, start = rest[2 * chips :]
    chip = lax.axis_index("rad") // 2
    for distance, piece in enumerate(pieces):
        ends[lax.rem(chip + chips - distance, chips)] = piece[...]
    size = ports.shape[2]
    chunk = min(32, size)

    def step(index, _):
        rows = pl.ds(pl.multiple_of(index * chunk, chunk), chunk)
        value = jnp.zeros((chunk, LANES), F32)
        for place in range(chips):
            b1, b2, pivot = (ports[place, kind, rows, :] for kind in range(3))
            carry = ports[place, 4, rows, :]
            before[place] = value
            origin = (ends[place, 0, rows, :] + b1 * value) * pivot
            start[place] = origin
            value = ends[place, 1, rows, :] + b2 * (value + carry * origin)
        after = jnp.zeros((chunk, LANES), F32)
        for place in range(chips - 1, -1, -1):
            origin = start[place] + ports[place, 3, rows, :] * after
            sides[place, 0, rows, :] = before[place] + ports[place, 4, rows, :] * origin
            sides[place, 1, rows, :] = after
            after = origin
        return 0

    lax.fori_loop(0, size // chunk, step, 0)
    for distance, out in enumerate(outs):
        out[...] = sides[lax.rem(chip + distance, chips)]


def parts_kernel(chips, keep, got, ports, *rest):
    pieces = rest[:chips]
    own, send, sides = rest[chips:]
    half = keep.shape[1]
    piece_rows = half // chips
    core = lax.rem(lax.axis_index("rad"), 2)
    chip = lax.axis_index("rad") // 2
    for distance, piece in enumerate(pieces):
        target = lax.rem(chip + chips - distance, chips)
        sides[:, pl.ds(pl.multiple_of(target * piece_rows, piece_rows), piece_rows), :] = piece[...]
    chunk = 32

    def step(index, _):
        rows = pl.ds(pl.multiple_of(index * chunk, chunk), chunk)
        _g1, b2, g2, c1, h1, _c2, mid = (ports[place, rows, :] for place in range(7))
        left, right = sides[0, rows, :], sides[1, rows, :]
        last = jnp.where(core == 0, keep[1, rows, :], got[1, rows, :]) + b2 * left
        opening = jnp.where(core == 0, got[0, rows, :], keep[0, rows, :]) + h1 * right
        upper = (opening + c1 * last) * mid
        lower = last + g2 * upper
        own[0, rows, :] = jnp.where(core == 0, left, lower)
        own[1, rows, :] = jnp.where(core == 0, upper, right)
        send[0, rows, :] = jnp.where(core == 0, lower, left)
        send[1, rows, :] = jnp.where(core == 0, right, upper)
        return 0

    lax.fori_loop(0, half // chunk, step, 0)


def fold_rows(values):
    total = values[:8]
    for start in range(8, values.shape[0], 8):
        total = total + values[start : start + 8]
    return total


def ratios(radial, first, lam, mu, left_store, right_store):
    total = radial.total
    shape = lam.shape

    def leftward(cell, factor):
        pivot = inverse(radial.diagonal(cell, lam, mu) - radial.previous(cell) * factor)
        factor = radial.coupling(cell) * pivot
        left_store[cell] = factor
        return factor

    def rightward(step, factor):
        cell = total - 1 - step
        pivot = inverse(radial.diagonal(cell, lam, mu) - radial.coupling(cell) * factor)
        factor = radial.previous(cell) * pivot
        right_store[cell] = factor
        return factor

    zero = jnp.zeros(shape, F32)
    left = lax.fori_loop(0, first, leftward, zero)
    right = lax.fori_loop(0, total - CELLS - first, rightward, zero)
    return left, right


def ends_kernel(total, spectrum, lam, ends, mu, *rest):
    radial = Radial(*rest[:4], total)
    out, store, sums = rest[4:]
    first = lax.axis_index("rad") * CELLS
    level = mu[...][:1]
    chunk = spectrum.shape[1] // 8
    sums[...] = jnp.zeros_like(sums)

    def step(index, _):
        kind = lax.rem(index, 2)
        rows = pl.ds(pl.multiple_of(index * chunk, chunk), chunk)
        values = lam[rows, :]
        left, right = ratios(radial, first, values, level, store, store)
        weight = 2.0 * ends[rows, :]
        answer = solve_block(
            radial,
            first,
            values,
            level,
            [weight * spectrum[cell, rows, :] for cell in range(CELLS)],
            radial.previous(first) * left,
            radial.coupling(first + CELLS - 1) * right,
        )
        for place in range(CELLS):
            sums[kind, first + place] += fold_rows(answer[place])

        def outward_left(move, value):
            cell = first - 1 - move
            value = store[cell] * value
            sums[kind, cell] += fold_rows(value)
            return value

        def outward_right(cell, value):
            value = store[cell] * value
            sums[kind, cell] += fold_rows(value)
            return value

        lax.fori_loop(0, first, outward_left, answer[0])
        lax.fori_loop(first + CELLS, total, outward_right, answer[-1])
        return 0

    lax.fori_loop(0, 8, step, 0)
    for kind in range(2):
        for cell in range(total):
            out[kind, cell : cell + 1, :] = jnp.sum(sums[kind, cell], axis=0, keepdims=True)


def response_kernel(total, lam, weight, mu, *rest):
    radial = Radial(*rest[:4], total)
    out, store, sums = rest[4:]
    first = lax.axis_index("rad") * CELLS
    level = mu[pl.ds(lax.axis_index("az"), 1), :]
    group = LANES // SLABS
    chunk = lam.shape[1] // 2
    sums[...] = jnp.zeros_like(sums)

    def step(index, _):
        kind = index // 2
        rows = pl.ds(pl.multiple_of(lax.rem(index, 2) * chunk, chunk), chunk)
        values = lam[kind, rows, :]
        left, right = ratios(radial, first, values, level, store, store)
        source = weight[kind, rows, :]
        zero = jnp.zeros_like(source)
        openings, closings = [], []
        for place in range(CELLS):
            answer = solve_block(
                radial,
                first,
                values,
                level,
                [source if cell == place else zero for cell in range(CELLS)],
                radial.previous(first) * left,
                radial.coupling(first + CELLS - 1) * right,
            )
            for cell in range(CELLS):
                sums[kind, place, first + cell] += fold_rows(answer[cell])
            openings.append(answer[0])
            closings.append(answer[-1])

        def outward(cell, factor, edges):
            factor = store[cell] * factor
            for place in range(CELLS):
                sums[kind, place, cell] += fold_rows(factor * edges[place])
            return factor

        one = jnp.ones_like(source)
        lax.fori_loop(
            0, first, lambda move, factor: outward(first - 1 - move, factor, openings), one
        )
        lax.fori_loop(
            first + CELLS, total, lambda cell, factor: outward(cell, factor, closings), one
        )
        return 0

    lax.fori_loop(0, 4, step, 0)
    lane = lax.broadcasted_iota(jnp.int32, (1, LANES), 1) // group

    def close(cell, _):
        for kind in range(2):
            result = jnp.zeros((1, LANES), F32)
            for place in range(CELLS):
                row = jnp.sum(sums[kind, place, cell], axis=0, keepdims=True)
                row = row + pltpu.roll(row, 2 * group, 1)
                row = row + pltpu.roll(row, group, 1)
                result = jnp.where(lane == place, row, result)
            out[kind, pl.ds(cell, 1), :] = result
        return 0

    lax.fori_loop(0, total, close, 0)


def invert(matrix, total):
    rows = lax.broadcasted_iota(jnp.int32, (total, LANES), 0)

    def step(pivot, _):
        mark = rows == pivot
        scale = 1.0 / matrix[pivot, pl.ds(pivot, 1), :]
        line = jnp.where(mark, 1.0, matrix[pivot]) * scale

        def row(index, _):
            factor = matrix[index, pl.ds(pivot, 1), :]
            matrix[index] = jnp.where(mark, 0.0, matrix[index]) - factor * line
            return 0

        lax.fori_loop(0, total, row, 0, unroll=8)
        matrix[pivot] = line
        return 0

    lax.fori_loop(0, total, step, 0)


def capacity_kernel(total, chips, azimuth, *rest):
    pieces = rest[:chips]
    first_out, second_out, sum_matrix = rest[chips:]
    chip = lax.axis_index("rad") // 2
    core = lax.rem(lax.axis_index("rad"), 2)
    group = LANES // SLABS
    lane = lax.broadcasted_iota(jnp.int32, (1, LANES), 1) // group
    cells = lax.broadcasted_iota(jnp.int32, (total, LANES), 0)
    for distance, piece in enumerate(pieces):
        origin = lax.rem(chip + chips - distance, chips)
        for side in range(2):
            block = 2 * origin + lax.rem(core + side, 2)
            for kind in range(2):
                packed = piece[side, kind]
                for place in range(CELLS):
                    row = jnp.where(lane == place, packed, 0.0)
                    row = row + pltpu.roll(row, 2 * group, 1)
                    row = row + pltpu.roll(row, group, 1)
                    cell = block * CELLS + place
                    own = jnp.where(cells == cell, 0.5 / azimuth[cell], 0.0)
                    if kind == 0:
                        sum_matrix[cell] = own + row
                    else:
                        first_out[cell] = own - row
    invert(first_out, total)
    weight = jnp.where(lane < 2, 0.25, 0.0)

    def column(cell, value):
        return jnp.where(cells == cell, 1.0 / azimuth[cell], value)

    scale = lax.fori_loop(0, total, column, jnp.zeros((total, LANES), F32)) * weight

    def add(cell, _):
        second_out[cell] = sum_matrix[cell] + first_out[cell] * scale * (1.0 / azimuth[cell])
        return 0

    lax.fori_loop(0, total, add, 0)
    invert(second_out, total)


def apply_matrix(matrix, vector):
    total = vector.shape[0]
    result = matrix[0] * vector[0:1, :]
    for cell in range(1, total):
        result = result + matrix[cell] * vector[cell : cell + 1, :]
    return result


def times_i(values):
    group = LANES // SLABS
    lane = lax.broadcasted_iota(jnp.int32, (1, LANES), 1) // group
    ahead = pltpu.roll(values, group, 1)
    behind = pltpu.roll(values, LANES - group, 1)
    return jnp.where(lane == 0, -behind, jnp.where(lane == 1, ahead, 0.0))


def slabs_kernel(total, azimuth, first_matrix, second_matrix, *rest):
    pieces, outs = rest[:SLABS], rest[SLABS : 2 * SLABS]
    values, results = rest[2 * SLABS :]
    slab = lax.axis_index("az")
    group = LANES // SLABS
    lane = lax.broadcasted_iota(jnp.int32, (1, LANES), 1) // group
    cells = lax.broadcasted_iota(jnp.int32, (total, LANES), 0)
    for distance, piece in enumerate(pieces):
        values[slab ^ distance] = piece[...]

    def channels(kind):
        u = [values[place, kind] for place in range(SLABS)]
        mixed = (u[0] - u[2], u[3] - u[1], (u[0] + u[2]) - (u[1] + u[3]))
        result = jnp.zeros((total, LANES), F32)
        for channel, value in enumerate(mixed):
            shift = lax.rem(channel - slab + SLABS, SLABS) * group
            result = jnp.where(lane == channel, pltpu.roll(value, shift, 1), result)
        return result

    def column(cell, value):
        return jnp.where(cells == cell, 0.5 / azimuth[cell], value)

    scale = lax.fori_loop(0, total, column, jnp.zeros((total, LANES), F32))
    sums, differences = channels(0), channels(1)
    lead = apply_matrix(first_matrix, differences)
    plus = apply_matrix(second_matrix, times_i(lead) * scale - sums)
    plus = jnp.where(lane < 3, plus, 0.0)
    minus = lead + apply_matrix(first_matrix, times_i(plus) * scale)
    minus = jnp.where(lane < 3, minus, 0.0)
    for kind, value in enumerate((plus, minus)):
        parts = []
        for channel in range(3):
            shift = lax.rem(slab - channel + SLABS, SLABS) * group
            part = pltpu.roll(value, shift, 1)
            parts.append(jnp.where(lane == slab, part, 0.0))
        real, imag, alternate = parts
        results[0, kind] = 0.25 * (2.0 * real + alternate)
        results[1, kind] = 0.25 * (-2.0 * imag - alternate)
        results[2, kind] = 0.25 * (alternate - 2.0 * real)
        results[3, kind] = 0.25 * (2.0 * imag - alternate)
    for distance, out in enumerate(outs):
        out[...] = results[slab ^ distance]


def sides_kernel(total, lam, ends, mu, *rest):
    radial = Radial(*rest[:4], total)
    pieces = rest[4 : 4 + SLABS]
    sources, out = rest[4 + SLABS :]
    sources[...] = (pieces[0][...] + pieces[1][...]) + (pieces[2][...] + pieces[3][...])
    first = lax.axis_index("rad") * CELLS
    level = mu[...][:1]
    chunk = lam.shape[0] // 8

    def step(index, _):
        kind = lax.rem(index, 2)
        rows = pl.ds(pl.multiple_of(index * chunk, chunk), chunk)
        values = lam[rows, :]
        zero = jnp.zeros((chunk, LANES), F32)

        def leftward(cell, carry):
            factor, value = carry
            before = radial.previous(cell)
            pivot = inverse(radial.diagonal(cell, values, level) - before * factor)
            value = (sources[kind, pl.ds(cell, 1), :] + before * value) * pivot
            return radial.coupling(cell) * pivot, value

        def rightward(move, carry):
            cell = total - 1 - move
            factor, value = carry
            after = radial.coupling(cell)
            pivot = inverse(radial.diagonal(cell, values, level) - after * factor)
            value = (sources[kind, pl.ds(cell, 1), :] + after * value) * pivot
            return radial.previous(cell) * pivot, value

        left, left_value = lax.fori_loop(0, first, leftward, (zero, zero))
        right, right_value = lax.fori_loop(0, total - CELLS - first, rightward, (zero, zero))
        entry, leave = radial.previous(first), radial.coupling(first + CELLS - 1)
        own = [sources[kind, pl.ds(first + place, 1), :] for place in range(CELLS)]
        own[0] = own[0] + entry * left_value
        own[-1] = own[-1] + leave * right_value
        answer = solve_block(radial, first, values, level, own, entry * left, leave * right)
        weight = ends[rows, :]
        out[0, rows, :] = weight * (left_value + left * answer[0])
        out[1, rows, :] = weight * (right_value + right * answer[-1])
        return 0

    lax.fori_loop(0, 8, step, 0)


def backward_kernel(total, spectrum, own, got, extra, sources, wide, stage_high, stage_low, *rest):
    lam, ends, mu = rest[:3]
    radial = Radial(*rest[3:7], total)
    out, high, low, middle = rest[7:]
    length = spectrum.shape[1]
    quarter = length // 8
    half = length // 2
    root = math.sqrt(0.5)
    core = lax.rem(lax.axis_index("rad"), 2)
    first = lax.axis_index("rad") * CELLS
    level = mu[...][:1]
    chunk = 32
    entry, leave = radial.previous(first), radial.coupling(first + CELLS - 1)

    for slot in range(4):

        def step(index, _):
            kind = index // (quarter // chunk)
            spot = pl.ds(pl.multiple_of(index * chunk, chunk), chunk)
            rows = pl.ds(pl.multiple_of(slot * 2 * quarter + index * chunk, chunk), chunk)
            near = pl.ds(pl.multiple_of(slot % 2 * 2 * quarter + index * chunk, chunk), chunk)
            mine = core == slot // 2
            side = [
                jnp.where(mine, own[place, near, :], got[place, near, :]) + extra[place, rows, :]
                for place in range(2)
            ]
            weight = ends[rows, :]
            right = [
                spectrum[cell, rows, :] + weight * sources[kind, pl.ds(first + cell, 1), :]
                for cell in range(CELLS)
            ]
            right[0] = right[0] + entry * side[0]
            right[-1] = right[-1] + leave * side[1]
            answer = solve_block(radial, first, lam[rows, :], level, right)
            for cell in range(CELLS):
                one, two = split(answer[cell])
                columns = slice(cell * LANES, (cell + 1) * LANES)
                high[slot, spot, columns] = one
                low[slot, spot, columns] = two
            return 0

        lax.fori_loop(0, 2 * quarter // chunk, step, 0)
        middle[slot] = (
            dot(stage_high[slot], high[slot])
            + dot(stage_high[slot], low[slot])
            + dot(stage_low[slot], high[slot])
        )
    for cell in range(CELLS):
        columns = slice(cell * LANES, (cell + 1) * LANES)
        y = [
            middle[place // 2, place % 2 * quarter : (place % 2 + 1) * quarter, columns]
            for place in range(8)
        ]
        plus, minus = y[0] + y[1], y[0] - y[1]
        s = (plus + y[4], minus - y[5], plus - y[4], minus + y[5])
        real, imag = root * (y[2] - y[6]), root * (y[3] + y[7])
        d = (y[2] + y[6], real - imag, y[7] - y[3], -real - imag)
        for n in range(4):
            for sign in range(2):
                value = s[n] + d[n] if sign == 0 else s[n] - d[n]
                place = n + 4 * sign
                out[place * quarter : (place + 1) * quarter, cell, :] = times_basis(
                    value, wide[...]
                )


def call(kernel, out_shapes, args, scalars=(), scratch=(), flops=0, name=None):
    specs = [
        pl.BlockSpec(memory_space=pltpu.SMEM if place in scalars else pltpu.VMEM)
        for place in range(len(args))
    ]
    outs = [jax.ShapeDtypeStruct(shape, F32) for shape in out_shapes]
    moved = sum(math.prod(shape) for shape in out_shapes) + sum(math.prod(a.shape) for a in args)
    return pl.pallas_call(
        kernel,
        out_shape=outs,
        in_specs=specs,
        out_specs=[pl.BlockSpec(memory_space=pltpu.VMEM)] * len(outs),
        scratch_shapes=list(scratch),
        compiler_params=pltpu.CompilerParams(vmem_limit_bytes=VMEM_LIMIT),
        cost_estimate=pl.CostEstimate(flops=flops, bytes_accessed=4 * moved, transcendentals=0),
        name=name,
    )(*args)


def other_core(values):
    count = lax.axis_size("rad")
    return lax.ppermute(values, "rad", [(index, index ^ 1) for index in range(count)])


def along_chips(values, distance):
    chips = lax.axis_size("rad") // 2
    route = [
        (2 * chip + core, 2 * ((chip + distance) % chips) + core)
        for chip in range(chips)
        for core in range(2)
    ]
    return lax.ppermute(values, "rad", route)


def across_slabs(values, distance):
    return lax.ppermute(values, "az", [(slab, slab ^ distance) for slab in range(SLABS)])


def on_device(source, helmholtz, azimuth, vertical, radial):
    length, cells, depth = source.shape
    blocks = lax.axis_size("rad")
    chips = blocks // 2
    total = blocks * cells
    assert cells == CELLS and depth == LANES and lax.axis_size("az") == SLABS
    half = length // 2
    piece = half // chips
    quarter = length // 8
    scalars4 = (helmholtz, azimuth, vertical, radial)

    basis = cosine_basis(depth)
    stage, eigen, end_weights, parity = slab_tables(length)
    stage_high, stage_low = two_halves(stage)
    back_high, back_low = two_halves(np.swapaxes(stage, 1, 2))
    lam = jnp.asarray(spread(eigen))
    ends = jnp.asarray(spread(end_weights))
    vertical_eigen = 2.0 - 2.0 * np.cos(math.pi / depth * np.arange(depth))
    mu = jnp.asarray(np.broadcast_to(vertical_eigen[None, :], (8, depth)).astype(np.float32))
    group = depth // SLABS
    mu_groups = jnp.asarray(
        np.tile(vertical_eigen.reshape(SLABS, group), (1, SLABS)).astype(np.float32)
    )

    def packed(column):
        table = np.stack([column[parity > 0], column[parity < 0]]).reshape(2, quarter, SLABS)
        return jnp.asarray(np.repeat(table, group, axis=2).astype(np.float32))

    lam_groups = packed(eigen)
    weight_groups = packed(2.0 * end_weights**2)

    def smem(start):
        return tuple(range(start, start + 4))

    spectrum, keep, send = call(
        functools.partial(forward_kernel, total),
        [(CELLS, length, LANES), (2, half, LANES), (2, half, LANES)],
        (source, jnp.asarray(wide_basis(basis)), jnp.asarray(stage_high), jnp.asarray(stage_low), lam, mu)
        + scalars4,
        smem(6),
        [pltpu.VMEM((4, 2 * quarter, CELLS * LANES), BF16)] * 2,
        name="forward",
    )
    got = other_core(send)
    (ports,) = call(
        functools.partial(pair_ports_kernel, total),
        [(7, half, LANES)],
        (lam, mu) + scalars4,
        smem(2),
        name="pair_ports",
    )
    merged = call(
        functools.partial(merge_kernel, chips),
        [(2, piece, LANES)] * chips,
        (keep, got, ports),
        (),
        [pltpu.VMEM((2, half, LANES), F32)],
        name="merge",
    )
    gathered = [merged[0]] + [along_chips(merged[d], d) for d in range(1, chips)]
    (chain_ports,) = call(
        functools.partial(chain_ports_kernel, total, chips),
        [(chips, 5, piece, LANES)],
        (lam, mu) + scalars4,
        smem(2),
        name="chain_ports",
    )
    chain_chunk = min(32, piece)
    sides = call(
        functools.partial(chain_kernel, chips),
        [(2, piece, LANES)] * chips,
        (chain_ports, *gathered),
        (),
        [pltpu.VMEM((chips, 2, piece, LANES), F32)] * 2
        + [pltpu.VMEM((chips, chain_chunk, LANES), F32)] * 2,
        name="chain",
    )
    returned = [sides[0]] + [along_chips(sides[d], d) for d in range(1, chips)]
    own_sides, send_sides = call(
        functools.partial(parts_kernel, chips),
        [(2, half, LANES)] * 2,
        (keep, got, ports, *returned),
        (),
        [pltpu.VMEM((2, half, LANES), F32)],
        name="parts",
    )
    got_sides = other_core(send_sides)

    (response,) = call(
        functools.partial(response_kernel, total),
        [(2, total, LANES)],
        (lam_groups, weight_groups, mu_groups) + scalars4,
        smem(3),
        [
            pltpu.VMEM((total, quarter // 2, LANES), F32),
            pltpu.VMEM((2, CELLS, total, 8, LANES), F32),
        ],
        name="response",
    )
    both = jnp.stack([response, other_core(response)])
    responses = [both] + [along_chips(both, d) for d in range(1, chips)]
    first_matrix, second_matrix = call(
        functools.partial(capacity_kernel, total, chips),
        [(total, total, LANES)] * 2,
        (azimuth, *responses),
        (0,),
        [pltpu.VMEM((total, total, LANES), F32)],
        name="capacity",
    )

    (partial_ends,) = call(
        functools.partial(ends_kernel, total),
        [(2, total, LANES)],
        (spectrum, lam, ends, mu) + scalars4,
        smem(4),
        [
            pltpu.VMEM((total, quarter, LANES), F32),
            pltpu.VMEM((2, total, 8, LANES), F32),
        ],
        name="ends",
    )
    pair_ends = partial_ends + other_core(partial_ends)
    slab_ends = pair_ends + sum(along_chips(pair_ends, d) for d in range(1, chips))
    all_ends = [slab_ends] + [across_slabs(slab_ends, d) for d in range(1, SLABS)]
    end_sources = call(
        functools.partial(slabs_kernel, total),
        [(2, total, LANES)] * SLABS,
        (azimuth, first_matrix, second_matrix, *all_ends),
        (0,),
        [pltpu.VMEM((SLABS, 2, total, LANES), F32)] * 2,
        name="slabs",
    )
    sources = [end_sources[0]] + [across_slabs(end_sources[d], d) for d in range(1, SLABS)]
    all_sources, extra = call(
        functools.partial(sides_kernel, total),
        [(2, total, LANES), (2, length, LANES)],
        (lam, ends, mu) + scalars4 + tuple(sources),
        smem(3),
        name="sides",
    )
    (pressure,) = call(
        functools.partial(backward_kernel, total),
        [(length, CELLS, LANES)],
        (
            spectrum,
            own_sides,
            got_sides,
            extra,
            all_sources,
            jnp.asarray(wide_basis(basis.T)),
            jnp.asarray(back_high),
            jnp.asarray(back_low),
            lam,
            ends,
            mu,
        )
        + scalars4,
        smem(11),
        [pltpu.VMEM((4, 2 * quarter, CELLS * LANES), BF16)] * 2
        + [pltpu.VMEM((4, 2 * quarter, CELLS * LANES), F32)],
        name="backward",
    )
    return pressure


def solution(mesh):
    in_specs = (P("az", "rad", None), P(), P(), P(), P())
    return jax.shard_map(
        on_device,
        mesh=mesh,
        in_specs=in_specs,
        out_specs=P("az", "rad", None),
        check_vma=False,
    )
```

time: 659 us -> 153 us (0.23)
  waiting for transfers between devices: 429 us -> 16.9 us
  Pallas kernels: 0 us -> 96.7 us
  matrix products: 71.5 us -> 0 us
  local copies, waits for them, and re-layouts: 69.8 us -> 4.83 us
  other arithmetic: 63.6 us -> 1.54 us
  starting transfers between devices: 17.3 us -> 32.9 us
    ppermute x4 -> x22, waiting for transfers between devices: 262 us -> 16.9 us  [the longest x12 14.2 us: along_chips(): return lax.ppermute(values, 'rad', route)]
    all_to_all x2 -> x0, waiting for transfers between devices: 167 us -> none  [the longest x1 93.7 us: on_device(): lax.all_to_all(solved, 'rad', split_axis=2, concat_axis=1, tiled=True)]
    pallas_call x0 -> x12, Pallas kernels: none -> 96.7 us  [call(): pl.pallas_call(kernel, out_shape=outs, in_specs=specs, out_specs=[pl.Bloc...]
    dot_general x18 -> x0, matrix products: 71.5 us -> none  [the longest x16 64.1 us: contract(): return jnp.einsum(pattern, matrix, values, precision=lax.Precision.HIGHEST)]
    slice x26 -> x0, local copies, waits for them, and re-layouts: 33.9 us -> none  [the longest x15 21.3 us: from_below(): return jnp.concatenate([block, values[..., :-stride, :]], axis=-2)]
    add x11 -> x2, other arithmetic: 29.6 us -> 0.77 us  [the longest x1 0.76 us: on_device(): pair_ends = partial_ends + other_core(partial_ends)]
    ppermute x4 -> x22, starting transfers between devices: 7.74 us -> 32.9 us  [the longest x12 22.9 us: along_chips(): return lax.ppermute(values, 'rad', route)]
    another operation x3 -> x0, local copies, waits for them, and re-layouts: 9.6 us -> none  [the longest x1 4.72 us: on_device(): jnp.stack([spec_real, spec_imag])]
  transfers between devices with their start and end apart: 6 -> 22, of which waited for: 6 -> 8; matrix products, arithmetic and copies ran while one was open for 4% -> 1% of each run, Pallas kernels for 0% -> 42%
where the time goes in v1:
time: 153 us
  Pallas kernels  96.7 us (63%)
  starting transfers between devices  32.9 us (22%)
  waiting for transfers between devices  16.9 us (11%)
  local copies, waits for them, and re-layouts  4.83 us (3%)
  other arithmetic  1.54 us (1%)
    pallas_call x12, Pallas kernels, call(): pl.pallas_call(kernel, out_shape=outs, in_specs=specs, out_specs=[pl.Bloc...  96.7 us
    ppermute x12, starting transfers between devices, along_chips(): return lax.ppermute(values, 'rad', route)  22.9 us
    ppermute x12, waiting for transfers between devices, along_chips(): return lax.ppermute(values, 'rad', route)  14.2 us
    ppermute x6, starting transfers between devices, across_slabs(): lax.ppermute(values, 'az', [(slab, slab ^ distance) for slab in range(SLA...  9.01 us
    unnamed x38, local copies, waits for them, and re-layouts  4.83 us
  transfers between devices with their start and end apart: 22, of which 8 were waited for; matrix products, arithmetic and copies ran while one was open for 1% of the time, Pallas kernels for 42%

profile of v1, /device:TPU:0, one launch (start us, length us, event | category | flops | bytes accessed | tf_op | source)
XLA Modules:
  0.0 153.0 jit_solution(7386794797143607035)
XLA Ops:
  0.0 13.9 %forward.1 = (f32[4,1024,128]{2,1,0:T(8,128)}, f32[2,512,128]{2,1,0:T(8,128)}, f32[2,512,128]{2,1,0:T(8,128)}) custom-call(f32[1024,4,128]{2,1,0:T(4,128)} %source.1, bf16[256,256]{1,0:T(8,128)(2,1)} %constant.30.clone.wide, bf16[4,256,256]{2,1,0:T(8,128)(2,1)} %constant.31.clone.stage_high, bf16[4,256,256]{2,1,0:T(8,128)(2,1)} %constant.32.clone.stage_low, ...), custom_call_target="tpu_custom_call" | custom-call | bytes 8131072 | tf_op jit(solution)/shard_map/forward/pallas_call | solution.py:764
  13.9 0.5 collective-permute-start
  14.4 3.5 %pair_ports.1.ports = f32[7,512,128]{2,1,0:T(8,128)} custom-call(f32[1024,128]{1,0:T(8,128)} %constant.24.clone.lam.rest_0_, f32[8,128]{1,0:T(8,128)} %constant.26.clone.mu.rest_2_, f32[32]{0:T(128)} %rest_3_.13, f32[32]{0:T(128)} %rest_4_.1, f32[32]{0:T(128)} %rest_5_.1, f32[32]{0:T(128)} %rest_6_.1), custom_call_target="tpu_custom_call" | custom-call | bytes 2363904 | tf_op jit(solution)/shard_map/pair_ports/pallas_call | solution.py:764
  17.9 0.0 collective-permute-done.got
  17.9 0.8 copy-done
  18.7 2.9 %merge.1 = (f32[2,128,128]{2,1,0:T(8,128)}, f32[2,128,128]{2,1,0:T(8,128)}, f32[2,128,128]{2,1,0:T(8,128)}, f32[2,128,128]{2,1,0:T(8,128)}) custom-call(f32[2,512,128]{2,1,0:T(8,128)} %get-tuple-element.27.keep, f32[2,512,128]{2,1,0:T(8,128)} %copy-done, f32[7,512,128]{2,1,0:T(8,128)} %pair_ports.1.ports), custom_call_target="tpu_custom_call" | custom-call | bytes 3407872 | tf_op jit(solution)/shard_map/merge/pallas_call | solution.py:764
  21.6 2.6 %collective-permute-start.1 = (f32[2,128,128]{2,1,0:T(8,128)}, f32[2,128,128]{2,1,0:T(8,128)S(1)}, u32[]{:S(2)}, u32[]{:S(2)}) collective-permute-start(f32[2,128,128]{2,1,0:T(8,128)} %get-tuple-element.30), channel_id=1, source_target_pairs={{0,2},{1,3},{2,4},{3,5},{4,6},{5,7},{6,0},{7,1},{8,10},{9,11},{10,... | collective-permute-start | bytes 393224 | tf_op jit(solution)/shard_map/ppermute | solution.py:788
  24.2 2.6 %collective-permute-start.2 = (f32[2,128,128]{2,1,0:T(8,128)}, f32[2,128,128]{2,1,0:T(8,128)S(1)}, u32[]{:S(2)}, u32[]{:S(2)}) collective-permute-start(f32[2,128,128]{2,1,0:T(8,128)} %get-tuple-element.31), channel_id=1, source_target_pairs={{0,4},{1,5},{2,6},{3,7},{4,0},{5,1},{6,2},{7,3},{8,12},{9,13},{10,... | collective-permute-start | bytes 393224 | tf_op jit(solution)/shard_map/ppermute | solution.py:788
  26.8 1.3 collective-permute-start.3
  28.1 3.2 %chain_ports.1.ports = f32[4,5,128,128]{3,2,1,0:T(8,128)} custom-call(f32[1024,128]{1,0:T(8,128)} %constant.24.clone.lam.rest_0_, f32[8,128]{1,0:T(8,128)} %constant.26.clone.mu.rest_2_, f32[32]{0:T(128)} %rest_3_.13, f32[32]{0:T(128)} %rest_4_.1, f32[32]{0:T(128)} %rest_5_.1, f32[32]{0:T(128)} %rest_6_.1), custom_call_target="tpu_custom_call" | custom-call | bytes 1839616 | tf_op jit(solution)/shard_map/chain_ports/pallas_call | solution.py:764
  31.4 0.0 collective-permute-done.1.rest_1_
  31.4 4.9 %collective-permute-done.2.rest_2_ = f32[2,128,128]{2,1,0:T(8,128)S(1)} collective-permute-done((f32[2,128,128]{2,1,0:T(8,128)}, f32[2,128,128]{2,1,0:T(8,128)S(1)}, u32[]{:S(2)}, u32[]{:S(2)}) %collective-permute-start.2) | collective-permute-done | bytes 131104 | tf_op jit(solution)/shard_map/ppermute | solution.py:788
  36.3 0.0 collective-permute-done.3.rest_3_
  36.3 0.6 copy-done.4
  36.9 0.0 copy-done.5
  37.0 2.5 %chain.1 = (f32[2,128,128]{2,1,0:T(8,128)}, f32[2,128,128]{2,1,0:T(8,128)}, f32[2,128,128]{2,1,0:T(8,128)}, f32[2,128,128]{2,1,0:T(8,128)}) custom-call(f32[4,5,128,128]{3,2,1,0:T(8,128)} %chain_ports.1.ports, f32[2,128,128]{2,1,0:T(8,128)} %get-tuple-element.29.rest_0_, f32[2,128,128]{2,1,0:T(8,128)} %copy-done.3, f32[2,128,128]{2,1,0:T(8,128)} %copy-done.4, ...), custom_call_target="tpu_custom_call" | custom-call | bytes 2359296 | tf_op jit(solution)/shard_map/chain/pallas_call | solution.py:764
  39.5 3.3 %collective-permute-start.4 = (f32[2,128,128]{2,1,0:T(8,128)}, f32[2,128,128]{2,1,0:T(8,128)S(1)}, u32[]{:S(2)}, u32[]{:S(2)}) collective-permute-start(f32[2,128,128]{2,1,0:T(8,128)} %get-tuple-element.34), channel_id=1, source_target_pairs={{0,2},{1,3},{2,4},{3,5},{4,6},{5,7},{6,0},{7,1},{8,10},{9,11},{10,... | collective-permute-start | bytes 393224 | tf_op jit(solution)/shard_map/ppermute | solution.py:788
  42.8 1.7 %collective-permute-start.5 = (f32[2,128,128]{2,1,0:T(8,128)}, f32[2,128,128]{2,1,0:T(8,128)S(1)}, u32[]{:S(2)}, u32[]{:S(2)}) collective-permute-start(f32[2,128,128]{2,1,0:T(8,128)} %get-tuple-element.35), channel_id=1, source_target_pairs={{0,4},{1,5},{2,6},{3,7},{4,0},{5,1},{6,2},{7,3},{8,12},{9,13},{10,... | collective-permute-start | bytes 393224 | tf_op jit(solution)/shard_map/ppermute | solution.py:788
  44.4 0.7 collective-permute-start.6
  45.1 3.4 %collective-permute-done.4.rest_1_ = f32[2,128,128]{2,1,0:T(8,128)S(1)} collective-permute-done((f32[2,128,128]{2,1,0:T(8,128)}, f32[2,128,128]{2,1,0:T(8,128)S(1)}, u32[]{:S(2)}, u32[]{:S(2)}) %collective-permute-start.4) | collective-permute-done | bytes 131104 | tf_op jit(solution)/shard_map/ppermute | solution.py:788
  48.5 4.7 %collective-permute-done.5.rest_2_ = f32[2,128,128]{2,1,0:T(8,128)S(1)} collective-permute-done((f32[2,128,128]{2,1,0:T(8,128)}, f32[2,128,128]{2,1,0:T(8,128)S(1)}, u32[]{:S(2)}, u32[]{:S(2)}) %collective-permute-start.5) | collective-permute-done | bytes 131104 | tf_op jit(solution)/shard_map/ppermute | solution.py:788
  53.2 0.0 collective-permute-done.6.rest_3_
  53.2 0.6 copy-done.8
  53.8 0.1 copy-done.9
  53.9 3.2 %parts.1 = (f32[2,512,128]{2,1,0:T(8,128)}, f32[2,512,128]{2,1,0:T(8,128)}) custom-call(f32[2,512,128]{2,1,0:T(8,128)} %get-tuple-element.27.keep, f32[2,512,128]{2,1,0:T(8,128)} %copy-done, f32[7,512,128]{2,1,0:T(8,128)} %pair_ports.1.ports, f32[2,128,128]{2,1,0:T(8,128)} %get-tuple-element.33.rest_0_, f32[2,128,128]{2,1,0:T(8,128)} %copy-done.7, ...), custom_call_target="tpu_custom_call" | custom-call | bytes 4456448 | tf_op jit(solution)/shard_map/parts/pallas_call | solution.py:764
  57.1 0.0 collective-permute-start.7
  57.2 14.0 %ends.3 = f32[2,32,128]{2,1,0:T(8,128)} custom-call(f32[4,1024,128]{2,1,0:T(8,128)} %get-tuple-element.26.spectrum, f32[1024,128]{1,0:T(8,128)} %constant.24.clone.lam.rest_0_, f32[1024,128]{1,0:T(8,128)} %constant.25.clone.ends.rest_1_, f32[8,128]{1,0:T(8,128)} %constant.26.clone.mu.rest_2_, f32[32]{0:T(128)} %rest_3_.13, f32[32]{0:T(128)} %rest_4_.1, ...), custom_call_target="tpu_custom_call" | custom-call | bytes 3183104 | tf_op jit(solution)/shard_map/ends/pallas_call | solution.py:764
  71.1 0.5 collective-permute-start.12
  71.6 11.7 %response.1 = f32[2,32,128]{2,1,0:T(8,128)} custom-call(f32[2,128,128]{2,1,0:T(8,128)} %constant.28.clone.lam, f32[2,128,128]{2,1,0:T(8,128)} %constant.29.clone.weight, f32[4,128]{1,0:T(4,128)} %constant.27.clone.mu, f32[32]{0:T(128)} %rest_3_.13, f32[32]{0:T(128)} %rest_4_.1, f32[32]{0:T(128)} %rest_5_.1, f32[32]{0:T(128)} %rest_6_.1), custom_call_target="tpu_custom_call" | custom-call | bytes 297472 | tf_op jit(solution)/shard_map/response/pallas_call | solution.py:764
  83.3 0.0 collective-permute-start.8
  83.4 0.0 collective-permute-done.12
  83.4 0.8 add.12
  84.1 4.5 %collective-permute-start.15 = (f32[2,32,128]{2,1,0:T(8,128)S(1)}, f32[2,32,128]{2,1,0:T(8,128)S(1)}, u32[]{:S(2)}, u32[]{:S(2)}) collective-permute-start(f32[2,32,128]{2,1,0:T(8,128)S(1)} %add.12), channel_id=1, source_target_pairs={{0,6},{1,7},{2,0},{3,1},{4,2},{5,3},{6,4},{7,5},{8,14},{9,15},{10,... | collective-permute-start | bytes 98312 | tf_op jit(solution)/shard_map/ppermute | solution.py:788
  88.6 0.0 collective-permute-start.13
  88.6 0.6 collective-permute-start.14
  89.3 0.0 collective-permute-done.8
  89.3 0.8 pad_maximum_fusion.rest_0_
  90.0 3.8 %collective-permute-start.9 = (f32[2,2,32,128]{3,2,1,0:T(8,128)S(1)}, f32[2,2,32,128]{3,2,1,0:T(8,128)S(1)}, u32[]{:S(2)}, u32[]{:S(2)}) collective-permute-start(f32[2,2,32,128]{3,2,1,0:T(8,128)S(1)} %pad_maximum_fusion.rest_0_), channel_id=1, source_target_pairs={{0,2},{1,3},{2,4},{3,5},{4,6},{5,7},{6,0},{7,1},{8,10},{9,11},{10,... | collective-permute-start | bytes 196616 | tf_op jit(solution)/shard_map/ppermute | solution.py:788
  93.8 0.0 collective-permute-done.15
  93.8 0.0 collective-permute-start.10
  93.8 0.6 collective-permute-done.13
  94.4 1.8 %collective-permute-start.11 = (f32[2,2,32,128]{3,2,1,0:T(8,128)S(1)}, f32[2,2,32,128]{3,2,1,0:T(8,128)S(1)}, u32[]{:S(2)}, u32[]{:S(2)}) collective-permute-start(f32[2,2,32,128]{3,2,1,0:T(8,128)S(1)} %pad_maximum_fusion.rest_0_), channel_id=1, source_target_pairs={{0,6},{1,7},{2,0},{3,1},{4,2},{5,3},{6,4},{7,5},{8,14},{9,15},{10,... | collective-permute-start | bytes 196616 | tf_op jit(solution)/shard_map/ppermute | solution.py:788
  96.2 0.0 collective-permute-done.14
  96.3 1.6 %collective-permute-start.16 = (f32[2,32,128]{2,1,0:T(8,128)S(1)}, f32[2,32,128]{2,1,0:T(8,128)S(1)}, u32[]{:S(2)}, u32[]{:S(2)}) collective-permute-start(f32[2,32,128]{2,1,0:T(8,128)S(1)} %add_add_fusion.rest_0_), channel_id=1, source_target_pairs={{0,8},{8,0},{16,24},{24,16},{1,9},{9,1},{17,25},{25,17},{2,10},{10... | collective-permute-start | bytes 98312 | tf_op jit(solution)/shard_map/ppermute | solution.py:792
  97.9 1.5 collective-permute-start.17
  99.4 0.6 collective-permute-done.10.rest_2_
  100.0 2.4 %collective-permute-start.18 = (f32[2,32,128]{2,1,0:T(8,128)S(1)}, f32[2,32,128]{2,1,0:T(8,128)S(1)}, u32[]{:S(2)}, u32[]{:S(2)}) collective-permute-start(f32[2,32,128]{2,1,0:T(8,128)S(1)} %add_add_fusion.rest_0_), channel_id=1, source_target_pairs={{0,24},{8,16},{16,8},{24,0},{1,25},{9,17},{17,9},{25,1},{2,26},{10... | collective-permute-start | bytes 98312 | tf_op jit(solution)/shard_map/ppermute | solution.py:792
  102.4 0.6 copy-done.12
  103.0 17.8 %capacity.1 = (f32[32,32,128]{2,1,0:T(8,128)}, f32[32,32,128]{2,1,0:T(8,128)}) custom-call(f32[32]{0:T(128)} %rest_4_.1, f32[2,2,32,128]{3,2,1,0:T(8,128)} %copy-done.2, f32[2,2,32,128]{3,2,1,0:T(8,128)} %copy-done.10, f32[2,2,32,128]{3,2,1,0:T(8,128)} %copy-done.11, f32[2,2,32,128]{3,2,1,0:T(8,128)} %copy-done.12), custom_call_target="tpu_custom_call" | custom-call | bytes 1310848 | tf_op jit(solution)/shard_map/capacity/pallas_call | solution.py:764
  120.8 0.0 collective-permute-done.18.rest_3_
  120.9 0.6 copy-done.13
  121.4 0.0 copy-done.14
  121.4 0.0 copy-done.15
  121.5 3.8 %slabs.1 = (f32[2,32,128]{2,1,0:T(8,128)}, f32[2,32,128]{2,1,0:T(8,128)}, f32[2,32,128]{2,1,0:T(8,128)}, f32[2,32,128]{2,1,0:T(8,128)}) custom-call(f32[32]{0:T(128)} %rest_4_.1, f32[32,32,128]{2,1,0:T(8,128)} %get-tuple-element.39.first_matrix, f32[32,32,128]{2,1,0:T(8,128)} %get-tuple-element.40.second_matrix, f32[2,32,128]{2,1,0:T(8,128)} %copy-done.6, ...), custom_call_target="tpu_custom_call" | custom-call | bytes 1310848 | tf_op jit(solution)/shard_map/slabs/pallas_call | solution.py:764
  125.2 0.5 collective-permute-start.19
  125.8 0.6 collective-permute-start.20
  126.4 2.3 %collective-permute-start.21 = (f32[2,32,128]{2,1,0:T(8,128)}, f32[2,32,128]{2,1,0:T(8,128)S(1)}, u32[]{:S(2)}, u32[]{:S(2)}) collective-permute-start(f32[2,32,128]{2,1,0:T(8,128)} %get-tuple-element.44), channel_id=1, source_target_pairs={{0,24},{8,16},{16,8},{24,0},{1,25},{9,17},{17,9},{25,1},{2,26},{10... | collective-permute-start | bytes 98312 | tf_op jit(solution)/shard_map/ppermute | solution.py:792
  128.7 0.6 collective-permute-done.19.rest_5_
  129.4 0.5 collective-permute-done.20.rest_6_
  129.9 1.5 collective-permute-done.21.rest_7_
  131.4 0.6 copy-done.18
  132.0 10.8 %sides.1 = (f32[2,32,128]{2,1,0:T(8,128)}, f32[2,1024,128]{2,1,0:T(8,128)}) custom-call(f32[1024,128]{1,0:T(8,128)} %constant.24.clone.lam.rest_0_, f32[1024,128]{1,0:T(8,128)} %constant.25.clone.ends.rest_1_, f32[8,128]{1,0:T(8,128)} %constant.26.clone.mu.rest_2_, f32[32]{0:T(128)} %rest_3_.13, f32[32]{0:T(128)} %rest_4_.1, f32[32]{0:T(128)} %rest_5_.1, ...), custom_call_target="tpu_custom_call" | custom-call | bytes 2265600 | tf_op jit(solution)/shard_map/sides/pallas_call | solution.py:764
  142.9 0.8 copy-done.1
  143.6 9.3 %backward.1 = f32[1024,4,128]{2,1,0:T(4,128)} custom-call(f32[4,1024,128]{2,1,0:T(8,128)} %get-tuple-element.26.spectrum, f32[2,512,128]{2,1,0:T(8,128)} %get-tuple-element.37.own, f32[2,512,128]{2,1,0:T(8,128)} %copy-done.1, f32[2,1024,128]{2,1,0:T(8,128)} %get-tuple-element.45.extra, f32[2,32,128]{2,1,0:T(8,128)} %get-tuple-element.46.sources, ...), custom_call_target="tpu_custom_call" | custom-call | bytes 9736704 | tf_op jit(solution)/shard_map/backward/pallas_call | solution.py:764
  (33 shorter events, 0.1 us)
Async XLA Ops:
  13.9 4.0 %collective-permute-start = (f32[2,512,128]{2,1,0:T(8,128)}, f32[2,512,128]{2,1,0:T(8,128)S(1)}, u32[]{:S(2)}, u32[]{:S(2)}) collective-permute-start(f32[2,512,128]{2,1,0:T(8,128)} %get-tuple-element.28), channel_id=1, source_target_pairs={{0,1},{1,0},{2,3},{3,2},{4,5},{5,4},{6,7},{7,6},{8,9},{9,8},{10,11... | collective-permute-start | bytes 1572872 | tf_op jit(solution)/shard_map/ppermute | solution.py:778
  17.9 0.8 copy-start
  21.6 9.8 %collective-permute-start.1 = (f32[2,128,128]{2,1,0:T(8,128)}, f32[2,128,128]{2,1,0:T(8,128)S(1)}, u32[]{:S(2)}, u32[]{:S(2)}) collective-permute-start(f32[2,128,128]{2,1,0:T(8,128)} %get-tuple-element.30), channel_id=1, source_target_pairs={{0,2},{1,3},{2,4},{3,5},{4,6},{5,7},{6,0},{7,1},{8,10},{9,11},{10,... | collective-permute-start | bytes 393224 | tf_op jit(solution)/shard_map/ppermute | solution.py:788
  24.2 12.1 %collective-permute-start.2 = (f32[2,128,128]{2,1,0:T(8,128)}, f32[2,128,128]{2,1,0:T(8,128)S(1)}, u32[]{:S(2)}, u32[]{:S(2)}) collective-permute-start(f32[2,128,128]{2,1,0:T(8,128)} %get-tuple-element.31), channel_id=1, source_target_pairs={{0,4},{1,5},{2,6},{3,7},{4,0},{5,1},{6,2},{7,3},{8,12},{9,13},{10,... | collective-permute-start | bytes 393224 | tf_op jit(solution)/shard_map/ppermute | solution.py:788
  26.8 9.5 %collective-permute-start.3 = (f32[2,128,128]{2,1,0:T(8,128)}, f32[2,128,128]{2,1,0:T(8,128)S(1)}, u32[]{:S(2)}, u32[]{:S(2)}) collective-permute-start(f32[2,128,128]{2,1,0:T(8,128)} %get-tuple-element.32), channel_id=1, source_target_pairs={{0,6},{1,7},{2,0},{3,1},{4,2},{5,3},{6,4},{7,5},{8,14},{9,15},{10,... | collective-permute-start | bytes 393224 | tf_op jit(solution)/shard_map/ppermute | solution.py:788
  31.4 4.9 %copy-start.3 = (f32[2,128,128]{2,1,0:T(8,128)}, f32[2,128,128]{2,1,0:T(8,128)S(1)}, u32[]{:S(2)}) copy-start(f32[2,128,128]{2,1,0:T(8,128)S(1)} %collective-permute-done.1.rest_1_) | copy-start | bytes 393220
  36.3 0.7 copy-start.4
  36.3 0.7 copy-start.5
  39.5 9.0 %collective-permute-start.4 = (f32[2,128,128]{2,1,0:T(8,128)}, f32[2,128,128]{2,1,0:T(8,128)S(1)}, u32[]{:S(2)}, u32[]{:S(2)}) collective-permute-start(f32[2,128,128]{2,1,0:T(8,128)} %get-tuple-element.34), channel_id=1, source_target_pairs={{0,2},{1,3},{2,4},{3,5},{4,6},{5,7},{6,0},{7,1},{8,10},{9,11},{10,... | collective-permute-start | bytes 393224 | tf_op jit(solution)/shard_map/ppermute | solution.py:788
  42.8 10.4 %collective-permute-start.5 = (f32[2,128,128]{2,1,0:T(8,128)}, f32[2,128,128]{2,1,0:T(8,128)S(1)}, u32[]{:S(2)}, u32[]{:S(2)}) collective-permute-start(f32[2,128,128]{2,1,0:T(8,128)} %get-tuple-element.35), channel_id=1, source_target_pairs={{0,4},{1,5},{2,6},{3,7},{4,0},{5,1},{6,2},{7,3},{8,12},{9,13},{10,... | collective-permute-start | bytes 393224 | tf_op jit(solution)/shard_map/ppermute | solution.py:788
  44.4 8.7 %collective-permute-start.6 = (f32[2,128,128]{2,1,0:T(8,128)}, f32[2,128,128]{2,1,0:T(8,128)S(1)}, u32[]{:S(2)}, u32[]{:S(2)}) collective-permute-start(f32[2,128,128]{2,1,0:T(8,128)} %get-tuple-element.36), channel_id=1, source_target_pairs={{0,6},{1,7},{2,0},{3,1},{4,2},{5,3},{6,4},{7,5},{8,14},{9,15},{10,... | collective-permute-start | bytes 393224 | tf_op jit(solution)/shard_map/ppermute | solution.py:788
  48.5 4.7 %copy-start.7 = (f32[2,128,128]{2,1,0:T(8,128)}, f32[2,128,128]{2,1,0:T(8,128)S(1)}, u32[]{:S(2)}) copy-start(f32[2,128,128]{2,1,0:T(8,128)S(1)} %collective-permute-done.4.rest_1_) | copy-start | bytes 393220
  53.2 0.7 copy-start.8
  53.2 0.7 copy-start.9
  57.1 85.7 %collective-permute-start.7 = (f32[2,512,128]{2,1,0:T(8,128)}, f32[2,512,128]{2,1,0:T(8,128)S(1)}, u32[]{:S(2)}, u32[]{:S(2)}) collective-permute-start(f32[2,512,128]{2,1,0:T(8,128)} %get-tuple-element.38), channel_id=1, source_target_pairs={{0,1},{1,0},{2,3},{3,2},{4,5},{5,4},{6,7},{7,6},{8,9},{9,8},{10,11... | collective-permute-start | bytes 1572872 | tf_op jit(solution)/shard_map/ppermute | solution.py:778
  71.1 12.2 %collective-permute-start.12 = (f32[2,32,128]{2,1,0:T(8,128)}, f32[2,32,128]{2,1,0:T(8,128)S(1)}, u32[]{:S(2)}, u32[]{:S(2)}) collective-permute-start(f32[2,32,128]{2,1,0:T(8,128)} %ends.3), channel_id=1, source_target_pairs={{0,1},{1,0},{2,3},{3,2},{4,5},{5,4},{6,7},{7,6},{8,9},{9,8},{10,11... | collective-permute-start | bytes 98312 | tf_op jit(solution)/shard_map/ppermute | solution.py:778
  83.3 5.9 %collective-permute-start.8 = (f32[2,32,128]{2,1,0:T(8,128)}, f32[2,32,128]{2,1,0:T(8,128)S(1)}, u32[]{:S(2)}, u32[]{:S(2)}) collective-permute-start(f32[2,32,128]{2,1,0:T(8,128)} %response.1), channel_id=1, source_target_pairs={{0,1},{1,0},{2,3},{3,2},{4,5},{5,4},{6,7},{7,6},{8,9},{9,8},{10,11... | collective-permute-start | bytes 98312 | tf_op jit(solution)/shard_map/ppermute | solution.py:778
  84.1 9.7 %collective-permute-start.15 = (f32[2,32,128]{2,1,0:T(8,128)S(1)}, f32[2,32,128]{2,1,0:T(8,128)S(1)}, u32[]{:S(2)}, u32[]{:S(2)}) collective-permute-start(f32[2,32,128]{2,1,0:T(8,128)S(1)} %add.12), channel_id=1, source_target_pairs={{0,6},{1,7},{2,0},{3,1},{4,2},{5,3},{6,4},{7,5},{8,14},{9,15},{10,... | collective-permute-start | bytes 98312 | tf_op jit(solution)/shard_map/ppermute | solution.py:788
  88.6 5.8 %collective-permute-start.13 = (f32[2,32,128]{2,1,0:T(8,128)S(1)}, f32[2,32,128]{2,1,0:T(8,128)S(1)}, u32[]{:S(2)}, u32[]{:S(2)}) collective-permute-start(f32[2,32,128]{2,1,0:T(8,128)S(1)} %add.12), channel_id=1, source_target_pairs={{0,2},{1,3},{2,4},{3,5},{4,6},{5,7},{6,0},{7,1},{8,10},{9,11},{10,... | collective-permute-start | bytes 98312 | tf_op jit(solution)/shard_map/ppermute | solution.py:788
  88.6 7.6 %collective-permute-start.14 = (f32[2,32,128]{2,1,0:T(8,128)S(1)}, f32[2,32,128]{2,1,0:T(8,128)S(1)}, u32[]{:S(2)}, u32[]{:S(2)}) collective-permute-start(f32[2,32,128]{2,1,0:T(8,128)S(1)} %add.12), channel_id=1, source_target_pairs={{0,4},{1,5},{2,6},{3,7},{4,0},{5,1},{6,2},{7,3},{8,12},{9,13},{10,... | collective-permute-start | bytes 98312 | tf_op jit(solution)/shard_map/ppermute | solution.py:788
  90.0 12.4 %copy-start.2 = (f32[2,2,32,128]{3,2,1,0:T(8,128)}, f32[2,2,32,128]{3,2,1,0:T(8,128)S(1)}, u32[]{:S(2)}) copy-start(f32[2,2,32,128]{3,2,1,0:T(8,128)S(1)} %pad_maximum_fusion.rest_0_) | copy-start | bytes 196612
  90.0 7.8 %collective-permute-start.9 = (f32[2,2,32,128]{3,2,1,0:T(8,128)S(1)}, f32[2,2,32,128]{3,2,1,0:T(8,128)S(1)}, u32[]{:S(2)}, u32[]{:S(2)}) collective-permute-start(f32[2,2,32,128]{3,2,1,0:T(8,128)S(1)} %pad_maximum_fusion.rest_0_), channel_id=1, source_target_pairs={{0,2},{1,3},{2,4},{3,5},{4,6},{5,7},{6,0},{7,1},{8,10},{9,11},{10,... | collective-permute-start | bytes 196616 | tf_op jit(solution)/shard_map/ppermute | solution.py:788
  93.8 6.2 %collective-permute-start.10 = (f32[2,2,32,128]{3,2,1,0:T(8,128)S(1)}, f32[2,2,32,128]{3,2,1,0:T(8,128)S(1)}, u32[]{:S(2)}, u32[]{:S(2)}) collective-permute-start(f32[2,2,32,128]{3,2,1,0:T(8,128)S(1)} %pad_maximum_fusion.rest_0_), channel_id=1, source_target_pairs={{0,4},{1,5},{2,6},{3,7},{4,0},{5,1},{6,2},{7,3},{8,12},{9,13},{10,... | collective-permute-start | bytes 196616 | tf_op jit(solution)/shard_map/ppermute | solution.py:788
  94.4 8.0 %collective-permute-start.11 = (f32[2,2,32,128]{3,2,1,0:T(8,128)S(1)}, f32[2,2,32,128]{3,2,1,0:T(8,128)S(1)}, u32[]{:S(2)}, u32[]{:S(2)}) collective-permute-start(f32[2,2,32,128]{3,2,1,0:T(8,128)S(1)} %pad_maximum_fusion.rest_0_), channel_id=1, source_target_pairs={{0,6},{1,7},{2,0},{3,1},{4,2},{5,3},{6,4},{7,5},{8,14},{9,15},{10,... | collective-permute-start | bytes 196616 | tf_op jit(solution)/shard_map/ppermute | solution.py:788
  96.3 24.6 %copy-start.6 = (f32[2,32,128]{2,1,0:T(8,128)}, f32[2,32,128]{2,1,0:T(8,128)S(1)}, u32[]{:S(2)}) copy-start(f32[2,32,128]{2,1,0:T(8,128)S(1)} %add_add_fusion.rest_0_) | copy-start | bytes 98308
  96.3 24.5 %collective-permute-start.16 = (f32[2,32,128]{2,1,0:T(8,128)S(1)}, f32[2,32,128]{2,1,0:T(8,128)S(1)}, u32[]{:S(2)}, u32[]{:S(2)}) collective-permute-start(f32[2,32,128]{2,1,0:T(8,128)S(1)} %add_add_fusion.rest_0_), channel_id=1, source_target_pairs={{0,8},{8,0},{16,24},{24,16},{1,9},{9,1},{17,25},{25,17},{2,10},{10... | collective-permute-start | bytes 98312 | tf_op jit(solution)/shard_map/ppermute | solution.py:792
  97.9 4.5 %copy-start.10 = (f32[2,2,32,128]{3,2,1,0:T(8,128)}, f32[2,2,32,128]{3,2,1,0:T(8,128)S(1)}, u32[]{:S(2)}) copy-start(f32[2,2,32,128]{3,2,1,0:T(8,128)S(1)} %collective-permute-done.9.rest_1_) | copy-start | bytes 196612
  97.9 23.0 %collective-permute-start.17 = (f32[2,32,128]{2,1,0:T(8,128)S(1)}, f32[2,32,128]{2,1,0:T(8,128)S(1)}, u32[]{:S(2)}, u32[]{:S(2)}) collective-permute-start(f32[2,32,128]{2,1,0:T(8,128)S(1)} %add_add_fusion.rest_0_), channel_id=1, source_target_pairs={{0,16},{8,24},{16,0},{24,8},{1,17},{9,25},{17,1},{25,9},{2,18},{10... | collective-permute-start | bytes 98312 | tf_op jit(solution)/shard_map/ppermute | solution.py:792
  100.0 2.5 %copy-start.11 = (f32[2,2,32,128]{3,2,1,0:T(8,128)}, f32[2,2,32,128]{3,2,1,0:T(8,128)S(1)}, u32[]{:S(2)}) copy-start(f32[2,2,32,128]{3,2,1,0:T(8,128)S(1)} %collective-permute-done.10.rest_2_) | copy-start | bytes 196612
  100.0 20.9 %collective-permute-start.18 = (f32[2,32,128]{2,1,0:T(8,128)S(1)}, f32[2,32,128]{2,1,0:T(8,128)S(1)}, u32[]{:S(2)}, u32[]{:S(2)}) collective-permute-start(f32[2,32,128]{2,1,0:T(8,128)S(1)} %add_add_fusion.rest_0_), channel_id=1, source_target_pairs={{0,24},{8,16},{16,8},{24,0},{1,25},{9,17},{17,9},{25,1},{2,26},{10... | collective-permute-start | bytes 98312 | tf_op jit(solution)/shard_map/ppermute | solution.py:792
  102.4 0.6 copy-start.12
  120.8 0.6 copy-start.13
  120.8 0.6 copy-start.14
  120.9 0.6 copy-start.15
  125.2 4.1 %collective-permute-start.19 = (f32[2,32,128]{2,1,0:T(8,128)}, f32[2,32,128]{2,1,0:T(8,128)S(1)}, u32[]{:S(2)}, u32[]{:S(2)}) collective-permute-start(f32[2,32,128]{2,1,0:T(8,128)} %get-tuple-element.42), channel_id=1, source_target_pairs={{0,8},{8,0},{16,24},{24,16},{1,9},{9,1},{17,25},{25,17},{2,10},{10... | collective-permute-start | bytes 98312 | tf_op jit(solution)/shard_map/ppermute | solution.py:792
  125.8 4.1 %collective-permute-start.20 = (f32[2,32,128]{2,1,0:T(8,128)}, f32[2,32,128]{2,1,0:T(8,128)S(1)}, u32[]{:S(2)}, u32[]{:S(2)}) collective-permute-start(f32[2,32,128]{2,1,0:T(8,128)} %get-tuple-element.43), channel_id=1, source_target_pairs={{0,16},{8,24},{16,0},{24,8},{1,17},{9,25},{17,1},{25,9},{2,18},{10... | collective-permute-start | bytes 98312 | tf_op jit(solution)/shard_map/ppermute | solution.py:792
  126.4 5.0 %collective-permute-start.21 = (f32[2,32,128]{2,1,0:T(8,128)}, f32[2,32,128]{2,1,0:T(8,128)S(1)}, u32[]{:S(2)}, u32[]{:S(2)}) collective-permute-start(f32[2,32,128]{2,1,0:T(8,128)} %get-tuple-element.44), channel_id=1, source_target_pairs={{0,24},{8,16},{16,8},{24,0},{1,25},{9,17},{17,9},{25,1},{2,26},{10... | collective-permute-start | bytes 98312 | tf_op jit(solution)/shard_map/ppermute | solution.py:792
  129.4 2.1 %copy-start.16 = (f32[2,32,128]{2,1,0:T(8,128)}, f32[2,32,128]{2,1,0:T(8,128)S(1)}, u32[]{:S(2)}) copy-start(f32[2,32,128]{2,1,0:T(8,128)S(1)} %collective-permute-done.19.rest_5_) | copy-start | bytes 98308
  129.9 1.5 copy-start.17
  131.4 0.6 copy-start.18
  142.9 0.8 copy-start.1

commit v2 on v1

v2 whole, which is shorter than its diff:
```python
import functools
import math

import jax
import jax.numpy as jnp
import ml_dtypes
import numpy as np
from jax import lax
from jax.experimental import pallas as pl
from jax.experimental.pallas import tpu as pltpu
from jax.sharding import PartitionSpec as P

F32 = jnp.float32
BF16 = jnp.bfloat16
CELLS = 4
SLABS = 4
LANES = 128


def two_halves(table):
    high = table.astype(np.float32).astype(ml_dtypes.bfloat16)
    low = (table - high.astype(np.float64)).astype(np.float32).astype(ml_dtypes.bfloat16)
    return high, low


def cosine_basis(depth):
    rows = np.arange(depth)
    phases = (2 * rows[:, None] + 1) * rows[None, :] % (4 * depth)
    scales = np.where(rows == 0, math.sqrt(1.0 / depth), math.sqrt(2.0 / depth))
    return np.cos(math.pi / (2 * depth) * phases) * scales[None, :]


def wide_basis(basis):
    high, low = two_halves(basis)
    top = np.concatenate([high, low], axis=1)
    bottom = np.concatenate([high, np.zeros_like(high)], axis=1)
    return np.concatenate([top, bottom], axis=0)


def slab_tables(length):
    quarter = length // 8
    half = quarter // 2
    offsets = np.arange(quarter) + 0.5
    stage = np.zeros((4, 2 * quarter, 2 * quarter))
    modes = np.zeros((4, 2 * quarter), np.int64)

    def angle(mode):
        return 2 * np.pi * (mode[:, None] * offsets[None, :] % length) / length

    def scale(mode):
        single = (mode == 0) | (mode == length // 2)
        return np.where(single, np.sqrt(1 / length), np.sqrt(2 / length))[:, None]

    steps = np.arange(half)
    for first, mode, column, wave in (
        (0, 8 * steps, 0, np.cos),
        (half, 8 * steps + 4, quarter, np.cos),
        (quarter, 8 * (steps + 1), 0, np.sin),
        (quarter + half, 8 * steps + 4, quarter, np.sin),
    ):
        stage[0, first : first + half, column : column + quarter] = scale(mode) * wave(angle(mode))
        modes[0, first : first + half] = mode
    for slot in (1, 2, 3):
        mode = slot + 8 * np.arange(quarter)
        cosine, sine = scale(mode) * np.cos(angle(mode)), scale(mode) * np.sin(angle(mode))
        stage[slot] = np.block([[cosine, sine], [sine, -cosine]])
        modes[slot] = np.concatenate([mode, mode])
    modes = modes.reshape(-1)
    parity = np.tile(np.repeat([1, -1], quarter), 4)
    single = (modes == 0) | (modes == length // 2)
    size = np.where(single, np.sqrt(1 / length), np.sqrt(2 / length))
    ends = size * np.where(parity > 0, np.cos(np.pi * modes / length), np.sin(np.pi * modes / length))
    eigen = 2.0 - 2.0 * np.cos(2 * np.pi * modes / length)
    return stage, eigen, ends, parity


def spread(column):
    return np.broadcast_to(column[..., None], column.shape + (LANES,)).astype(np.float32)


def split(values):
    high = values.astype(BF16)
    low = (values - high.astype(F32)).astype(BF16)
    return high, low


def dot(left, right):
    return jnp.dot(left, right, preferred_element_type=F32)


def times_basis(values, wide):
    high, low = split(values)
    both = dot(jnp.concatenate([high, low], axis=1), wide)
    depth = values.shape[1]
    return both[:, :depth] + both[:, depth:]


class Radial:
    def __init__(self, helmholtz, azimuth, vertical, radial, total):
        self.refs = (helmholtz, azimuth, vertical, radial)
        self.total = total

    def coupling(self, cell):
        cell = jnp.asarray(cell, jnp.int32)
        return jnp.where(cell < self.total - 1, self.refs[3][cell], 0.0)

    def previous(self, cell):
        cell = jnp.asarray(cell, jnp.int32)
        return jnp.where(cell > 0, self.refs[3][jnp.maximum(cell - 1, 0)], 0.0)

    def diagonal(self, cell, lam, mu):
        base = self.refs[0][cell] + self.coupling(cell) + self.previous(cell)
        return lam * self.refs[1][cell] + (mu * self.refs[2][cell] + base)


def inverse(values):
    return pl.reciprocal(values, approx=False)


def solve_block(radial, first, lam, mu, right, add_first=None, add_last=None):
    rows = []
    factor = values = None
    for place in range(CELLS):
        cell = first + place
        diagonal = radial.diagonal(cell, lam, mu)
        if place == 0 and add_first is not None:
            diagonal = diagonal - add_first
        if place == CELLS - 1 and add_last is not None:
            diagonal = diagonal - add_last
        if place > 0:
            before = radial.previous(cell)
            pivot = inverse(diagonal - before * factor)
            values = (right[place] + before * values) * pivot
        else:
            pivot = inverse(diagonal)
            values = right[place] * pivot
        factor = radial.coupling(cell) * pivot
        rows.append((values, factor))
    answer = [rows[-1][0]]
    for values, factor in rows[-2::-1]:
        answer.insert(0, values + factor * answer[0])
    return answer


def block_ports(radial, first, lam, mu):
    diagonals = [radial.diagonal(first + place, lam, mu) for place in range(CELLS)]
    pivot = inverse(diagonals[0])
    forward = [pivot]
    for place in range(1, CELLS):
        before = radial.previous(first + place)
        pivot = inverse(diagonals[place] - before * before * pivot)
        forward.append(pivot)
    last = forward[-1]
    cross = last
    for place in range(CELLS - 2, -1, -1):
        cross = radial.coupling(first + place) * forward[place] * cross
    backward = inverse(diagonals[-1])
    for place in range(CELLS - 2, -1, -1):
        after = radial.coupling(first + place)
        backward = inverse(diagonals[place] - after * after * backward)
    entry, leave = radial.previous(first), radial.coupling(first + CELLS - 1)
    return backward * entry, cross * leave, cross * entry, last * leave


def chip_ports(radial, first, lam, mu):
    b1, g1, b2, g2 = block_ports(radial, first, lam, mu)
    c1, h1, c2, h2 = block_ports(radial, first + CELLS, lam, mu)
    mid = inverse(1.0 - g2 * c1)
    low = c1 * b2 * mid
    high = h1 * mid
    whole = (
        b1 + g1 * low,
        g1 * high,
        c2 * (b2 + g2 * low),
        h2 + c2 * g2 * high,
    )
    return (b1, g1, b2, g2), (c1, h1, c2, h2), mid, whole


def spread_parts(x):
    root = math.sqrt(0.5)
    s = [x[n] + x[n + 4] for n in range(4)]
    d = [x[n] - x[n + 4] for n in range(4)]
    even, odd = s[0] + s[2], s[1] + s[3]
    minus, plus = root * (d[1] - d[3]), root * (d[1] + d[3])
    return (
        even + odd,
        even - odd,
        d[0] + minus,
        -plus - d[2],
        s[0] - s[2],
        s[3] - s[1],
        d[0] - minus,
        d[2] - plus,
    )


def gather_parts(y):
    root = math.sqrt(0.5)
    plus, minus = y[0] + y[1], y[0] - y[1]
    s = (plus + y[4], minus - y[5], plus - y[4], minus + y[5])
    real, imag = root * (y[2] - y[6]), root * (y[3] + y[7])
    d = (y[2] + y[6], real - imag, y[7] - y[3], -real - imag)
    return [s[n] + d[n] for n in range(4)] + [s[n] - d[n] for n in range(4)]


def forward_kernel(total, source_in, tables_in, stages_in, *rest):
    scalars_in = rest[:4]
    spectrum, keep, send = rest[4:7]
    source, tables, stages, s0, s1, s2, s3, wide_rows, high, low, sems = rest[7:]
    scalars = (s0, s1, s2, s3)
    pairs = [(source_in, source), (stages_in, stages), (tables_in, tables)]
    pairs += list(zip(scalars_in, scalars))
    copies = [
        pltpu.make_async_copy(origin, target, sems.at[place])
        for place, (origin, target) in enumerate(pairs)
    ]
    for copy in copies:
        copy.start()
    radial = Radial(*scalars, total)
    length = source.shape[0] // CELLS
    quarter = length // 8
    core = lax.rem(lax.axis_index("rad"), 2)
    first = lax.axis_index("rad") * CELLS
    chunk = 16
    copies[0].wait()
    for cell in range(CELLS):
        for start in range(0, quarter, chunk):
            x = [
                source[pl.ds((n * quarter + start) * CELLS + cell, chunk, stride=CELLS), :]
                for n in range(8)
            ]
            for place, part in enumerate(spread_parts(x)):
                one, two = split(part)
                row = cell * length + place * quarter + start
                wide_rows[row : row + chunk, :LANES] = one
                wide_rows[row : row + chunk, LANES:] = two
    copies[1].wait()
    wide = stages[8 * 2 * quarter : 8 * 2 * quarter + 2 * LANES, :]
    for cell in range(CELLS):
        for slot in range(4):
            row = cell * length + slot * 2 * quarter
            both = dot(wide_rows[row : row + 2 * quarter, :], wide)
            one, two = split(both[:, :LANES] + both[:, LANES:])
            columns = slice(cell * LANES, (cell + 1) * LANES)
            high[slot, :, columns] = one
            low[slot, :, columns] = two
    for slot in range(4):
        upper = stages[slot * 2 * quarter : (slot + 1) * 2 * quarter, :]
        lower = stages[(4 + slot) * 2 * quarter : (5 + slot) * 2 * quarter, :]
        result = dot(upper, high[slot]) + dot(upper, low[slot]) + dot(lower, high[slot])
        for cell in range(CELLS):
            spectrum[cell, slot * 2 * quarter : (slot + 1) * 2 * quarter, :] = result[
                :, cell * LANES : (cell + 1) * LANES
            ]
    for copy in copies[2:]:
        copy.wait()
    chunk = 64
    half = length // 2
    level = tables[length : length + 1, :]

    def step(index, _):
        ends = []
        for part in range(2):
            rows = pl.ds(pl.multiple_of(part * half + index * chunk, chunk), chunk)
            right = [spectrum[cell, rows, :] for cell in range(CELLS)]
            answer = solve_block(radial, first, tables[rows, :], level, right)
            ends.append((answer[0], answer[-1]))
        rows = pl.ds(pl.multiple_of(index * chunk, chunk), chunk)
        for place in range(2):
            keep[place, rows, :] = jnp.where(core == 0, ends[0][place], ends[1][place])
            send[place, rows, :] = jnp.where(core == 0, ends[1][place], ends[0][place])
        return 0

    lax.fori_loop(0, half // chunk, step, 0)


def shared_row(slot, kind, quarter):
    return pl.multiple_of(jnp.where(slot == 0, kind, slot + 1) * quarter, quarter)


def pair_ports_kernel(total, lam, mu, edges, *rest):
    radial = Radial(*rest[:4], total)
    (out,) = rest[4:]
    half = out.shape[1]
    quarter = half // 4
    chips = total // (2 * CELLS)
    core = lax.rem(lax.axis_index("rad"), 2)
    chip = lax.axis_index("rad") // 2
    left_side = chip < chips // 2
    first = chip * (2 * CELLS)
    level = mu[...][:1]
    chunk = min(64, quarter)

    def step(index, _):
        rows = pl.ds(pl.multiple_of(index * chunk, chunk), chunk)
        spot = pl.ds(pl.multiple_of(core * half + index * chunk, chunk), chunk)
        block = index * chunk // quarter
        start = shared_row(core * 2 + block // 2, lax.rem(block, 2), quarter)
        spot5 = pl.ds(pl.multiple_of(start + lax.rem(index * chunk, quarter), chunk), chunk)
        (b1, g1, b2, g2), (c1, h1, c2, h2), mid, (w1, w2, w3, w4) = chip_ports(
            radial, first, lam[spot, :], level
        )
        for place, value in enumerate((g1, b2, g2, c1, h1, c2, mid)):
            out[place, rows, :] = value
        left, right = edges[0, spot5, :], edges[1, spot5, :]
        far, near = jnp.where(left_side, left, right), jnp.where(left_side, right, left)
        rff, rnn = jnp.where(left_side, w1, w4), jnp.where(left_side, w4, w1)
        rfn, rnf = jnp.where(left_side, w2, w3), jnp.where(left_side, w3, w2)
        pivot = inverse(1.0 - rff * far)
        onward = rnn + rnf * far * rfn * pivot
        for place, value in enumerate(
            (rff, pivot, rfn * pivot, rnf, far, near, inverse(1.0 - near * onward))
        ):
            out[7 + place, rows, :] = value
        return 0

    lax.fori_loop(0, half // chunk, step, 0)


def merge_kernel(chips, keep, got, ports, whole, out):
    half = keep.shape[1]
    core = lax.rem(lax.axis_index("rad"), 2)
    left_side = lax.axis_index("rad") // 2 < chips // 2
    chunk = 32

    def step(index, _):
        rows = pl.ds(pl.multiple_of(index * chunk, chunk), chunk)
        g1, b2, g2, c1, h1, c2, mid = (ports[place, rows, :] for place in range(7))
        mine = [keep[place, rows, :] for place in range(2)]
        other = [got[place, rows, :] for place in range(2)]
        low = [jnp.where(core == 0, m, o) for m, o in zip(mine, other)]
        high = [jnp.where(core == 0, o, m) for m, o in zip(mine, other)]
        upper = (high[0] + c1 * low[1]) * mid
        first = low[0] + g1 * upper
        last = high[1] + c2 * (low[1] + g2 * upper)
        near = jnp.where(left_side, last, first)
        whole[0, rows, :] = jnp.where(left_side, first, last)
        whole[1, rows, :] = near
        out[rows, :] = near
        return 0

    lax.fori_loop(0, half // chunk, step, 0)


def inward_kernel(whole, incoming, ports, out):
    half = out.shape[0]
    chunk = 32

    def step(index, _):
        rows = pl.ds(pl.multiple_of(index * chunk, chunk), chunk)
        rff, pivot, _rfn, rnf, far = (ports[7 + place, rows, :] for place in range(5))
        value = incoming[rows, :]
        origin = (whole[0, rows, :] + rff * value) * pivot
        out[rows, :] = whole[1, rows, :] + rnf * (value + far * origin)
        return 0

    lax.fori_loop(0, half // chunk, step, 0)


def middle_kernel(chips, whole, incoming, own, other, ports, near_out, far_out):
    half = far_out.shape[0]
    chip = lax.axis_index("rad") // 2
    inner = (chip == chips // 2) | (chip == chips // 2 - 1)
    chunk = 32

    def step(index, _):
        rows = pl.ds(pl.multiple_of(index * chunk, chunk), chunk)
        rff, pivot, hold, _rnf, _far, near, close = (
            ports[7 + place, rows, :] for place in range(7)
        )
        value = (other[rows, :] + near * own[rows, :]) * close
        value = jnp.where(inner, value, 0.0)
        origin = (whole[0, rows, :] + rff * incoming[rows, :]) * pivot
        near_out[rows, :] = value
        far_out[rows, :] = origin + hold * value
        return 0

    lax.fori_loop(0, half // chunk, step, 0)


def outward_kernel(whole, incoming, near_in, ports, far_out):
    half = far_out.shape[0]
    chunk = 32

    def step(index, _):
        rows = pl.ds(pl.multiple_of(index * chunk, chunk), chunk)
        rff, pivot, hold = (ports[7 + place, rows, :] for place in range(3))
        origin = (whole[0, rows, :] + rff * incoming[rows, :]) * pivot
        far_out[rows, :] = origin + hold * near_in[rows, :]
        return 0

    lax.fori_loop(0, half // chunk, step, 0)


def parts_kernel(chips, keep, got, ports, whole, incoming, near_one, near_two, own, send):
    half = keep.shape[1]
    core = lax.rem(lax.axis_index("rad"), 2)
    left_side = lax.axis_index("rad") // 2 < chips // 2
    chunk = 32

    def step(index, _):
        rows = pl.ds(pl.multiple_of(index * chunk, chunk), chunk)
        _g1, b2, g2, c1, h1, _c2, mid = (ports[place, rows, :] for place in range(7))
        rff, pivot, hold, _rnf, far = (ports[7 + place, rows, :] for place in range(5))
        near = near_one[rows, :] + near_two[rows, :]
        value = incoming[rows, :]
        outer = value + far * ((whole[0, rows, :] + rff * value) * pivot + hold * near)
        left, right = jnp.where(left_side, outer, near), jnp.where(left_side, near, outer)
        last = jnp.where(core == 0, keep[1, rows, :], got[1, rows, :]) + b2 * left
        opening = jnp.where(core == 0, got[0, rows, :], keep[0, rows, :]) + h1 * right
        upper = (opening + c1 * last) * mid
        lower = last + g2 * upper
        own[0, rows, :] = jnp.where(core == 0, left, lower)
        own[1, rows, :] = jnp.where(core == 0, upper, right)
        send[0, rows, :] = jnp.where(core == 0, lower, left)
        send[1, rows, :] = jnp.where(core == 0, right, upper)
        return 0

    lax.fori_loop(0, half // chunk, step, 0)


def fold_rows(values):
    parts = [values[start : start + 8] for start in range(0, values.shape[0], 8)]
    while len(parts) > 1:
        parts = [a + b for a, b in zip(parts[::2], parts[1::2])]
    return parts[0]


def by_blocks(count, body, carry):
    def block(index, carry):
        for place in range(CELLS):
            carry = body(index * CELLS + place, carry)
        return carry

    return lax.fori_loop(0, lax.div(count, CELLS), block, carry)


def ratios(radial, first, lam, mu, left_store, right_store):
    total = radial.total
    shape = lam.shape

    def leftward(cell, factor):
        pivot = inverse(radial.diagonal(cell, lam, mu) - radial.previous(cell) * factor)
        factor = radial.coupling(cell) * pivot
        left_store[cell] = factor
        return factor

    def rightward(step, factor):
        cell = total - 1 - step
        pivot = inverse(radial.diagonal(cell, lam, mu) - radial.coupling(cell) * factor)
        factor = radial.previous(cell) * pivot
        right_store[cell] = factor
        return factor

    zero = jnp.zeros(shape, F32)
    left = by_blocks(first, leftward, zero)
    right = by_blocks(total - CELLS - first, rightward, zero)
    return left, right


def ratios_kernel(total, kept, lam, mu, *rest):
    radial = Radial(*rest[:4], total)
    edges, store = rest[4:]
    first = lax.axis_index("rad") * CELLS
    opening = lax.axis_index("rad") // 2 * (2 * CELLS)
    level = mu[...][:1]
    chunk = lam.shape[0] // 5

    def step(index, _):
        rows = pl.ds(pl.multiple_of(index * chunk, chunk), chunk)
        view = store.at[:, rows, :] if kept else store
        ratios(radial, first, lam[rows, :], level, view, view)
        left = view[jnp.maximum(opening - 1, 0)]
        right = view[jnp.minimum(opening + 2 * CELLS, total - 1)]
        edges[0, rows, :] = jnp.where(opening > 0, left, 0.0)
        edges[1, rows, :] = jnp.where(opening + 2 * CELLS < total, right, 0.0)
        return 0

    lax.fori_loop(0, 5, step, 0)


def outside(view, first, total):
    left = jnp.where(first > 0, view[jnp.maximum(first - 1, 0)], 0.0)
    right = view[jnp.minimum(first + CELLS, total - 1)]
    return left, jnp.where(first + CELLS < total, right, 0.0)


def stored_view(store, index, chunk):
    start = shared_row(index // 2, lax.rem(index, 2), chunk)
    return store.at[:, pl.ds(start, chunk), :]


def ends_kernel(total, kept, response, spectrum, lam, ends, mu, *rest):
    radial = Radial(*rest[:4], total)
    if kept:
        store, out, sums = rest[4:]
    else:
        out, sums, store = rest[4:]
    first = lax.axis_index("rad") * CELLS
    level = mu[...][:1]
    chunk = spectrum.shape[1] // 8
    sums[...] = jnp.zeros_like(sums)

    def step(index, _):
        kind = lax.rem(index, 2)
        rows = pl.ds(pl.multiple_of(index * chunk, chunk), chunk)
        values = lam[rows, :]
        if kept:
            view = stored_view(store, index, chunk)
            left, right = outside(view, first, total)
        else:
            view = store
            left, right = ratios(radial, first, values, level, store, store)
        weight = 2.0 * ends[rows, :]
        answer = solve_block(
            radial,
            first,
            values,
            level,
            [weight * spectrum[cell, rows, :] for cell in range(CELLS)],
            radial.previous(first) * left,
            radial.coupling(first + CELLS - 1) * right,
        )
        for place in range(CELLS):
            sums[kind, first + place] += fold_rows(answer[place])

        def outward_left(move, value):
            cell = first - 1 - move
            value = view[cell] * value
            sums[kind, cell] += fold_rows(value)
            return value

        def outward_right(move, value):
            cell = first + CELLS + move
            value = view[cell] * value
            sums[kind, cell] += fold_rows(value)
            return value

        by_blocks(first, outward_left, answer[0])
        by_blocks(total - CELLS - first, outward_right, answer[-1])
        return 0

    lax.fori_loop(0, 8, step, 0)
    for kind in range(2):
        for cell in range(total):
            out[kind, cell : cell + 1, :] = jnp.sum(sums[kind, cell], axis=0, keepdims=True)
    out[2:4] = response[...]


def join_kernel(own, other, out):
    out[0:2] = own[0:2] + other[0:2]
    out[2:4] = own[2:4]
    out[4:6] = other[2:4]


def total_kernel(*rest):
    pieces, out = rest[:-1], rest[-1]
    value = pieces[0][0:2]
    for piece in pieces[1:]:
        value = value + piece[0:2]
    out[...] = value


def response_kernel(total, lam, weight, mu, *rest):
    radial = Radial(*rest[:4], total)
    out, store, sums, lines = rest[4:]
    first = lax.axis_index("rad") * CELLS
    level = mu[pl.ds(lax.axis_index("az"), 1), :]
    group = LANES // SLABS
    chunk = lam.shape[1]
    sums[...] = jnp.zeros_like(sums)

    def step(index, _):
        kind = index
        values = lam[kind]
        left, right = ratios(radial, first, values, level, store, store)
        source = weight[kind]
        zero = jnp.zeros_like(source)
        openings, closings = [], []
        for place in range(CELLS):
            answer = solve_block(
                radial,
                first,
                values,
                level,
                [source if cell == place else zero for cell in range(CELLS)],
                radial.previous(first) * left,
                radial.coupling(first + CELLS - 1) * right,
            )
            for cell in range(CELLS):
                sums[kind, place, first + cell] += fold_rows(answer[cell])
            openings.append(answer[0])
            closings.append(answer[-1])

        def outward(cell, factor, edges):
            factor = store[cell] * factor
            for place in range(CELLS):
                sums[kind, place, cell] += fold_rows(factor * edges[place])
            return factor

        one = jnp.ones_like(source)
        by_blocks(first, lambda move, factor: outward(first - 1 - move, factor, openings), one)
        by_blocks(
            total - CELLS - first,
            lambda move, factor: outward(first + CELLS + move, factor, closings),
            one,
        )
        return 0

    lax.fori_loop(0, 2, step, 0)
    lane = lax.broadcasted_iota(jnp.int32, (1, LANES), 1) // group

    def close(cell, _):
        for kind in range(2):
            for place in range(CELLS):
                lines[kind, place, pl.ds(cell, 1), :] = jnp.sum(
                    sums[kind, place, cell], axis=0, keepdims=True
                )
        return 0

    lax.fori_loop(0, total, close, 0, unroll=8)
    for kind in range(2):
        result = jnp.zeros((total, LANES), F32)
        for place in range(CELLS):
            line = lines[kind, place]
            line = line + pltpu.roll(line, 2 * group, 1)
            line = line + pltpu.roll(line, group, 1)
            result = jnp.where(lane == place, line, result)
        out[kind] = result


def lane_groups():
    return lax.broadcasted_iota(jnp.int32, (1, LANES), 1) // (LANES // SLABS)


def to_all_groups(values, group):
    width = LANES // SLABS
    values = jnp.where(lane_groups() == group, values, 0.0)
    values = values + pltpu.roll(values, 2 * width, 1)
    return values + pltpu.roll(values, width, 1)


def fold_cells(values):
    width = values.shape[0] // SLABS
    result = values[:width]
    for group in range(1, SLABS):
        part = values[group * width : (group + 1) * width]
        result = jnp.where(lane_groups() == group, part, result)
    return result


def unfold_cells(values):
    return jnp.concatenate([to_all_groups(values, group) for group in range(SLABS)])


def invert(matrices, total):
    width = total // SLABS
    step_size = 8
    rows = lax.broadcasted_iota(jnp.int32, (width, LANES), 0)
    cells = rows + lane_groups() * width

    def step(panel, _):
        base = pl.multiple_of(panel * step_size, step_size)
        group = lax.div(base, width)
        spot_rows = pl.ds(pl.multiple_of(lax.rem(base, width), step_size), step_size)
        inside = (cells >= base) & (cells < base + step_size)
        state = []
        for matrix in matrices:
            lines = [matrix[base + place] for place in range(step_size)]
            corners = [
                to_all_groups(matrix[base + place, spot_rows, :], group)
                for place in range(step_size)
            ]
            state.append((lines, corners))
        for place in range(step_size):
            mark = cells == base + place
            spot = lax.broadcasted_iota(jnp.int32, (step_size, LANES), 0) == place
            for lines, corners in state:
                scale = inverse(corners[place][place : place + 1])
                line = jnp.where(mark, 1.0, lines[place]) * scale
                corner = jnp.where(spot, 1.0, corners[place]) * scale
                for row in range(step_size):
                    if row == place:
                        continue
                    factor = corners[row][place : place + 1]
                    lines[row] = jnp.where(mark, 0.0, lines[row]) - factor * line
                    corners[row] = jnp.where(spot, 0.0, corners[row]) - factor * corner
                lines[place], corners[place] = line, corner

        batch = 16

        def update(index, _):
            for matrix, (lines, _corners) in zip(matrices, state):
                spots = [index * batch + place for place in range(batch)]
                corners = [to_all_groups(matrix[spot, spot_rows, :], group) for spot in spots]
                values = [jnp.where(inside, 0.0, matrix[spot]) for spot in spots]
                for place in range(step_size):
                    values = [
                        value - corner[place : place + 1] * lines[place]
                        for value, corner in zip(values, corners)
                    ]
                for spot, value in zip(spots, values):
                    matrix[spot] = value
            return 0

        lax.fori_loop(0, total // batch, update, 0)
        for matrix, (lines, _corners) in zip(matrices, state):
            for place in range(step_size):
                matrix[base + place] = lines[place]
        return 0

    lax.fori_loop(0, total // step_size, step, 0)


def per_cell(total, azimuth, top):
    width = total // SLABS
    cells = lax.broadcasted_iota(jnp.int32, (width, LANES), 0) + lane_groups() * width

    def column(cell, value):
        return jnp.where(cells == cell, top / azimuth[cell], value)

    return lax.fori_loop(0, total, column, jnp.zeros((width, LANES), F32), unroll=8)


def capacity_kernel(total, chips, azimuth, *rest):
    pieces = rest[:chips]
    minus_out, alternate_out, pair_out = rest[chips:]
    chip = lax.axis_index("rad") // 2
    core = lax.rem(lax.axis_index("rad"), 2)
    width = total // SLABS
    shift = LANES // SLABS
    lane = lane_groups()
    cells = lax.broadcasted_iota(jnp.int32, (width, LANES), 0) + lane * width
    for distance, piece in enumerate(pieces):
        origin = lax.rem(chip + chips - distance, chips)
        for side in range(2):
            block = 2 * origin + lax.rem(core + side, 2)
            for kind in range(2):
                parts = [
                    piece[2 + 2 * side + kind, group * width : (group + 1) * width, :]
                    for group in range(SLABS)
                ]
                for place in range(CELLS):
                    row = jnp.zeros((width, LANES), F32)
                    for group, part in enumerate(parts):
                        turn = (group - place) % SLABS
                        part = pltpu.roll(part, turn * shift, 1) if turn else part
                        row = jnp.where(lane == group, part, row)
                    cell = block * CELLS + place
                    own = jnp.where(cells == cell, 0.5 / azimuth[cell], 0.0)
                    if kind == 0:
                        alternate_out[cell] = own + row
                        pair_out[cell] = own + row
                    else:
                        minus_out[cell] = own - row
    invert([minus_out, alternate_out], total)
    scale = per_cell(total, azimuth, 0.25)

    def add(cell, _):
        pair_out[cell] = pair_out[cell] + minus_out[cell] * scale * (1.0 / azimuth[cell])
        return 0

    lax.fori_loop(0, total, add, 0, unroll=8)
    invert([pair_out], total)


def apply_matrix(matrix, store, slots):
    total = matrix.shape[0]
    results = [[None] * 4 for _ in slots]
    for cell in range(total):
        line = matrix[cell]
        for place, slot in enumerate(slots):
            term = line * store[slot, cell : cell + 1, :]
            before = results[place][cell % 4]
            results[place][cell % 4] = term if before is None else before + term
    return [(r[0] + r[1]) + (r[2] + r[3]) for r in results]


def slabs_kernel(total, azimuth, minus_matrix, alternate_matrix, pair_matrix, *rest):
    pieces, outs = rest[:SLABS], rest[SLABS : 2 * SLABS]
    values, results, store = rest[2 * SLABS :]
    slab = lax.axis_index("az")
    width = total // SLABS
    shift = LANES // SLABS
    lane = lane_groups()
    for distance, piece in enumerate(pieces):
        values[slab ^ distance] = piece[...]

    def channels(kind):
        u = [values[place, kind] for place in range(SLABS)]
        mixed = (u[0] - u[2], u[3] - u[1], (u[0] + u[2]) - (u[1] + u[3]))
        return [to_all_groups(value, slab) for value in mixed]

    sums, differences = channels(0), channels(1)
    half = per_cell(total, azimuth, 0.5)
    for place in range(3):
        store[place] = differences[place]
    store[3] = -sums[2]
    lead_real, lead_imag, minus_alternate = apply_matrix(minus_matrix, store, (0, 1, 2))
    (plus_alternate,) = apply_matrix(alternate_matrix, store, (3,))
    store[4] = unfold_cells(-half * lead_imag - fold_cells(sums[0]))
    store[5] = unfold_cells(half * lead_real - fold_cells(sums[1]))
    plus_real, plus_imag = apply_matrix(pair_matrix, store, (4, 5))
    store[6] = unfold_cells(-half * plus_imag)
    store[7] = unfold_cells(half * plus_real)
    more_real, more_imag = apply_matrix(minus_matrix, store, (6, 7))
    found = (
        (plus_real, plus_imag, plus_alternate),
        (lead_real + more_real, lead_imag + more_imag, minus_alternate),
    )
    for kind, (real, imag, alternate) in enumerate(found):
        folded = (
            0.25 * (2.0 * real + alternate),
            0.25 * (-2.0 * imag - alternate),
            0.25 * (alternate - 2.0 * real),
            0.25 * (2.0 * imag - alternate),
        )
        for place, value in enumerate(folded):
            for group in range(SLABS):
                turn = lax.rem(slab - group + SLABS, SLABS) * shift
                rows = slice(group * width, (group + 1) * width)
                results[place, kind, rows, :] = jnp.where(
                    lane == slab, pltpu.roll(value, turn, 1), 0.0
                )
    for distance, out in enumerate(outs):
        out[...] = results[slab ^ distance]


def sides_kernel(total, kept, lam, ends, mu, *rest):
    radial = Radial(*rest[:4], total)
    pieces = rest[4 : 4 + SLABS]
    if kept:
        store, sources, out = rest[4 + SLABS :]
    else:
        sources, out, store = rest[4 + SLABS :]
    sources[...] = (pieces[0][...] + pieces[1][...]) + (pieces[2][...] + pieces[3][...])
    first = lax.axis_index("rad") * CELLS
    level = mu[...][:1]
    chunk = lam.shape[0] // 8

    def step(index, _):
        kind = lax.rem(index, 2)
        rows = pl.ds(pl.multiple_of(index * chunk, chunk), chunk)
        values = lam[rows, :]
        if kept:
            view = stored_view(store, index, chunk)
            left, right = outside(view, first, total)
        else:
            view = store
            left, right = ratios(radial, first, values, level, store, store)
        zero = jnp.zeros((chunk, LANES), F32)

        def passed(cell, value):
            return view[cell] * (sources[kind, pl.ds(cell, 1), :] + value)

        from_left = by_blocks(first, passed, zero)
        from_right = by_blocks(
            total - CELLS - first,
            lambda move, value: passed(total - 1 - move, value),
            zero,
        )
        entry, leave = radial.previous(first), radial.coupling(first + CELLS - 1)
        own = [sources[kind, pl.ds(first + place, 1), :] for place in range(CELLS)]
        own[0] = own[0] + from_left
        own[-1] = own[-1] + from_right
        answer = solve_block(radial, first, values, level, own, entry * left, leave * right)
        weight = ends[rows, :]
        out[0, rows, :] = weight * (from_left + entry * left * answer[0])
        out[1, rows, :] = weight * (from_right + leave * right * answer[-1])
        return 0

    lax.fori_loop(0, 8, step, 0)


def backward_kernel(total, spectrum, own, got, extra, sources, stages, lam, ends, mu, *rest):
    radial = Radial(*rest[:4], total)
    out, high, low, middle, wide_rows = rest[4:]
    length = spectrum.shape[1]
    quarter = length // 8
    core = lax.rem(lax.axis_index("rad"), 2)
    first = lax.axis_index("rad") * CELLS
    level = mu[...][:1]
    chunk = min(64, quarter)
    entry, leave = radial.previous(first), radial.coupling(first + CELLS - 1)

    for slot in range(4):

        def step(index, _):
            kind = index // (quarter // chunk)
            spot = pl.ds(pl.multiple_of(index * chunk, chunk), chunk)
            rows = pl.ds(pl.multiple_of(slot * 2 * quarter + index * chunk, chunk), chunk)
            near = pl.ds(pl.multiple_of(slot % 2 * 2 * quarter + index * chunk, chunk), chunk)
            mine = core == slot // 2
            side = [jnp.where(mine, own[place, near, :], got[place, near, :]) for place in range(2)]
            weight = ends[rows, :]
            right = [
                spectrum[cell, rows, :] + weight * sources[kind, pl.ds(first + cell, 1), :]
                for cell in range(CELLS)
            ]
            right[0] = right[0] + (entry * side[0] + extra[0, rows, :])
            right[-1] = right[-1] + (leave * side[1] + extra[1, rows, :])
            answer = solve_block(radial, first, lam[rows, :], level, right)
            for cell in range(CELLS):
                one, two = split(answer[cell])
                columns = slice(cell * LANES, (cell + 1) * LANES)
                high[slot, spot, columns] = one
                low[slot, spot, columns] = two
            return 0

        lax.fori_loop(0, 2 * quarter // chunk, step, 0)
        upper = stages[slot * 2 * quarter : (slot + 1) * 2 * quarter, :]
        lower = stages[(4 + slot) * 2 * quarter : (5 + slot) * 2 * quarter, :]
        middle[slot] = dot(upper, high[slot]) + dot(upper, low[slot]) + dot(lower, high[slot])
    chunk = 16
    wide = stages[8 * 2 * quarter : 8 * 2 * quarter + 2 * LANES, :]
    for cell in range(CELLS):
        columns = slice(cell * LANES, (cell + 1) * LANES)
        for start in range(0, quarter, chunk):
            y = [
                middle[place // 2, pl.ds(place % 2 * quarter + start, chunk), columns]
                for place in range(8)
            ]
            for place, value in enumerate(gather_parts(y)):
                one, two = split(value)
                row = place * quarter + start
                wide_rows[row : row + chunk, :LANES] = one
                wide_rows[row : row + chunk, LANES:] = two
        for start in range(0, length, 2 * quarter):
            both = dot(wide_rows[start : start + 2 * quarter, :], wide)
            out[pl.ds(start * CELLS + cell, 2 * quarter, stride=CELLS), :] = (
                both[:, :LANES] + both[:, LANES:]
            )


def call(kernel, out_shapes, args, scalars=(), scratch=(), cost=1, room=20, held=(), name=None):
    specs = []
    for place in range(len(args)):
        space = pltpu.SMEM if place in scalars else pltpu.HBM if place in held else pltpu.VMEM
        specs.append(pl.BlockSpec(memory_space=space))
    outs = [jax.ShapeDtypeStruct(shape, F32) for shape in out_shapes]
    return pl.pallas_call(
        kernel,
        out_shape=outs,
        in_specs=specs,
        out_specs=[pl.BlockSpec(memory_space=pltpu.VMEM)] * len(outs),
        scratch_shapes=list(scratch),
        compiler_params=pltpu.CompilerParams(vmem_limit_bytes=room * 2**20),
        cost_estimate=pl.CostEstimate(
            flops=0, bytes_accessed=int(cost * 3.69e6), transcendentals=0
        ),
        name=name,
    )(*args)


def other_core(values):
    count = lax.axis_size("rad")
    return lax.ppermute(values, "rad", [(index, index ^ 1) for index in range(count)])


def between_chips(values, pairs):
    route = [(2 * a + core, 2 * b + core) for a, b in pairs for core in range(2)]
    return lax.ppermute(values, "rad", route)


def along_chips(values, distance):
    chips = lax.axis_size("rad") // 2
    return between_chips(values, [(chip, (chip + distance) % chips) for chip in range(chips)])


def across_slabs(values, distance):
    return lax.ppermute(values, "az", [(slab, slab ^ distance) for slab in range(SLABS)])


def on_device(source, helmholtz, azimuth, vertical, radial):
    length, cells, depth = source.shape
    blocks = lax.axis_size("rad")
    chips = blocks // 2
    total = blocks * cells
    assert cells == CELLS and depth == LANES and lax.axis_size("az") == SLABS
    assert chips % 2 == 0
    half = length // 2
    quarter = length // 8
    scalars4 = (helmholtz, azimuth, vertical, radial)
    kept = total * 5 * quarter * LANES * 4 <= 12 * 2**20
    room = 20 if kept else 56

    basis = cosine_basis(depth)
    stage, eigen, end_weights, parity = slab_tables(length)

    def matrices(stages, last):
        high, low = two_halves(stages.reshape(-1, stages.shape[-1]))
        return jnp.asarray(np.concatenate([high, low, wide_basis(last)]))

    vertical_eigen = 2.0 - 2.0 * np.cos(math.pi / depth * np.arange(depth))
    levels = np.broadcast_to(vertical_eigen[None, :], (8, depth)).astype(np.float32)
    lam = jnp.asarray(spread(eigen))
    ends = jnp.asarray(spread(end_weights))
    mu = jnp.asarray(levels)
    tables = jnp.asarray(np.concatenate([spread(eigen), levels]))
    by_slot = eigen.reshape(4, 2, quarter)
    lam_shared = jnp.asarray(
        spread(np.concatenate([by_slot[0, 0], by_slot[0, 1], by_slot[1:, 0].reshape(-1)]))
    )
    group = depth // SLABS
    mu_groups = jnp.asarray(
        np.tile(vertical_eigen.reshape(SLABS, group), (1, SLABS)).astype(np.float32)
    )

    def packed(column):
        table = np.stack([column[parity > 0], column[parity < 0]]).reshape(2, quarter, SLABS)
        return jnp.asarray(np.repeat(table, group, axis=2).astype(np.float32))

    lam_groups = packed(eigen)
    weight_groups = packed(2.0 * end_weights**2)

    def smem(start):
        return tuple(range(start, start + 4))

    wide_shape = (2 * quarter, CELLS * LANES)
    stages = matrices(stage, basis)
    spectrum, keep, send = call(
        functools.partial(forward_kernel, total),
        [(CELLS, length, LANES), (2, half, LANES), (2, half, LANES)],
        (source.reshape(length * CELLS, LANES), tables, stages) + scalars4,
        (),
        [
            pltpu.VMEM((length * CELLS, LANES), F32),
            pltpu.VMEM(tables.shape, F32),
            pltpu.VMEM(stages.shape, BF16),
        ]
        + [pltpu.SMEM((total,), F32)] * 4
        + [pltpu.VMEM((length * CELLS, 2 * LANES), BF16)]
        + [pltpu.VMEM((4,) + wide_shape, BF16)] * 2
        + [pltpu.SemaphoreType.DMA((7,))],
        cost=8,
        held=tuple(range(7)),
        room=57,
        name="forward",
    )
    got = other_core(send)

    store_shape = (total, (5 if kept else 1) * quarter, LANES)
    edge_shape = (2, 5 * quarter, LANES)
    ratios_out = call(
        functools.partial(ratios_kernel, total, kept),
        [edge_shape] + ([store_shape] if kept else []),
        (lam_shared, mu) + scalars4,
        smem(2),
        [] if kept else [pltpu.VMEM(store_shape, F32)],
        cost=5,
        room=room,
        name="ratios",
    )
    edges, store = ratios_out[0], tuple(ratios_out[1:])
    scratch_store = [] if kept else [pltpu.VMEM(store_shape, F32)]

    (ports,) = call(
        functools.partial(pair_ports_kernel, total),
        [(14, half, LANES)],
        (lam, mu, edges) + scalars4,
        smem(3),
        cost=2,
        room=room,
        name="pair_ports",
    )
    line = (half, LANES)
    whole, out = call(
        functools.partial(merge_kernel, chips),
        [(2, half, LANES), line],
        (keep, got, ports),
        cost=0.3,
        room=room,
        name="merge",
    )
    out, spectrum_late, helmholtz_late = lax.optimization_barrier((out, spectrum, helmholtz))
    scalars_late = (helmholtz_late,) + scalars4[1:]
    (response,) = call(
        functools.partial(response_kernel, total),
        [(2, total, LANES)],
        (lam_groups, weight_groups, mu_groups) + scalars_late,
        smem(3),
        [
            pltpu.VMEM((total, quarter, LANES), F32),
            pltpu.VMEM((2, CELLS, total, 8, LANES), F32),
            pltpu.VMEM((2, CELLS, total, LANES), F32),
        ],
        cost=5,
        room=room,
        name="response",
    )
    (packed_ends,) = call(
        functools.partial(ends_kernel, total, kept),
        [(4, total, LANES)],
        (response, spectrum_late, lam, ends, mu) + scalars4 + store,
        smem(5),
        [pltpu.VMEM((2, total, 8, LANES), F32)] + scratch_store,
        cost=3,
        room=room,
        name="ends",
    )
    incoming = None
    (joint,) = call(
        join_kernel,
        [(6, total, LANES)],
        (packed_ends, other_core(packed_ends)),
        cost=0.3,
        room=room,
        name="join",
    )
    whole_late, joint = lax.optimization_barrier((whole, joint))
    for edge in range(chips // 2 - 1):
        moved = between_chips(out, [(edge, edge + 1), (chips - 1 - edge, chips - 2 - edge)])
        incoming = moved if incoming is None else incoming + moved
        (out,) = call(
            inward_kernel,
            [line],
            (whole_late, incoming, ports),
            cost=0.3,
            room=room,
            name="inward",
        )
    joints = [joint] + [along_chips(joint, d) for d in range(1, chips)]
    (slab_ends,) = call(
        total_kernel, [(2, total, LANES)], tuple(joints), cost=0.3, room=room, name="total"
    )
    all_ends = [slab_ends] + [across_slabs(slab_ends, d) for d in range(1, SLABS)]
    matrices3 = call(
        functools.partial(capacity_kernel, total, chips),
        [(total, total // SLABS, LANES)] * 3,
        (azimuth, *joints),
        (0,),
        cost=6,
        room=room,
        name="capacity",
    )
    low, high = chips // 2 - 1, chips // 2
    other = between_chips(out, [(low, high), (high, low)])
    whole_last, _, _ = lax.optimization_barrier((whole, matrices3[0], tuple(all_ends)))
    near, far = call(
        functools.partial(middle_kernel, chips),
        [line, line],
        (whole_last, incoming, out, other, ports),
        cost=0.3,
        room=room,
        name="middle",
    )
    passed = None
    for edge in range(chips // 2 - 2, -1, -1):
        moved = between_chips(far, [(edge + 1, edge), (chips - 2 - edge, chips - 1 - edge)])
        passed = moved if passed is None else passed + moved
        if edge > 0:
            (far,) = call(
                outward_kernel,
                [line],
                (whole, incoming, passed, ports),
                cost=0.3,
                room=room,
                name="outward",
            )
    own_sides, send_sides = call(
        functools.partial(parts_kernel, chips),
        [(2, half, LANES)] * 2,
        (keep, got, ports, whole, incoming, near, passed),
        cost=0.4,
        room=room,
        name="parts",
    )
    got_sides = other_core(send_sides)
    end_sources = call(
        functools.partial(slabs_kernel, total),
        [(2, total, LANES)] * SLABS,
        (azimuth, *matrices3, *all_ends),
        (0,),
        [pltpu.VMEM((SLABS, 2, total, LANES), F32)] * 2 + [pltpu.VMEM((8, total, LANES), F32)],
        cost=2,
        room=room,
        name="slabs",
    )
    sources = [end_sources[0]] + [across_slabs(end_sources[d], d) for d in range(1, SLABS)]
    all_sources, extra = call(
        functools.partial(sides_kernel, total, kept),
        [(2, total, LANES), (2, length, LANES)],
        (lam, ends, mu) + scalars4 + tuple(sources) + store,
        smem(3),
        scratch_store,
        cost=3,
        room=room,
        name="sides",
    )
    (pressure,) = call(
        functools.partial(backward_kernel, total),
        [(length * CELLS, LANES)],
        (
            spectrum,
            own_sides,
            got_sides,
            extra,
            all_sources,
            matrices(np.swapaxes(stage, 1, 2), basis.T),
            lam,
            ends,
            mu,
        )
        + scalars4,
        smem(9),
        [pltpu.VMEM((4,) + wide_shape, BF16)] * 2
        + [pltpu.VMEM((4,) + wide_shape, F32), pltpu.VMEM((length, 2 * LANES), BF16)],
        cost=7,
        room=room,
        name="backward",
    )
    return pressure.reshape(length, CELLS, LANES)


def solution(mesh):
    in_specs = (P("az", "rad", None), P(), P(), P(), P())
    return jax.shard_map(
        on_device,
        mesh=mesh,
        in_specs=in_specs,
        out_specs=P("az", "rad", None),
        check_vma=False,
    )
```

time: 153 us -> 82 us (0.54)
  Pallas kernels: 96.7 us -> 37.3 us
  starting transfers between devices: 32.9 us -> 18.7 us
  waiting for transfers between devices: 16.9 us -> 25.4 us
  local copies, waits for them, and re-layouts: 4.83 us -> 0.07 us
  other arithmetic: 1.54 us -> 0 us
    pallas_call x12 -> x15, Pallas kernels: 96.7 us -> 37.3 us  [call(): pl.pallas_call(kernel, out_shape=outs, in_specs=specs, out_specs=[pl.Bloc...]
    ppermute x12 -> x6, starting transfers between devices: 22.9 us -> 10.8 us  [between_chips(): return lax.ppermute(values, 'rad', route)]
    ppermute x12 -> x6, waiting for transfers between devices: 14.2 us -> 19.9 us  [between_chips(): return lax.ppermute(values, 'rad', route)]
    unnamed x38 -> x28, local copies, waits for them, and re-layouts: 4.83 us -> 0.07 us
    ppermute x6, starting transfers between devices: 9.01 us -> 7.11 us  [across_slabs(): lax.ppermute(values, 'az', [(slab, slab ^ distance) for slab in range(SLA...]
    ppermute x6, waiting for transfers between devices: 2.69 us -> 4.35 us  [across_slabs(): lax.ppermute(values, 'az', [(slab, slab ^ distance) for slab in range(SLA...]
  transfers between devices with their start and end apart: 22 -> 15, of which waited for: 8 -> 7; matrix products, arithmetic and copies ran while one was open for 1% -> 0% of each run, Pallas kernels for 42% -> 30%
where the time goes in v2:
time: 82 us; the launch traced here: 81.8 us
  Pallas kernels  37.3 us (45%)
  waiting for transfers between devices  25.4 us (31%)
  starting transfers between devices  18.7 us (23%)
    pallas_call x15, Pallas kernels, call(): pl.pallas_call(kernel, out_shape=outs, in_specs=specs, out_specs=[pl.Bloc...  37.3 us
    ppermute x6, waiting for transfers between devices, between_chips(): return lax.ppermute(values, 'rad', route)  19.9 us
    ppermute x6, starting transfers between devices, between_chips(): return lax.ppermute(values, 'rad', route)  10.8 us
    ppermute x6, starting transfers between devices, across_slabs(): lax.ppermute(values, 'az', [(slab, slab ^ distance) for slab in range(SLA...  7.11 us
    ppermute x6, waiting for transfers between devices, across_slabs(): lax.ppermute(values, 'az', [(slab, slab ^ distance) for slab in range(SLA...  4.35 us
  transfers between devices with their start and end apart: 15, of which 7 were waited for; matrix products, arithmetic and copies ran while one was open for 0% of the time, Pallas kernels for 30%

profile of v2, /device:TPU:0, one launch (start us, length us, event | category | flops | bytes accessed | tf_op | source)
XLA Modules:
  0.0 81.8 jit_solution(6782647427869206585)
XLA Ops:
  0.0 0.0 copy-start.11
  0.0 0.0 copy-start.10
  0.0 6.3 %forward.1 = (f32[4,1024,128]{2,1,0:T(8,128)}, f32[2,512,128]{2,1,0:T(8,128)}, f32[2,512,128]{2,1,0:T(8,128)}) custom-call(f32[4096,128]{1,0:T(8,128)} %bitcast.2, f32[1032,128]{1,0:T(8,128)} %constant.23.clone.tables_in, bf16[2304,256]{1,0:T(8,128)(2,1)} %constant.28.clone.stages_in, f32[32]{0:T(128)} %rest_0_.12, f32[32]{0:T(128)} %rest_1_.13, ...), custom_call_target="tpu_custom_call" | custom-call | bytes 29520000 | tf_op jit(solution)/shard_map/forward/pallas_call | solution.py:942
  6.3 0.6 collective-permute-start
  6.9 0.0 copy-done.8
  6.9 0.0 copy-done.5
  6.9 0.0 copy-done.9
  6.9 0.0 copy-done.12
  6.9 0.0 copy-done.11
  6.9 0.0 copy-done.10
  6.9 3.6 %ratios.1 = (f32[2,640,128]{2,1,0:T(8,128)S(1)}, f32[32,640,128]{2,1,0:T(8,128)S(1)}) custom-call(f32[640,128]{1,0:T(8,128)S(1)} %copy-done.5, f32[8,128]{1,0:T(8,128)S(1)} %copy-done.8, f32[32]{0:T(128)S(1)} %copy-done.10, f32[32]{0:T(128)S(1)} %copy-done.9, f32[32]{0:T(128)S(1)} %copy-done.11, f32[32]{0:T(128)S(1)} %copy-done.12), custom_call_target="tpu_custom_call" | custom-call | bytes 18450000 | tf_op jit(solution)/shard_map/ratios/pallas_call | solution.py:942
  10.6 0.0 copy-done.1
  10.6 0.0 copy-start.3
  10.6 1.7 %pair_ports.1.ports = f32[14,512,128]{2,1,0:T(8,128)S(1)} custom-call(f32[1024,128]{1,0:T(8,128)S(1)} %copy-done.1, f32[8,128]{1,0:T(8,128)S(1)} %copy-done.8, f32[2,640,128]{2,1,0:T(8,128)S(1)} %get-tuple-element.34.edges, f32[32]{0:T(128)S(1)} %copy-done.10, f32[32]{0:T(128)S(1)} %copy-done.9, f32[32]{0:T(128)S(1)} %copy-done.11, f32[32]{0:T(128)S(1)} %copy-done.12), custom_call_target="tpu_custom_call" | custom-call | bytes 7380000 | tf_op jit(solution)/shard_map/pair_ports/pallas_call | solution.py:942
  12.3 0.0 collective-permute-done.got
  12.3 0.0 copy-done.3
  12.4 0.0 copy-start.6
  12.4 0.0 copy-start.7
  12.4 0.0 copy-start.13
  12.4 0.0 copy-start
  12.4 0.0 copy-start.2
  12.4 0.3 merge.1
  12.7 4.5 %collective-permute-start.1 = (f32[512,128]{1,0:T(8,128)S(1)}, f32[512,128]{1,0:T(8,128)S(1)}, u32[]{:S(2)}, u32[]{:S(2)}) collective-permute-start(f32[512,128]{1,0:T(8,128)S(1)} %get-tuple-element.37), channel_id=1, source_target_pairs={{0,2},{1,3},{6,4},{7,5},{8,10},{9,11},{14,12},{15,13},{16,18},{17,... | collective-permute-start | bytes 786440 | tf_op jit(solution)/shard_map/ppermute | solution.py:963
  17.2 0.0 copy-done.6
  17.2 0.0 copy-done.7
  17.3 0.0 copy-done.13
  17.3 4.3 %response.1 = f32[2,32,128]{2,1,0:T(8,128)S(1)} custom-call(f32[2,128,128]{2,1,0:T(8,128)S(1)} %copy-done.7, f32[2,128,128]{2,1,0:T(8,128)S(1)} %copy-done.6, f32[4,128]{1,0:T(4,128)S(1)} %copy-done.13, f32[32]{0:T(128)S(1)} %copy-done.10, f32[32]{0:T(128)S(1)} %copy-done.9, f32[32]{0:T(128)S(1)} %copy-done.11, f32[32]{0:T(128)S(1)} %copy-done.12), custom_call_target="tpu_custom_call" | custom-call | bytes 18450000 | tf_op jit(solution)/shard_map/response/pallas_call | solution.py:942
  21.5 0.0 copy-done
  21.5 0.0 copy-done.2
  21.5 3.3 %ends.4.own = f32[4,32,128]{2,1,0:T(8,128)S(1)} custom-call(f32[2,32,128]{2,1,0:T(8,128)S(1)} %response.1, f32[4,1024,128]{2,1,0:T(8,128)S(1)} %copy-done, f32[1024,128]{1,0:T(8,128)S(1)} %copy-done.1, f32[1024,128]{1,0:T(8,128)S(1)} %copy-done.2, f32[8,128]{1,0:T(8,128)S(1)} %copy-done.8, f32[32]{0:T(128)S(1)} %copy-done.10, f32[32]{0:T(128)S(1)} %copy-done.9, ...), custom_call_target="tpu_custom_call" | custom-call | bytes 11070000 | tf_op jit(solution)/shard_map/ends/pallas_call | solution.py:942
  24.8 0.1 collective-permute-start.2
  25.0 1.2 %collective-permute-done.2.other = f32[4,32,128]{2,1,0:T(8,128)S(1)} collective-permute-done((f32[4,32,128]{2,1,0:T(8,128)S(1)}, f32[4,32,128]{2,1,0:T(8,128)S(1)}, u32[]{:S(2)}, u32[]{:S(2)}) %collective-permute-start.2) | collective-permute-done | bytes 65568 | tf_op jit(solution)/shard_map/ppermute | solution.py:958
  26.2 0.0 collective-permute-done.1.incoming
  26.2 0.2 inward.1.own
  26.4 0.7 collective-permute-start.9
  27.1 2.3 %collective-permute-start.5 = (f32[6,32,128]{2,1,0:T(8,128)S(1)}, f32[6,32,128]{2,1,0:T(8,128)S(1)}, u32[]{:S(2)}, u32[]{:S(2)}) collective-permute-start(f32[6,32,128]{2,1,0:T(8,128)S(1)} %join.1.rest_0_), channel_id=1, source_target_pairs={{0,6},{1,7},{2,0},{3,1},{4,2},{5,3},{6,4},{7,5},{8,14},{9,15},{10,... | collective-permute-start | bytes 294920 | tf_op jit(solution)/shard_map/ppermute | solution.py:963
  29.3 1.5 %collective-permute-start.4 = (f32[6,32,128]{2,1,0:T(8,128)S(1)}, f32[6,32,128]{2,1,0:T(8,128)S(1)}, u32[]{:S(2)}, u32[]{:S(2)}) collective-permute-start(f32[6,32,128]{2,1,0:T(8,128)S(1)} %join.1.rest_0_), channel_id=1, source_target_pairs={{0,4},{1,5},{2,6},{3,7},{4,0},{5,1},{6,2},{7,3},{8,12},{9,13},{10,... | collective-permute-start | bytes 294920 | tf_op jit(solution)/shard_map/ppermute | solution.py:963
  30.8 0.6 collective-permute-start.3
  31.4 1.1 %collective-permute-done.5.rest_3_ = f32[6,32,128]{2,1,0:T(8,128)S(1)} collective-permute-done((f32[6,32,128]{2,1,0:T(8,128)S(1)}, f32[6,32,128]{2,1,0:T(8,128)S(1)}, u32[]{:S(2)}, u32[]{:S(2)}) %collective-permute-start.5) | collective-permute-done | bytes 98336 | tf_op jit(solution)/shard_map/ppermute | solution.py:963
  32.5 11.5 %collective-permute-done.4.rest_2_ = f32[6,32,128]{2,1,0:T(8,128)S(1)} collective-permute-done((f32[6,32,128]{2,1,0:T(8,128)S(1)}, f32[6,32,128]{2,1,0:T(8,128)S(1)}, u32[]{:S(2)}, u32[]{:S(2)}) %collective-permute-start.4) | collective-permute-done | bytes 98336 | tf_op jit(solution)/shard_map/ppermute | solution.py:963
  44.0 0.0 collective-permute-done.3.rest_1_
  44.0 2.5 %collective-permute-start.8 = (f32[2,32,128]{2,1,0:T(8,128)S(1)}, f32[2,32,128]{2,1,0:T(8,128)S(1)}, u32[]{:S(2)}, u32[]{:S(2)}) collective-permute-start(f32[2,32,128]{2,1,0:T(8,128)S(1)} %total.1.rest_0_), channel_id=1, source_target_pairs={{0,24},{8,16},{16,8},{24,0},{1,25},{9,17},{17,9},{25,1},{2,26},{10... | collective-permute-start | bytes 98312 | tf_op jit(solution)/shard_map/ppermute | solution.py:972
  46.6 0.5 collective-permute-start.7
  47.1 0.5 collective-permute-start.6
  47.6 6.9 %capacity.1 = (f32[32,8,128]{2,1,0:T(8,128)S(1)}, f32[32,8,128]{2,1,0:T(8,128)S(1)}, f32[32,8,128]{2,1,0:T(8,128)S(1)}) custom-call(f32[32]{0:T(128)S(1)} %copy-done.9, f32[6,32,128]{2,1,0:T(8,128)S(1)} %join.1.rest_0_, f32[6,32,128]{2,1,0:T(8,128)S(1)} %collective-permute-done.3.rest_1_, f32[6,32,128]{2,1,0:T(8,128)S(1)} %collective-permute-done.4.rest_2_, ...), custom_call_target="tpu_custom_call" | custom-call | bytes 22140000 | tf_op jit(solution)/shard_map/capacity/pallas_call | solution.py:942
  54.5 0.0 collective-permute-done.8.rest_3_
  54.5 0.0 collective-permute-done.7.rest_2_
  54.5 0.0 collective-permute-done.6.rest_1_
  54.5 0.0 collective-permute-done.9.other
  54.5 0.2 middle.1
  54.7 1.3 %collective-permute-start.10 = (f32[512,128]{1,0:T(8,128)S(1)}, f32[512,128]{1,0:T(8,128)S(1)}, u32[]{:S(2)}, u32[]{:S(2)}) collective-permute-start(f32[512,128]{1,0:T(8,128)S(1)} %get-tuple-element.46), channel_id=1, source_target_pairs={{2,0},{3,1},{4,6},{5,7},{10,8},{11,9},{12,14},{13,15},{18,16},{19,... | collective-permute-start | bytes 786440 | tf_op jit(solution)/shard_map/ppermute | solution.py:963
  56.0 7.2 %collective-permute-done.10.near_two = f32[512,128]{1,0:T(8,128)S(1)} collective-permute-done((f32[512,128]{1,0:T(8,128)S(1)}, f32[512,128]{1,0:T(8,128)S(1)}, u32[]{:S(2)}, u32[]{:S(2)}) %collective-permute-start.10) | collective-permute-done | bytes 262176 | tf_op jit(solution)/shard_map/ppermute | solution.py:963
  63.3 0.4 parts.1
  63.7 0.1 collective-permute-start.11
  63.8 1.4 %slabs.1 = (f32[2,32,128]{2,1,0:T(8,128)S(1)}, f32[2,32,128]{2,1,0:T(8,128)S(1)}, f32[2,32,128]{2,1,0:T(8,128)S(1)}, f32[2,32,128]{2,1,0:T(8,128)S(1)}) custom-call(f32[32]{0:T(128)S(1)} %copy-done.9, f32[32,8,128]{2,1,0:T(8,128)S(1)} %get-tuple-element.42.minus_matrix, f32[32,8,128]{2,1,0:T(8,128)S(1)} %get-tuple-element.49.alternate_matrix, ...), custom_call_target="tpu_custom_call" | custom-call | bytes 7380000 | tf_op jit(solution)/shard_map/slabs/pallas_call | solution.py:942
  65.2 1.6 %collective-permute-start.12 = (f32[2,32,128]{2,1,0:T(8,128)S(1)}, f32[2,32,128]{2,1,0:T(8,128)S(1)}, u32[]{:S(2)}, u32[]{:S(2)}) collective-permute-start(f32[2,32,128]{2,1,0:T(8,128)S(1)} %get-tuple-element.52), channel_id=1, source_target_pairs={{0,8},{8,0},{16,24},{24,16},{1,9},{9,1},{17,25},{25,17},{2,10},{10... | collective-permute-start | bytes 98312 | tf_op jit(solution)/shard_map/ppermute | solution.py:972
  66.7 1.5 %collective-permute-start.13 = (f32[2,32,128]{2,1,0:T(8,128)S(1)}, f32[2,32,128]{2,1,0:T(8,128)S(1)}, u32[]{:S(2)}, u32[]{:S(2)}) collective-permute-start(f32[2,32,128]{2,1,0:T(8,128)S(1)} %get-tuple-element.53), channel_id=1, source_target_pairs={{0,16},{8,24},{16,0},{24,8},{1,17},{9,25},{17,1},{25,9},{2,18},{10... | collective-permute-start | bytes 98312 | tf_op jit(solution)/shard_map/ppermute | solution.py:972
  68.2 0.5 collective-permute-start.14
  68.7 0.4 collective-permute-done.12.rest_5_
  69.1 1.5 %collective-permute-done.13.rest_6_ = f32[2,32,128]{2,1,0:T(8,128)S(1)} collective-permute-done((f32[2,32,128]{2,1,0:T(8,128)S(1)}, f32[2,32,128]{2,1,0:T(8,128)S(1)}, u32[]{:S(2)}, u32[]{:S(2)}) %collective-permute-start.13) | collective-permute-done | bytes 32800 | tf_op jit(solution)/shard_map/ppermute | solution.py:972
  70.6 2.4 %collective-permute-done.14.rest_7_ = f32[2,32,128]{2,1,0:T(8,128)S(1)} collective-permute-done((f32[2,32,128]{2,1,0:T(8,128)S(1)}, f32[2,32,128]{2,1,0:T(8,128)S(1)}, u32[]{:S(2)}, u32[]{:S(2)}) %collective-permute-start.14) | collective-permute-done | bytes 32800 | tf_op jit(solution)/shard_map/ppermute | solution.py:972
  73.1 3.0 %sides.1 = (f32[2,32,128]{2,1,0:T(8,128)S(1)}, f32[2,1024,128]{2,1,0:T(8,128)S(1)}) custom-call(f32[1024,128]{1,0:T(8,128)S(1)} %copy-done.1, f32[1024,128]{1,0:T(8,128)S(1)} %copy-done.2, f32[8,128]{1,0:T(8,128)S(1)} %copy-done.8, f32[32]{0:T(128)S(1)} %copy-done.10, f32[32]{0:T(128)S(1)} %copy-done.9, f32[32]{0:T(128)S(1)} %copy-done.11, ...), custom_call_target="tpu_custom_call" | custom-call | bytes 11070000 | tf_op jit(solution)/shard_map/sides/pallas_call | solution.py:942
  76.1 0.0 collective-permute-done.11.got
  76.1 5.8 %backward.1 = f32[4096,128]{1,0:T(8,128)} custom-call(f32[4,1024,128]{2,1,0:T(8,128)S(1)} %copy-done, f32[2,512,128]{2,1,0:T(8,128)S(1)} %get-tuple-element.47.own, f32[2,512,128]{2,1,0:T(8,128)S(1)} %collective-permute-done.11.got, f32[2,1024,128]{2,1,0:T(8,128)S(1)} %get-tuple-element.55.extra, f32[2,32,128]{2,1,0:T(8,128)S(1)} %get-tuple-element.56.sources, ...), custom_call_target="tpu_custom_call" | custom-call | bytes 25830000 | tf_op jit(solution)/shard_map/backward/pallas_call | solution.py:942
  (9 shorter events, 0.0 us)
Async XLA Ops:
  0.0 6.9 %copy-start.8 = (f32[8,128]{1,0:T(8,128)S(1)}, f32[8,128]{1,0:T(8,128)}, u32[]{:S(2)}) copy-start(f32[8,128]{1,0:T(8,128)} %constant.22.clone.mu) | copy-start | bytes 12292
  0.0 6.9 %copy-start.5 = (f32[640,128]{1,0:T(8,128)S(1)}, f32[640,128]{1,0:T(8,128)}, u32[]{:S(2)}) copy-start(f32[640,128]{1,0:T(8,128)} %constant.24.clone.lam) | copy-start | bytes 983044
  0.0 10.6 %copy-start.1 = (f32[1024,128]{1,0:T(8,128)S(1)}, f32[1024,128]{1,0:T(8,128)}, u32[]{:S(2)}) copy-start(f32[1024,128]{1,0:T(8,128)} %constant.20.clone.lam) | copy-start | bytes 1572868
  0.0 6.9 %copy-start.9 = (f32[32]{0:T(128)S(1)}, f32[32]{0:T(128)}, u32[]{:S(2)}) copy-start(f32[32]{0:T(128)} %rest_1_.13) | copy-start | bytes 388
  0.0 6.9 %copy-start.12 = (f32[32]{0:T(128)S(1)}, f32[32]{0:T(128)}, u32[]{:S(2)}) copy-start(f32[32]{0:T(128)} %rest_3_.13) | copy-start | bytes 388
  0.0 6.9 %copy-start.11 = (f32[32]{0:T(128)S(1)}, f32[32]{0:T(128)}, u32[]{:S(2)}) copy-start(f32[32]{0:T(128)} %rest_2_.13) | copy-start | bytes 388
  0.0 6.9 %copy-start.10 = (f32[32]{0:T(128)S(1)}, f32[32]{0:T(128)}, u32[]{:S(2)}) copy-start(f32[32]{0:T(128)} %rest_0_.12) | copy-start | bytes 388
  6.3 6.0 %collective-permute-start = (f32[2,512,128]{2,1,0:T(8,128)}, f32[2,512,128]{2,1,0:T(8,128)S(1)}, u32[]{:S(2)}, u32[]{:S(2)}) collective-permute-start(f32[2,512,128]{2,1,0:T(8,128)} %get-tuple-element.33), channel_id=1, source_target_pairs={{0,1},{1,0},{2,3},{3,2},{4,5},{5,4},{6,7},{7,6},{8,9},{9,8},{10,11... | collective-permute-start | bytes 1572872 | tf_op jit(solution)/shard_map/ppermute | solution.py:958
  10.6 1.8 %copy-start.3 = (f32[2,512,128]{2,1,0:T(8,128)S(1)}, f32[2,512,128]{2,1,0:T(8,128)}, u32[]{:S(2)}) copy-start(f32[2,512,128]{2,1,0:T(8,128)} %get-tuple-element.32.keep) | copy-start | bytes 1572868
  12.4 4.9 %copy-start.6 = (f32[2,128,128]{2,1,0:T(8,128)S(1)}, f32[2,128,128]{2,1,0:T(8,128)}, u32[]{:S(2)}) copy-start(f32[2,128,128]{2,1,0:T(8,128)} %constant.27.clone.weight) | copy-start | bytes 393220
  12.4 4.9 %copy-start.7 = (f32[2,128,128]{2,1,0:T(8,128)S(1)}, f32[2,128,128]{2,1,0:T(8,128)}, u32[]{:S(2)}) copy-start(f32[2,128,128]{2,1,0:T(8,128)} %constant.26.clone.lam) | copy-start | bytes 393220
  12.4 4.9 %copy-start.13 = (f32[4,128]{1,0:T(4,128)S(1)}, f32[4,128]{1,0:T(4,128)}, u32[]{:S(2)}) copy-start(f32[4,128]{1,0:T(4,128)} %constant.25.clone.mu) | copy-start | bytes 6148
  12.4 9.1 %copy-start = (f32[4,1024,128]{2,1,0:T(8,128)S(1)}, f32[4,1024,128]{2,1,0:T(8,128)}, u32[]{:S(2)}) copy-start(f32[4,1024,128]{2,1,0:T(8,128)} %get-tuple-element.39.spectrum) | copy-start | bytes 6291460
  12.4 9.1 %copy-start.2 = (f32[1024,128]{1,0:T(8,128)S(1)}, f32[1024,128]{1,0:T(8,128)}, u32[]{:S(2)}) copy-start(f32[1024,128]{1,0:T(8,128)} %constant.21.clone.ends) | copy-start | bytes 1572868
  12.7 13.5 %collective-permute-start.1 = (f32[512,128]{1,0:T(8,128)S(1)}, f32[512,128]{1,0:T(8,128)S(1)}, u32[]{:S(2)}, u32[]{:S(2)}) collective-permute-start(f32[512,128]{1,0:T(8,128)S(1)} %get-tuple-element.37), channel_id=1, source_target_pairs={{0,2},{1,3},{6,4},{7,5},{8,10},{9,11},{14,12},{15,13},{16,18},{17,... | collective-permute-start | bytes 786440 | tf_op jit(solution)/shard_map/ppermute | solution.py:963
  24.8 1.3 %collective-permute-start.2 = (f32[4,32,128]{2,1,0:T(8,128)S(1)}, f32[4,32,128]{2,1,0:T(8,128)S(1)}, u32[]{:S(2)}, u32[]{:S(2)}) collective-permute-start(f32[4,32,128]{2,1,0:T(8,128)S(1)} %ends.4.own), channel_id=1, source_target_pairs={{0,1},{1,0},{2,3},{3,2},{4,5},{5,4},{6,7},{7,6},{8,9},{9,8},{10,11... | collective-permute-start | bytes 196616 | tf_op jit(solution)/shard_map/ppermute | solution.py:958
  26.4 28.1 %collective-permute-start.9 = (f32[512,128]{1,0:T(8,128)S(1)}, f32[512,128]{1,0:T(8,128)S(1)}, u32[]{:S(2)}, u32[]{:S(2)}) collective-permute-start(f32[512,128]{1,0:T(8,128)S(1)} %inward.1.own), channel_id=1, source_target_pairs={{2,4},{3,5},{4,2},{5,3},{10,12},{11,13},{12,10},{13,11},{18,20},{1... | collective-permute-start | bytes 786440 | tf_op jit(solution)/shard_map/ppermute | solution.py:963
  27.1 5.5 %collective-permute-start.5 = (f32[6,32,128]{2,1,0:T(8,128)S(1)}, f32[6,32,128]{2,1,0:T(8,128)S(1)}, u32[]{:S(2)}, u32[]{:S(2)}) collective-permute-start(f32[6,32,128]{2,1,0:T(8,128)S(1)} %join.1.rest_0_), channel_id=1, source_target_pairs={{0,6},{1,7},{2,0},{3,1},{4,2},{5,3},{6,4},{7,5},{8,14},{9,15},{10,... | collective-permute-start | bytes 294920 | tf_op jit(solution)/shard_map/ppermute | solution.py:963
  29.3 14.7 %collective-permute-start.4 = (f32[6,32,128]{2,1,0:T(8,128)S(1)}, f32[6,32,128]{2,1,0:T(8,128)S(1)}, u32[]{:S(2)}, u32[]{:S(2)}) collective-permute-start(f32[6,32,128]{2,1,0:T(8,128)S(1)} %join.1.rest_0_), channel_id=1, source_target_pairs={{0,4},{1,5},{2,6},{3,7},{4,0},{5,1},{6,2},{7,3},{8,12},{9,13},{10,... | collective-permute-start | bytes 294920 | tf_op jit(solution)/shard_map/ppermute | solution.py:963
  30.8 13.2 %collective-permute-start.3 = (f32[6,32,128]{2,1,0:T(8,128)S(1)}, f32[6,32,128]{2,1,0:T(8,128)S(1)}, u32[]{:S(2)}, u32[]{:S(2)}) collective-permute-start(f32[6,32,128]{2,1,0:T(8,128)S(1)} %join.1.rest_0_), channel_id=1, source_target_pairs={{0,2},{1,3},{2,4},{3,5},{4,6},{5,7},{6,0},{7,1},{8,10},{9,11},{10,... | collective-permute-start | bytes 294920 | tf_op jit(solution)/shard_map/ppermute | solution.py:963
  44.0 10.4 %collective-permute-start.8 = (f32[2,32,128]{2,1,0:T(8,128)S(1)}, f32[2,32,128]{2,1,0:T(8,128)S(1)}, u32[]{:S(2)}, u32[]{:S(2)}) collective-permute-start(f32[2,32,128]{2,1,0:T(8,128)S(1)} %total.1.rest_0_), channel_id=1, source_target_pairs={{0,24},{8,16},{16,8},{24,0},{1,25},{9,17},{17,9},{25,1},{2,26},{10... | collective-permute-start | bytes 98312 | tf_op jit(solution)/shard_map/ppermute | solution.py:972
  46.6 7.9 %collective-permute-start.7 = (f32[2,32,128]{2,1,0:T(8,128)S(1)}, f32[2,32,128]{2,1,0:T(8,128)S(1)}, u32[]{:S(2)}, u32[]{:S(2)}) collective-permute-start(f32[2,32,128]{2,1,0:T(8,128)S(1)} %total.1.rest_0_), channel_id=1, source_target_pairs={{0,16},{8,24},{16,0},{24,8},{1,17},{9,25},{17,1},{25,9},{2,18},{10... | collective-permute-start | bytes 98312 | tf_op jit(solution)/shard_map/ppermute | solution.py:972
  47.1 7.4 %collective-permute-start.6 = (f32[2,32,128]{2,1,0:T(8,128)S(1)}, f32[2,32,128]{2,1,0:T(8,128)S(1)}, u32[]{:S(2)}, u32[]{:S(2)}) collective-permute-start(f32[2,32,128]{2,1,0:T(8,128)S(1)} %total.1.rest_0_), channel_id=1, source_target_pairs={{0,8},{8,0},{16,24},{24,16},{1,9},{9,1},{17,25},{25,17},{2,10},{10... | collective-permute-start | bytes 98312 | tf_op jit(solution)/shard_map/ppermute | solution.py:972
  54.7 8.5 %collective-permute-start.10 = (f32[512,128]{1,0:T(8,128)S(1)}, f32[512,128]{1,0:T(8,128)S(1)}, u32[]{:S(2)}, u32[]{:S(2)}) collective-permute-start(f32[512,128]{1,0:T(8,128)S(1)} %get-tuple-element.46), channel_id=1, source_target_pairs={{2,0},{3,1},{4,6},{5,7},{10,8},{11,9},{12,14},{13,15},{18,16},{19,... | collective-permute-start | bytes 786440 | tf_op jit(solution)/shard_map/ppermute | solution.py:963
  63.7 12.4 %collective-permute-start.11 = (f32[2,512,128]{2,1,0:T(8,128)S(1)}, f32[2,512,128]{2,1,0:T(8,128)S(1)}, u32[]{:S(2)}, u32[]{:S(2)}) collective-permute-start(f32[2,512,128]{2,1,0:T(8,128)S(1)} %get-tuple-element.48), channel_id=1, source_target_pairs={{0,1},{1,0},{2,3},{3,2},{4,5},{5,4},{6,7},{7,6},{8,9},{9,8},{10,11... | collective-permute-start | bytes 1572872 | tf_op jit(solution)/shard_map/ppermute | solution.py:958
  65.2 4.0 %collective-permute-start.12 = (f32[2,32,128]{2,1,0:T(8,128)S(1)}, f32[2,32,128]{2,1,0:T(8,128)S(1)}, u32[]{:S(2)}, u32[]{:S(2)}) collective-permute-start(f32[2,32,128]{2,1,0:T(8,128)S(1)} %get-tuple-element.52), channel_id=1, source_target_pairs={{0,8},{8,0},{16,24},{24,16},{1,9},{9,1},{17,25},{25,17},{2,10},{10... | collective-permute-start | bytes 98312 | tf_op jit(solution)/shard_map/ppermute | solution.py:972
  66.7 3.9 %collective-permute-start.13 = (f32[2,32,128]{2,1,0:T(8,128)S(1)}, f32[2,32,128]{2,1,0:T(8,128)S(1)}, u32[]{:S(2)}, u32[]{:S(2)}) collective-permute-start(f32[2,32,128]{2,1,0:T(8,128)S(1)} %get-tuple-element.53), channel_id=1, source_target_pairs={{0,16},{8,24},{16,0},{24,8},{1,17},{9,25},{17,1},{25,9},{2,18},{10... | collective-permute-start | bytes 98312 | tf_op jit(solution)/shard_map/ppermute | solution.py:972
  68.2 4.8 %collective-permute-start.14 = (f32[2,32,128]{2,1,0:T(8,128)S(1)}, f32[2,32,128]{2,1,0:T(8,128)S(1)}, u32[]{:S(2)}, u32[]{:S(2)}) collective-permute-start(f32[2,32,128]{2,1,0:T(8,128)S(1)} %get-tuple-element.54), channel_id=1, source_target_pairs={{0,24},{8,16},{16,8},{24,0},{1,25},{9,17},{17,9},{25,1},{2,26},{10... | collective-permute-start | bytes 98312 | tf_op jit(solution)/shard_map/ppermute | solution.py:972
  73.1 3.0 %copy-start.4 = (bf16[2304,256]{1,0:T(8,128)(2,1)S(1)}, bf16[2304,256]{1,0:T(8,128)(2,1)}, u32[]{:S(2)}) copy-start(bf16[2304,256]{1,0:T(8,128)(2,1)} %constant.29.clone.stages) | copy-start | bytes 3538948

commit v3 on v2

--- a/solution.py
+++ b/solution.py
@@ -206,10 +206,17 @@
 
 def forward_kernel(total, source_in, tables_in, stages_in, *rest):
     scalars_in = rest[:4]
-    spectrum, keep, send = rest[4:7]
-    source, tables, stages, s0, s1, s2, s3, wide_rows, high, low, sems = rest[7:]
+    spectrum_out, keep, send = rest[4:7]
+    source, tables, stages, s0, s1, s2, s3, wide_rows, high, low, spectrum, sems = rest[7:]
     scalars = (s0, s1, s2, s3)
-    pairs = [(source_in, source), (stages_in, stages), (tables_in, tables)]
+    length = source.shape[0] * source.shape[1] // CELLS
+    quarter = length // 8
+    eighth = quarter * CELLS
+    pairs = []
+    for part in range(2):
+        rows = pl.ds(part * eighth // 2, eighth // 2)
+        pairs.append((source_in.at[:, rows, :], source.at[:, rows, :]))
+    pairs += [(stages_in, stages), (tables_in, tables)]
     pairs += list(zip(scalars_in, scalars))
     copies = [
         pltpu.make_async_copy(origin, target, sems.at[place])
@@ -218,24 +225,22 @@
     for copy in copies:
         copy.start()
     radial = Radial(*scalars, total)
-    length = source.shape[0] // CELLS
-    quarter = length // 8
     core = lax.rem(lax.axis_index("rad"), 2)
     first = lax.axis_index("rad") * CELLS
     chunk = 16
-    copies[0].wait()
-    for cell in range(CELLS):
-        for start in range(0, quarter, chunk):
+    for start in range(0, quarter, chunk):
+        if start * 2 % quarter == 0:
+            copies[start * 2 // quarter].wait()
+        for cell in range(CELLS):
             x = [
-                source[pl.ds((n * quarter + start) * CELLS + cell, chunk, stride=CELLS), :]
-                for n in range(8)
+                source[n, pl.ds(start * CELLS + cell, chunk, stride=CELLS), :] for n in range(8)
             ]
             for place, part in enumerate(spread_parts(x)):
                 one, two = split(part)
                 row = cell * length + place * quarter + start
                 wide_rows[row : row + chunk, :LANES] = one
                 wide_rows[row : row + chunk, LANES:] = two
-    copies[1].wait()
+    copies[2].wait()
     wide = stages[8 * 2 * quarter : 8 * 2 * quarter + 2 * LANES, :]
     for cell in range(CELLS):
         for slot in range(4):
@@ -245,6 +250,7 @@
             columns = slice(cell * LANES, (cell + 1) * LANES)
             high[slot, :, columns] = one
             low[slot, :, columns] = two
+    leaving = []
     for slot in range(4):
         upper = stages[slot * 2 * quarter : (slot + 1) * 2 * quarter, :]
         lower = stages[(4 + slot) * 2 * quarter : (5 + slot) * 2 * quarter, :]
@@ -253,7 +259,14 @@
             spectrum[cell, slot * 2 * quarter : (slot + 1) * 2 * quarter, :] = result[
                 :, cell * LANES : (cell + 1) * LANES
             ]
-    for copy in copies[2:]:
+        rows = pl.ds(slot * 2 * quarter, 2 * quarter)
+        leaving.append(
+            pltpu.make_async_copy(
+                spectrum.at[:, rows, :], spectrum_out.at[:, rows, :], sems.at[8 + slot]
+            )
+        )
+        leaving[-1].start()
+    for copy in copies[3:]:
         copy.wait()
     chunk = 64
     half = length // 2
@@ -273,13 +286,15 @@
         return 0
 
     lax.fori_loop(0, half // chunk, step, 0)
+    for copy in leaving:
+        copy.wait()
 
 
 def shared_row(slot, kind, quarter):
     return pl.multiple_of(jnp.where(slot == 0, kind, slot + 1) * quarter, quarter)
 
 
-def pair_ports_kernel(total, lam, mu, edges, *rest):
+def pair_ports_kernel(total, lam, mu, *rest):
     radial = Radial(*rest[:4], total)
     (out,) = rest[4:]
     half = out.shape[1]
@@ -295,24 +310,39 @@
     def step(index, _):
         rows = pl.ds(pl.multiple_of(index * chunk, chunk), chunk)
         spot = pl.ds(pl.multiple_of(core * half + index * chunk, chunk), chunk)
-        block = index * chunk // quarter
-        start = shared_row(core * 2 + block // 2, lax.rem(block, 2), quarter)
-        spot5 = pl.ds(pl.multiple_of(start + lax.rem(index * chunk, quarter), chunk), chunk)
         (b1, g1, b2, g2), (c1, h1, c2, h2), mid, (w1, w2, w3, w4) = chip_ports(
             radial, first, lam[spot, :], level
         )
-        for place, value in enumerate((g1, b2, g2, c1, h1, c2, mid)):
-            out[place, rows, :] = value
-        left, right = edges[0, spot5, :], edges[1, spot5, :]
-        far, near = jnp.where(left_side, left, right), jnp.where(left_side, right, left)
         rff, rnn = jnp.where(left_side, w1, w4), jnp.where(left_side, w4, w1)
         rfn, rnf = jnp.where(left_side, w2, w3), jnp.where(left_side, w3, w2)
+        for place, value in enumerate((g1, b2, g2, c1, h1, c2, mid, rff, rfn, rnf, rnn)):
+            out[place, rows, :] = value
+        return 0
+
+    lax.fori_loop(0, half // chunk, step, 0)
+
+
+def chain_links_kernel(chips, ports, edges, out):
+    half = out.shape[1]
+    quarter = half // 4
+    core = lax.rem(lax.axis_index("rad"), 2)
+    left_side = lax.axis_index("rad") // 2 < chips // 2
+    chunk = min(64, quarter)
+
+    def step(index, _):
+        rows = pl.ds(pl.multiple_of(index * chunk, chunk), chunk)
+        block = index * chunk // quarter
+        start = shared_row(core * 2 + block // 2, lax.rem(block, 2), quarter)
+        spot = pl.ds(pl.multiple_of(start + lax.rem(index * chunk, quarter), chunk), chunk)
+        rff, rfn, rnf, rnn = (ports[7 + place, rows, :] for place in range(4))
+        left, right = edges[0, spot, :], edges[1, spot, :]
+        far, near = jnp.where(left_side, left, right), jnp.where(left_side, right, left)
         pivot = inverse(1.0 - rff * far)
         onward = rnn + rnf * far * rfn * pivot
         for place, value in enumerate(
             (rff, pivot, rfn * pivot, rnf, far, near, inverse(1.0 - near * onward))
         ):
-            out[7 + place, rows, :] = value
+            out[place, rows, :] = value
         return 0
 
     lax.fori_loop(0, half // chunk, step, 0)
@@ -343,13 +373,13 @@
     lax.fori_loop(0, half // chunk, step, 0)
 
 
-def inward_kernel(whole, incoming, ports, out):
+def inward_kernel(whole, incoming, links, out):
     half = out.shape[0]
     chunk = 32
 
     def step(index, _):
         rows = pl.ds(pl.multiple_of(index * chunk, chunk), chunk)
-        rff, pivot, _rfn, rnf, far = (ports[7 + place, rows, :] for place in range(5))
+        rff, pivot, _rfn, rnf, far = (links[place, rows, :] for place in range(5))
         value = incoming[rows, :]
         origin = (whole[0, rows, :] + rff * value) * pivot
         out[rows, :] = whole[1, rows, :] + rnf * (value + far * origin)
@@ -358,7 +388,7 @@
     lax.fori_loop(0, half // chunk, step, 0)
 
 
-def middle_kernel(chips, whole, incoming, own, other, ports, near_out, far_out):
+def middle_kernel(chips, whole, incoming, own, other, links, near_out, far_out):
     half = far_out.shape[0]
     chip = lax.axis_index("rad") // 2
     inner = (chip == chips // 2) | (chip == chips // 2 - 1)
@@ -367,7 +397,7 @@
     def step(index, _):
         rows = pl.ds(pl.multiple_of(index * chunk, chunk), chunk)
         rff, pivot, hold, _rnf, _far, near, close = (
-            ports[7 + place, rows, :] for place in range(7)
+            links[place, rows, :] for place in range(7)
         )
         value = (other[rows, :] + near * own[rows, :]) * close
         value = jnp.where(inner, value, 0.0)
@@ -379,13 +409,13 @@
     lax.fori_loop(0, half // chunk, step, 0)
 
 
-def outward_kernel(whole, incoming, near_in, ports, far_out):
+def outward_kernel(whole, incoming, near_in, links, far_out):
     half = far_out.shape[0]
     chunk = 32
 
     def step(index, _):
         rows = pl.ds(pl.multiple_of(index * chunk, chunk), chunk)
-        rff, pivot, hold = (ports[7 + place, rows, :] for place in range(3))
+        rff, pivot, hold = (links[place, rows, :] for place in range(3))
         origin = (whole[0, rows, :] + rff * incoming[rows, :]) * pivot
         far_out[rows, :] = origin + hold * near_in[rows, :]
         return 0
@@ -393,7 +423,7 @@
     lax.fori_loop(0, half // chunk, step, 0)
 
 
-def parts_kernel(chips, keep, got, ports, whole, incoming, near_one, near_two, own, send):
+def parts_kernel(chips, keep, got, ports, links, whole, incoming, near_one, near_two, own, send):
     half = keep.shape[1]
     core = lax.rem(lax.axis_index("rad"), 2)
     left_side = lax.axis_index("rad") // 2 < chips // 2
@@ -402,7 +432,7 @@
     def step(index, _):
         rows = pl.ds(pl.multiple_of(index * chunk, chunk), chunk)
         _g1, b2, g2, c1, h1, _c2, mid = (ports[place, rows, :] for place in range(7))
-        rff, pivot, hold, _rnf, far = (ports[7 + place, rows, :] for place in range(5))
+        rff, pivot, hold, _rnf, far = (links[place, rows, :] for place in range(5))
         near = near_one[rows, :] + near_two[rows, :]
         value = incoming[rows, :]
         outer = value + far * ((whole[0, rows, :] + rff * value) * pivot + hold * near)
@@ -465,7 +495,7 @@
     first = lax.axis_index("rad") * CELLS
     opening = lax.axis_index("rad") // 2 * (2 * CELLS)
     level = mu[...][:1]
-    chunk = lam.shape[0] // 5
+    chunk = lam.shape[0] // (2 if kept else 5)
 
     def step(index, _):
         rows = pl.ds(pl.multiple_of(index * chunk, chunk), chunk)
@@ -477,7 +507,7 @@
         edges[1, rows, :] = jnp.where(opening + 2 * CELLS < total, right, 0.0)
         return 0
 
-    lax.fori_loop(0, 5, step, 0)
+    lax.fori_loop(0, lam.shape[0] // chunk, step, 0)
 
 
 def outside(view, first, total):
@@ -548,18 +578,21 @@
     out[2:4] = response[...]
 
 
-def join_kernel(own, other, out):
-    out[0:2] = own[0:2] + other[0:2]
-    out[2:4] = own[2:4]
-    out[4:6] = other[2:4]
-
-
-def total_kernel(*rest):
-    pieces, out = rest[:-1], rest[-1]
-    value = pieces[0][0:2]
-    for piece in pieces[1:]:
-        value = value + piece[0:2]
-    out[...] = value
+def join_kernel(axis, bit, common, own, other, out):
+    high = lax.rem(lax.div(lax.axis_index(axis), 1 << bit), 2)
+    count = own.shape[0] - common
+    if common:
+        out[0:common] = own[0:common] + other[0:common]
+    out[pl.ds(common + high * count, count)] = own[common:]
+    out[pl.ds(common + (1 - high) * count, count)] = other[common:]
+
+
+def halve_kernel(axis, bit, own, other, keep, send):
+    high = lax.rem(lax.div(lax.axis_index(axis), 1 << bit), 2)
+    count = keep.shape[0]
+    keep[...] = own[pl.ds(high * count, count)] + other[pl.ds(high * count, count)]
+    there = pl.ds((1 - high) * count, count)
+    send[...] = own[there] + other[there]
 
 
 def response_kernel(total, lam, weight, mu, *rest):
@@ -568,25 +601,24 @@
     first = lax.axis_index("rad") * CELLS
     level = mu[pl.ds(lax.axis_index("az"), 1), :]
     group = LANES // SLABS
-    chunk = lam.shape[1]
+    chunk = lam.shape[0] // 2
     sums[...] = jnp.zeros_like(sums)
-
-    def step(index, _):
-        kind = index
-        values = lam[kind]
-        left, right = ratios(radial, first, values, level, store, store)
-        source = weight[kind]
+    lefts, rights = ratios(radial, first, lam[...], level, store, store)
+
+    for kind in range(2):
+        rows = slice(kind * chunk, (kind + 1) * chunk)
+        source = weight[rows, :]
         zero = jnp.zeros_like(source)
         openings, closings = [], []
         for place in range(CELLS):
             answer = solve_block(
                 radial,
                 first,
-                values,
+                lam[rows, :],
                 level,
                 [source if cell == place else zero for cell in range(CELLS)],
-                radial.previous(first) * left,
-                radial.coupling(first + CELLS - 1) * right,
+                radial.previous(first) * lefts[rows],
+                radial.coupling(first + CELLS - 1) * rights[rows],
             )
             for cell in range(CELLS):
                 sums[kind, place, first + cell] += fold_rows(answer[cell])
@@ -594,7 +626,7 @@
             closings.append(answer[-1])
 
         def outward(cell, factor, edges):
-            factor = store[cell] * factor
+            factor = store[cell, rows, :] * factor
             for place in range(CELLS):
                 sums[kind, place, cell] += fold_rows(factor * edges[place])
             return factor
@@ -606,9 +638,7 @@
             lambda move, factor: outward(first + CELLS + move, factor, closings),
             one,
         )
-        return 0
-
-    lax.fori_loop(0, 2, step, 0)
+
     lane = lax.broadcasted_iota(jnp.int32, (1, LANES), 1) // group
 
     def close(cell, _):
@@ -718,47 +748,48 @@
     cells = lax.broadcasted_iota(jnp.int32, (width, LANES), 0) + lane_groups() * width
 
     def column(cell, value):
-        return jnp.where(cells == cell, top / azimuth[cell], value)
-
-    return lax.fori_loop(0, total, column, jnp.zeros((width, LANES), F32), unroll=8)
-
-
-def capacity_kernel(total, chips, azimuth, *rest):
-    pieces = rest[:chips]
-    minus_out, alternate_out, pair_out = rest[chips:]
-    chip = lax.axis_index("rad") // 2
-    core = lax.rem(lax.axis_index("rad"), 2)
+        return jnp.where(cells == cell, azimuth[cell], value)
+
+    return top * inverse(lax.fori_loop(0, total, column, jnp.ones((width, LANES), F32), unroll=8))
+
+
+def capacity_kernel(total, azimuth, responses, *outs):
+    minus_out, alternate_out, pair_out = outs
+    chips = total // (2 * CELLS)
     width = total // SLABS
     shift = LANES // SLABS
     lane = lane_groups()
     cells = lax.broadcasted_iota(jnp.int32, (width, LANES), 0) + lane * width
-    for distance, piece in enumerate(pieces):
-        origin = lax.rem(chip + chips - distance, chips)
-        for side in range(2):
-            block = 2 * origin + lax.rem(core + side, 2)
-            for kind in range(2):
-                parts = [
-                    piece[2 + 2 * side + kind, group * width : (group + 1) * width, :]
-                    for group in range(SLABS)
-                ]
-                for place in range(CELLS):
-                    row = jnp.zeros((width, LANES), F32)
-                    for group, part in enumerate(parts):
-                        turn = (group - place) % SLABS
-                        part = pltpu.roll(part, turn * shift, 1) if turn else part
-                        row = jnp.where(lane == group, part, row)
-                    cell = block * CELLS + place
-                    own = jnp.where(cells == cell, 0.5 / azimuth[cell], 0.0)
-                    if kind == 0:
-                        alternate_out[cell] = own + row
-                        pair_out[cell] = own + row
-                    else:
-                        minus_out[cell] = own - row
+    half = per_cell(total, azimuth, 0.5)
+    for block in range(2 * chips):
+        start = 2 + 2 * (block % 2 * chips + block // 2)
+        for kind in range(2):
+            parts = [
+                responses[start + kind, group * width : (group + 1) * width, :]
+                for group in range(SLABS)
+            ]
+            for place in range(CELLS):
+                row = jnp.zeros((width, LANES), F32)
+                for group, part in enumerate(parts):
+                    turn = (group - place) % SLABS
+                    part = pltpu.roll(part, turn * shift, 1) if turn else part
+                    row = jnp.where(lane == group, part, row)
+                cell = block * CELLS + place
+                own = jnp.where(cells == cell, half, 0.0)
+                if kind == 0:
+                    alternate_out[cell] = own + row
+                    pair_out[cell] = own + row
+                else:
+                    minus_out[cell] = own - row
     invert([minus_out, alternate_out], total)
+
+
+def pair_kernel(total, azimuth, minus_matrix, plus_matrix, pair_out):
     scale = per_cell(total, azimuth, 0.25)
 
     def add(cell, _):
-        pair_out[cell] = pair_out[cell] + minus_out[cell] * scale * (1.0 / azimuth[cell])
+        own = inverse(jnp.full((1, LANES), azimuth[cell], F32))
+        pair_out[cell] = plus_matrix[cell] + minus_matrix[cell] * (scale * own)
         return 0
 
     lax.fori_loop(0, total, add, 0, unroll=8)
@@ -778,17 +809,14 @@
 
 
 def slabs_kernel(total, azimuth, minus_matrix, alternate_matrix, pair_matrix, *rest):
-    pieces, outs = rest[:SLABS], rest[SLABS : 2 * SLABS]
-    values, results, store = rest[2 * SLABS :]
+    values, keep, send, results, store = rest
     slab = lax.axis_index("az")
     width = total // SLABS
     shift = LANES // SLABS
     lane = lane_groups()
-    for distance, piece in enumerate(pieces):
-        values[slab ^ distance] = piece[...]
 
     def channels(kind):
-        u = [values[place, kind] for place in range(SLABS)]
+        u = [values[2 * place + kind] for place in range(SLABS)]
         mixed = (u[0] - u[2], u[3] - u[1], (u[0] + u[2]) - (u[1] + u[3]))
         return [to_all_groups(value, slab) for value in mixed]
 
@@ -820,21 +848,22 @@
             for group in range(SLABS):
                 turn = lax.rem(slab - group + SLABS, SLABS) * shift
                 rows = slice(group * width, (group + 1) * width)
-                results[place, kind, rows, :] = jnp.where(
+                results[2 * place + kind, rows, :] = jnp.where(
                     lane == slab, pltpu.roll(value, turn, 1), 0.0
                 )
-    for distance, out in enumerate(outs):
-        out[...] = results[slab ^ distance]
+    high = lax.div(slab, SLABS // 2)
+    keep[...] = results[pl.ds(high * SLABS, SLABS)]
+    send[...] = results[pl.ds((1 - high) * SLABS, SLABS)]
 
 
 def sides_kernel(total, kept, lam, ends, mu, *rest):
     radial = Radial(*rest[:4], total)
-    pieces = rest[4 : 4 + SLABS]
+    own_part, other_part = rest[4:6]
     if kept:
-        store, sources, out = rest[4 + SLABS :]
+        store, sources, out = rest[6:]
     else:
-        sources, out, store = rest[4 + SLABS :]
-    sources[...] = (pieces[0][...] + pieces[1][...]) + (pieces[2][...] + pieces[3][...])
+        sources, out, store = rest[6:]
+    sources[...] = own_part[...] + other_part[...]
     first = lax.axis_index("rad") * CELLS
     level = mu[...][:1]
     chunk = lam.shape[0] // 8
@@ -875,7 +904,7 @@
 
 def backward_kernel(total, spectrum, own, got, extra, sources, stages, lam, ends, mu, *rest):
     radial = Radial(*rest[:4], total)
-    out, high, low, middle, wide_rows = rest[4:]
+    out, high, low, middle, wide_rows, field, sems = rest[4:]
     length = spectrum.shape[1]
     quarter = length // 8
     core = lax.rem(lax.axis_index("rad"), 2)
@@ -923,17 +952,26 @@
             ]
             for place, value in enumerate(gather_parts(y)):
                 one, two = split(value)
-                row = place * quarter + start
+                row = cell * length + place * quarter + start
                 wide_rows[row : row + chunk, :LANES] = one
                 wide_rows[row : row + chunk, LANES:] = two
-        for start in range(0, length, 2 * quarter):
-            both = dot(wide_rows[start : start + 2 * quarter, :], wide)
-            out[pl.ds(start * CELLS + cell, 2 * quarter, stride=CELLS), :] = (
+    copies = []
+    for part in range(4):
+        start = part * 2 * quarter
+        for cell in range(CELLS):
+            row = cell * length + start
+            both = dot(wide_rows[row : row + 2 * quarter, :], wide)
+            field[pl.ds(start * CELLS + cell, 2 * quarter, stride=CELLS), :] = (
                 both[:, :LANES] + both[:, LANES:]
             )
-
-
-def call(kernel, out_shapes, args, scalars=(), scratch=(), cost=1, room=20, held=(), name=None):
+        rows = pl.ds(start * CELLS, 2 * quarter * CELLS)
+        copies.append(pltpu.make_async_copy(field.at[rows], out.at[rows], sems.at[part]))
+        copies[-1].start()
+    for copy in copies:
+        copy.wait()
+
+
+def call(kernel, out_shapes, args, scalars=(), scratch=(), cost=1, room=20, held=(), out_held=(), name=None):
     specs = []
     for place in range(len(args)):
         space = pltpu.SMEM if place in scalars else pltpu.HBM if place in held else pltpu.VMEM
@@ -943,7 +981,10 @@
         kernel,
         out_shape=outs,
         in_specs=specs,
-        out_specs=[pl.BlockSpec(memory_space=pltpu.VMEM)] * len(outs),
+        out_specs=[
+            pl.BlockSpec(memory_space=pltpu.HBM if place in out_held else pltpu.VMEM)
+            for place in range(len(outs))
+        ],
         scratch_shapes=list(scratch),
         compiler_params=pltpu.CompilerParams(vmem_limit_bytes=room * 2**20),
         cost_estimate=pl.CostEstimate(
@@ -963,13 +1004,9 @@
     return lax.ppermute(values, "rad", route)
 
 
-def along_chips(values, distance):
-    chips = lax.axis_size("rad") // 2
-    return between_chips(values, [(chip, (chip + distance) % chips) for chip in range(chips)])
-
-
-def across_slabs(values, distance):
-    return lax.ppermute(values, "az", [(slab, slab ^ distance) for slab in range(SLABS)])
+def hop(axis, values, bit):
+    count = lax.axis_size(axis)
+    return lax.ppermute(values, axis, [(index, index ^ (1 << bit)) for index in range(count)])
 
 
 def on_device(source, helmholtz, azimuth, vertical, radial):
@@ -1008,8 +1045,8 @@
     )
 
     def packed(column):
-        table = np.stack([column[parity > 0], column[parity < 0]]).reshape(2, quarter, SLABS)
-        return jnp.asarray(np.repeat(table, group, axis=2).astype(np.float32))
+        table = np.stack([column[parity > 0], column[parity < 0]]).reshape(2 * quarter, SLABS)
+        return jnp.asarray(np.repeat(table, group, axis=1).astype(np.float32))
 
     lam_groups = packed(eigen)
     weight_groups = packed(2.0 * end_weights**2)
@@ -1022,44 +1059,31 @@
     spectrum, keep, send = call(
         functools.partial(forward_kernel, total),
         [(CELLS, length, LANES), (2, half, LANES), (2, half, LANES)],
-        (source.reshape(length * CELLS, LANES), tables, stages) + scalars4,
+        (source.reshape(8, quarter * CELLS, LANES), tables, stages)
+        + scalars4,
         (),
         [
-            pltpu.VMEM((length * CELLS, LANES), F32),
+            pltpu.VMEM((8, quarter * CELLS, LANES), F32),
             pltpu.VMEM(tables.shape, F32),
             pltpu.VMEM(stages.shape, BF16),
         ]
         + [pltpu.SMEM((total,), F32)] * 4
         + [pltpu.VMEM((length * CELLS, 2 * LANES), BF16)]
         + [pltpu.VMEM((4,) + wide_shape, BF16)] * 2
-        + [pltpu.SemaphoreType.DMA((7,))],
+        + [pltpu.VMEM((CELLS, length, LANES), F32), pltpu.SemaphoreType.DMA((12,))],
         cost=8,
         held=tuple(range(7)),
+        out_held=(0,),
         room=57,
         name="forward",
     )
     got = other_core(send)
-
-    store_shape = (total, (5 if kept else 1) * quarter, LANES)
-    edge_shape = (2, 5 * quarter, LANES)
-    ratios_out = call(
-        functools.partial(ratios_kernel, total, kept),
-        [edge_shape] + ([store_shape] if kept else []),
-        (lam_shared, mu) + scalars4,
-        smem(2),
-        [] if kept else [pltpu.VMEM(store_shape, F32)],
-        cost=5,
-        room=room,
-        name="ratios",
-    )
-    edges, store = ratios_out[0], tuple(ratios_out[1:])
-    scratch_store = [] if kept else [pltpu.VMEM(store_shape, F32)]
-
+    azimuth_ports, _ = lax.optimization_barrier((azimuth, send))
     (ports,) = call(
         functools.partial(pair_ports_kernel, total),
-        [(14, half, LANES)],
-        (lam, mu, edges) + scalars4,
-        smem(3),
+        [(11, half, LANES)],
+        (lam, mu, helmholtz, azimuth_ports, vertical, radial),
+        smem(2),
         cost=2,
         room=room,
         name="pair_ports",
@@ -1073,15 +1097,37 @@
         room=room,
         name="merge",
     )
-    out, spectrum_late, helmholtz_late = lax.optimization_barrier((out, spectrum, helmholtz))
-    scalars_late = (helmholtz_late,) + scalars4[1:]
+
+    out, azimuth_ratios = lax.optimization_barrier((out, azimuth))
+    store_shape = (total, (5 if kept else 1) * quarter, LANES)
+    edge_shape = (2, 5 * quarter, LANES)
+    ratios_out = call(
+        functools.partial(ratios_kernel, total, kept),
+        [edge_shape] + ([store_shape] if kept else []),
+        (lam_shared, mu, helmholtz, azimuth_ratios, vertical, radial),
+        smem(2),
+        [] if kept else [pltpu.VMEM(store_shape, F32)],
+        cost=5,
+        room=room,
+        name="ratios",
+    )
+    edges, store = ratios_out[0], tuple(ratios_out[1:])
+    scratch_store = [] if kept else [pltpu.VMEM(store_shape, F32)]
+    (links,) = call(
+        functools.partial(chain_links_kernel, chips),
+        [(7, half, LANES)],
+        (ports, edges),
+        cost=0.5,
+        room=room,
+        name="links",
+    )
     (response,) = call(
         functools.partial(response_kernel, total),
         [(2, total, LANES)],
-        (lam_groups, weight_groups, mu_groups) + scalars_late,
+        (lam_groups, weight_groups, mu_groups, helmholtz, azimuth_ratios, vertical, radial),
         smem(3),
         [
-            pltpu.VMEM((total, quarter, LANES), F32),
+            pltpu.VMEM((total, 2 * quarter, LANES), F32),
             pltpu.VMEM((2, CELLS, total, 8, LANES), F32),
             pltpu.VMEM((2, CELLS, total, LANES), F32),
         ],
@@ -1092,7 +1138,7 @@
     (packed_ends,) = call(
         functools.partial(ends_kernel, total, kept),
         [(4, total, LANES)],
-        (response, spectrum_late, lam, ends, mu) + scalars4 + store,
+        (response, spectrum, lam, ends, mu) + scalars4 + store,
         smem(5),
         [pltpu.VMEM((2, total, 8, LANES), F32)] + scratch_store,
         cost=3,
@@ -1100,47 +1146,72 @@
         name="ends",
     )
     incoming = None
-    (joint,) = call(
-        join_kernel,
-        [(6, total, LANES)],
-        (packed_ends, other_core(packed_ends)),
-        cost=0.3,
-        room=room,
-        name="join",
-    )
-    whole_late, joint = lax.optimization_barrier((whole, joint))
+    whole_late, _ = lax.optimization_barrier((whole, packed_ends))
     for edge in range(chips // 2 - 1):
         moved = between_chips(out, [(edge, edge + 1), (chips - 1 - edge, chips - 2 - edge)])
         incoming = moved if incoming is None else incoming + moved
         (out,) = call(
             inward_kernel,
             [line],
-            (whole_late, incoming, ports),
+            (whole_late, incoming, links),
             cost=0.3,
             room=room,
             name="inward",
         )
-    joints = [joint] + [along_chips(joint, d) for d in range(1, chips)]
-    (slab_ends,) = call(
-        total_kernel, [(2, total, LANES)], tuple(joints), cost=0.3, room=room, name="total"
-    )
-    all_ends = [slab_ends] + [across_slabs(slab_ends, d) for d in range(1, SLABS)]
-    matrices3 = call(
-        functools.partial(capacity_kernel, total, chips),
-        [(total, total // SLABS, LANES)] * 3,
-        (azimuth, *joints),
+
+    def join(axis, bit, common, own, other):
+        shape = (2 * own.shape[0] - common, total, LANES)
+        (result,) = call(
+            functools.partial(join_kernel, axis, bit, common),
+            [shape],
+            (own, other),
+            cost=0.3,
+            room=room,
+            name="join",
+        )
+        return result
+
+    gathered = packed_ends
+    for bit in range(1, blocks.bit_length() - 1):
+        moved = hop("rad", gathered, bit)
+        gathered = join("rad", bit, 2, gathered, moved)
+    gathered = join("rad", 0, 2, gathered, hop("rad", gathered, 0))
+    matrix_shape = (total, total // SLABS, LANES)
+    minus_matrix, alternate_matrix, plus_matrix = call(
+        functools.partial(capacity_kernel, total),
+        [matrix_shape] * 3,
+        (azimuth, gathered),
         (0,),
-        cost=6,
+        cost=4,
         room=room,
         name="capacity",
     )
+    slab_ends = gathered[0:2]
+    moved = hop("az", slab_ends, 0)
+    slab_ends, _ = lax.optimization_barrier((slab_ends, minus_matrix))
+    slab_ends = join("az", 0, 0, slab_ends, moved)
+    middle_after = slab_ends
+    azimuth_pair, _ = lax.optimization_barrier((azimuth, slab_ends))
+    (pair_matrix,) = call(
+        functools.partial(pair_kernel, total),
+        [matrix_shape],
+        (azimuth_pair, minus_matrix, plus_matrix),
+        (0,),
+        cost=3,
+        room=room,
+        name="pair",
+    )
+    moved = hop("az", slab_ends, 1)
+    slab_ends, _ = lax.optimization_barrier((slab_ends, pair_matrix))
+    slab_ends = join("az", 1, 0, slab_ends, moved)
+
     low, high = chips // 2 - 1, chips // 2
     other = between_chips(out, [(low, high), (high, low)])
-    whole_last, _, _ = lax.optimization_barrier((whole, matrices3[0], tuple(all_ends)))
+    whole_last, _ = lax.optimization_barrier((whole, middle_after))
     near, far = call(
         functools.partial(middle_kernel, chips),
         [line, line],
-        (whole_last, incoming, out, other, ports),
+        (whole_last, incoming, out, other, links),
         cost=0.3,
         room=room,
         name="middle",
@@ -1153,35 +1224,45 @@
             (far,) = call(
                 outward_kernel,
                 [line],
-                (whole, incoming, passed, ports),
+                (whole, incoming, passed, links),
                 cost=0.3,
                 room=room,
                 name="outward",
             )
+    keep_sources, send_sources = call(
+        functools.partial(slabs_kernel, total),
+        [(SLABS, total, LANES)] * 2,
+        (azimuth, minus_matrix, alternate_matrix, pair_matrix, slab_ends),
+        (0,),
+        [pltpu.VMEM((2 * SLABS, total, LANES), F32), pltpu.VMEM((8, total, LANES), F32)],
+        cost=2,
+        room=room,
+        name="slabs",
+    )
+    moved = hop("az", send_sources, 1)
+    keep_sources, send_sources = call(
+        functools.partial(halve_kernel, "az", 0),
+        [(2, total, LANES)] * 2,
+        (keep_sources, moved),
+        cost=0.3,
+        room=room,
+        name="halve",
+    )
+    whole_parts, _ = lax.optimization_barrier((whole, send_sources))
     own_sides, send_sides = call(
         functools.partial(parts_kernel, chips),
         [(2, half, LANES)] * 2,
-        (keep, got, ports, whole, incoming, near, passed),
+        (keep, got, ports, links, whole_parts, incoming, near, passed),
         cost=0.4,
         room=room,
         name="parts",
     )
     got_sides = other_core(send_sides)
-    end_sources = call(
-        functools.partial(slabs_kernel, total),
-        [(2, total, LANES)] * SLABS,
-        (azimuth, *matrices3, *all_ends),
-        (0,),
-        [pltpu.VMEM((SLABS, 2, total, LANES), F32)] * 2 + [pltpu.VMEM((8, total, LANES), F32)],
-        cost=2,
-        room=room,
-        name="slabs",
-    )
-    sources = [end_sources[0]] + [across_slabs(end_sources[d], d) for d in range(1, SLABS)]
+    sources = (keep_sources, hop("az", send_sources, 0))
     all_sources, extra = call(
         functools.partial(sides_kernel, total, kept),
         [(2, total, LANES), (2, length, LANES)],
-        (lam, ends, mu) + scalars4 + tuple(sources) + store,
+        (lam, ends, mu) + scalars4 + sources + store,
         smem(3),
         scratch_store,
         cost=3,
@@ -1205,7 +1286,9 @@
         + scalars4,
         smem(9),
         [pltpu.VMEM((4,) + wide_shape, BF16)] * 2
-        + [pltpu.VMEM((4,) + wide_shape, F32), pltpu.VMEM((length, 2 * LANES), BF16)],
+        + [pltpu.VMEM((4,) + wide_shape, F32), pltpu.VMEM((length * CELLS, 2 * LANES), BF16)]
+        + [pltpu.VMEM((length * CELLS, LANES), F32), pltpu.SemaphoreType.DMA((4,))],
+        out_held=(0,),
         cost=7,
         room=room,
         name="backward",

time: 82 us -> 66.8 us (0.81)
  waiting for transfers between devices: 25.4 us -> 17 us
  starting transfers between devices: 18.7 us -> 13.4 us
  Pallas kernels: 37.3 us -> 35.8 us
    ppermute x6 -> x3, waiting for transfers between devices: 19.9 us -> 0.01 us  [between_chips(): return lax.ppermute(values, 'rad', route)]
    ppermute x6 -> x7, waiting for transfers between devices: 4.35 us -> 16.9 us  [hop(): lax.ppermute(values, axis, [(index, index ^ 1 << bit) for index in range(...]
    ppermute x6 -> x3, starting transfers between devices: 10.8 us -> 6.97 us  [between_chips(): return lax.ppermute(values, 'rad', route)]
    pallas_call x15 -> x21, Pallas kernels: 37.3 us -> 35.8 us  [call(): pl.pallas_call(kernel, out_shape=outs, in_specs=specs, out_specs=[pl.Bloc...]
    ppermute x6 -> x7, starting transfers between devices: 7.11 us -> 5.8 us  [hop(): lax.ppermute(values, axis, [(index, index ^ 1 << bit) for index in range(...]
    ppermute x3 -> x2, waiting for transfers between devices: 1.19 us -> 0.1 us  [other_core(): lax.ppermute(values, 'rad', [(index, index ^ 1) for index in range(count)])]
  transfers between devices with their start and end apart: 15 -> 12, of which waited for: 7 -> 6; matrix products, arithmetic and copies ran while one was open for 0% -> 0% of each run, Pallas kernels for 30% -> 36%
where the time goes in v3:
time: 66.8 us; the launch traced here: 66.7 us
  Pallas kernels  35.8 us (54%)
  waiting for transfers between devices  17 us (25%)
  starting transfers between devices  13.4 us (20%)
    pallas_call x21, Pallas kernels, call(): pl.pallas_call(kernel, out_shape=outs, in_specs=specs, out_specs=[pl.Bloc...  35.8 us
    ppermute x7, waiting for transfers between devices, hop(): lax.ppermute(values, axis, [(index, index ^ 1 << bit) for index in range(...  16.9 us
    ppermute x3, starting transfers between devices, between_chips(): return lax.ppermute(values, 'rad', route)  6.97 us
    ppermute x7, starting transfers between devices, hop(): lax.ppermute(values, axis, [(index, index ^ 1 << bit) for index in range(...  5.8 us
  transfers between devices with their start and end apart: 12, of which 6 were waited for; matrix products, arithmetic and copies ran while one was open for 0% of the time, Pallas kernels for 36%

profile of v3, /device:TPU:0, one launch (start us, length us, event | category | flops | bytes accessed | tf_op | source)
XLA Modules:
  0.0 66.7 jit_solution(11426965837763097242)
XLA Ops:
  0.0 0.0 copy-start.8
  0.0 0.0 copy-start.1
  0.0 0.0 copy-start.9
  0.0 0.0 copy-start.12
  0.0 0.0 copy-start.11
  0.0 0.0 copy-start.10
  0.0 5.6 %forward.1 = (f32[4,1024,128]{2,1,0:T(8,128)}, f32[2,512,128]{2,1,0:T(8,128)}, f32[2,512,128]{2,1,0:T(8,128)}) custom-call(f32[8,512,128]{2,1,0:T(8,128)} %bitcast.2, f32[1032,128]{1,0:T(8,128)} %constant.23.clone.tables_in, bf16[2304,256]{1,0:T(8,128)(2,1)} %constant.28.clone.stages_in, f32[32]{0:T(128)} %rest_0_.13, f32[32]{0:T(128)} %rest_1_.10, ...), custom_call_target="tpu_custom_call" | custom-call | bytes 29520000 | tf_op jit(solution)/shard_map/forward/pallas_call | solution.py:980
  5.6 0.0 copy-start.3
  5.6 0.5 collective-permute-start
  6.2 0.0 copy-done.8
  6.2 0.0 copy-done.1
  6.2 0.0 copy-done.9
  6.2 0.0 copy-done.12
  6.2 0.0 copy-done.11
  6.2 0.0 copy-done.10
  6.2 1.6 %pair_ports.1.ports = f32[11,512,128]{2,1,0:T(8,128)S(1)} custom-call(f32[1024,128]{1,0:T(8,128)S(1)} %copy-done.1, f32[8,128]{1,0:T(8,128)S(1)} %copy-done.8, f32[32]{0:T(128)S(1)} %copy-done.10, f32[32]{0:T(128)S(1)} %copy-done.9, f32[32]{0:T(128)S(1)} %copy-done.11, f32[32]{0:T(128)S(1)} %copy-done.12), custom_call_target="tpu_custom_call" | custom-call | bytes 7380000 | tf_op jit(solution)/shard_map/pair_ports/pallas_call | solution.py:980
  7.8 0.0 copy-start.5
  7.8 0.1 collective-permute-done.got
  7.9 0.0 copy-done.3
  7.9 0.0 copy-start.6
  7.9 0.0 copy-start
  7.9 0.0 copy-start.2
  7.9 0.3 merge.1
  8.2 5.0 %collective-permute-start.7 = (f32[512,128]{1,0:T(8,128)S(1)}, f32[512,128]{1,0:T(8,128)S(1)}, u32[]{:S(2)}, u32[]{:S(2)}) collective-permute-start(f32[512,128]{1,0:T(8,128)S(1)} %get-tuple-element.53), channel_id=1, source_target_pairs={{0,2},{1,3},{6,4},{7,5},{8,10},{9,11},{14,12},{15,13},{16,18},{17,... | collective-permute-start | bytes 786440 | tf_op jit(solution)/shard_map/ppermute | solution.py:1004
  13.3 0.0 copy-done.5
  13.3 3.1 %ratios.1 = (f32[2,640,128]{2,1,0:T(8,128)S(1)}, f32[32,640,128]{2,1,0:T(8,128)S(1)}) custom-call(f32[640,128]{1,0:T(8,128)S(1)} %copy-done.5, f32[8,128]{1,0:T(8,128)S(1)} %copy-done.8, f32[32]{0:T(128)S(1)} %copy-done.10, f32[32]{0:T(128)S(1)} %copy-done.9, f32[32]{0:T(128)S(1)} %copy-done.11, f32[32]{0:T(128)S(1)} %copy-done.12), custom_call_target="tpu_custom_call" | custom-call | bytes 18450000 | tf_op jit(solution)/shard_map/ratios/pallas_call | solution.py:980
  16.4 0.0 copy-done.6
  16.4 0.0 copy-done.7
  16.4 0.0 copy-done.13
  16.4 4.1 %response.1 = f32[2,32,128]{2,1,0:T(8,128)S(1)} custom-call(f32[256,128]{1,0:T(8,128)S(1)} %copy-done.7, f32[256,128]{1,0:T(8,128)S(1)} %copy-done.6, f32[4,128]{1,0:T(4,128)S(1)} %copy-done.13, f32[32]{0:T(128)S(1)} %copy-done.10, f32[32]{0:T(128)S(1)} %copy-done.9, f32[32]{0:T(128)S(1)} %copy-done.11, f32[32]{0:T(128)S(1)} %copy-done.12), custom_call_target="tpu_custom_call" | custom-call | bytes 18450000 | tf_op jit(solution)/shard_map/response/pallas_call | solution.py:980
  20.5 0.0 copy-done
  20.5 0.0 copy-done.2
  20.5 3.3 %ends.4.own = f32[4,32,128]{2,1,0:T(8,128)S(1)} custom-call(f32[2,32,128]{2,1,0:T(8,128)S(1)} %response.1, f32[4,1024,128]{2,1,0:T(8,128)S(1)} %copy-done, f32[1024,128]{1,0:T(8,128)S(1)} %copy-done.1, f32[1024,128]{1,0:T(8,128)S(1)} %copy-done.2, f32[8,128]{1,0:T(8,128)S(1)} %copy-done.8, f32[32]{0:T(128)S(1)} %copy-done.10, f32[32]{0:T(128)S(1)} %copy-done.9, ...), custom_call_target="tpu_custom_call" | custom-call | bytes 11070000 | tf_op jit(solution)/shard_map/ends/pallas_call | solution.py:980
  23.8 0.1 collective-permute-start.1
  23.9 4.3 %collective-permute-done.1.other = f32[4,32,128]{2,1,0:T(8,128)S(1)} collective-permute-done((f32[4,32,128]{2,1,0:T(8,128)S(1)}, f32[4,32,128]{2,1,0:T(8,128)S(1)}, u32[]{:S(2)}, u32[]{:S(2)}) %collective-permute-start.1) | collective-permute-done | bytes 65568 | tf_op jit(solution)/shard_map/ppermute | solution.py:1009
  28.1 0.8 %collective-permute-start.2 = (f32[6,32,128]{2,1,0:T(8,128)S(1)}, f32[6,32,128]{2,1,0:T(8,128)S(1)}, u32[]{:S(2)}, u32[]{:S(2)}) collective-permute-start(f32[6,32,128]{2,1,0:T(8,128)S(1)} %join.5.own), channel_id=1, source_target_pairs={{0,4},{1,5},{2,6},{3,7},{4,0},{5,1},{6,2},{7,3},{8,12},{9,13},{10,... | collective-permute-start | bytes 294920 | tf_op jit(solution)/shard_map/ppermute | solution.py:1009
  28.9 0.3 links.1
  29.2 0.0 collective-permute-done.7.incoming
  29.3 0.2 inward.1.own
  29.4 0.7 %collective-permute-start.8 = (f32[512,128]{1,0:T(8,128)S(1)}, f32[512,128]{1,0:T(8,128)S(1)}, u32[]{:S(2)}, u32[]{:S(2)}) collective-permute-start(f32[512,128]{1,0:T(8,128)S(1)} %inward.1.own), channel_id=1, source_target_pairs={{2,4},{3,5},{4,2},{5,3},{10,12},{11,13},{12,10},{13,11},{18,20},{1... | collective-permute-start | bytes 786440 | tf_op jit(solution)/shard_map/ppermute | solution.py:1004
  30.1 4.7 %collective-permute-done.2.other = f32[6,32,128]{2,1,0:T(8,128)S(1)} collective-permute-done((f32[6,32,128]{2,1,0:T(8,128)S(1)}, f32[6,32,128]{2,1,0:T(8,128)S(1)}, u32[]{:S(2)}, u32[]{:S(2)}) %collective-permute-start.2) | collective-permute-done | bytes 98336 | tf_op jit(solution)/shard_map/ppermute | solution.py:1009
  34.9 0.1 collective-permute-start.3
  34.9 1.4 %collective-permute-done.3.other = f32[10,32,128]{2,1,0:T(8,128)S(1)} collective-permute-done((f32[10,32,128]{2,1,0:T(8,128)S(1)}, f32[10,32,128]{2,1,0:T(8,128)S(1)}, u32[]{:S(2)}, u32[]{:S(2)}) %collective-permute-start.3) | collective-permute-done | bytes 163872 | tf_op jit(solution)/shard_map/ppermute | solution.py:1009
  36.4 1.6 %collective-permute-start.4 = (f32[2,32,128]{2,1,0:T(8,128)S(1)}, f32[2,32,128]{2,1,0:T(8,128)S(1)}, u32[]{:S(2)}, u32[]{:S(2)}) collective-permute-start(f32[2,32,128]{2,1,0:T(8,128)S(1)} %slice.4.own), channel_id=1, source_target_pairs={{0,8},{8,0},{16,24},{24,16},{1,9},{9,1},{17,25},{25,17},{2,10},{10... | collective-permute-start | bytes 98312 | tf_op jit(solution)/shard_map/ppermute | solution.py:1009
  37.9 4.0 %capacity.1 = (f32[32,8,128]{2,1,0:T(8,128)S(1)}, f32[32,8,128]{2,1,0:T(8,128)S(1)}, f32[32,8,128]{2,1,0:T(8,128)S(1)}) custom-call(f32[32]{0:T(128)S(1)} %copy-done.9, f32[18,32,128]{2,1,0:T(8,128)S(1)} %join.7.responses), custom_call_target="tpu_custom_call" | custom-call | bytes 14760000 | tf_op jit(solution)/shard_map/capacity/pallas_call | solution.py:980
  41.9 0.0 collective-permute-done.4.other
  42.0 0.0 collective-permute-done.8.other
  42.0 0.2 middle.1
  42.2 1.3 %collective-permute-start.9 = (f32[512,128]{1,0:T(8,128)S(1)}, f32[512,128]{1,0:T(8,128)S(1)}, u32[]{:S(2)}, u32[]{:S(2)}) collective-permute-start(f32[512,128]{1,0:T(8,128)S(1)} %get-tuple-element.57), channel_id=1, source_target_pairs={{2,0},{3,1},{4,6},{5,7},{10,8},{11,9},{12,14},{13,15},{18,16},{19,... | collective-permute-start | bytes 786440 | tf_op jit(solution)/shard_map/ppermute | solution.py:1004
  43.5 1.6 %collective-permute-start.5 = (f32[4,32,128]{2,1,0:T(8,128)S(1)}, f32[4,32,128]{2,1,0:T(8,128)S(1)}, u32[]{:S(2)}, u32[]{:S(2)}) collective-permute-start(f32[4,32,128]{2,1,0:T(8,128)S(1)} %join.8.own), channel_id=1, source_target_pairs={{0,16},{8,24},{16,0},{24,8},{1,17},{9,25},{17,1},{25,9},{2,18},{10... | collective-permute-start | bytes 196616 | tf_op jit(solution)/shard_map/ppermute | solution.py:1009
  45.1 3.1 %pair.1.pair_matrix = f32[32,8,128]{2,1,0:T(8,128)S(1)} custom-call(f32[32]{0:T(128)S(1)} %copy-done.9, f32[32,8,128]{2,1,0:T(8,128)S(1)} %get-tuple-element.43.minus_matrix, f32[32,8,128]{2,1,0:T(8,128)S(1)} %get-tuple-element.47.plus_matrix), custom_call_target="tpu_custom_call" | custom-call | bytes 11070000 | tf_op jit(solution)/shard_map/pair/pallas_call | solution.py:980
  48.2 0.0 collective-permute-done.5.other
  48.3 1.2 %slabs.1 = (f32[4,32,128]{2,1,0:T(8,128)S(1)}, f32[4,32,128]{2,1,0:T(8,128)S(1)}) custom-call(f32[32]{0:T(128)S(1)} %copy-done.9, f32[32,8,128]{2,1,0:T(8,128)S(1)} %get-tuple-element.43.minus_matrix, f32[32,8,128]{2,1,0:T(8,128)S(1)} %get-tuple-element.44.alternate_matrix, f32[32,8,128]{2,1,0:T(8,128)S(1)} %pair.1.pair_matrix, f32[8,32,128]{2,1,0:T(8,128)S(1)} %join.9.rest_0_), custom_call_target="tpu_custom_call" | custom-call | bytes 7380000 | tf_op jit(solution)/shard_map/slabs/pallas_call | solution.py:980
  49.5 1.2 %collective-permute-start.6 = (f32[4,32,128]{2,1,0:T(8,128)S(1)}, f32[4,32,128]{2,1,0:T(8,128)S(1)}, u32[]{:S(2)}, u32[]{:S(2)}) collective-permute-start(f32[4,32,128]{2,1,0:T(8,128)S(1)} %get-tuple-element.50), channel_id=1, source_target_pairs={{0,16},{8,24},{16,0},{24,8},{1,17},{9,25},{17,1},{25,9},{2,18},{10... | collective-permute-start | bytes 196616 | tf_op jit(solution)/shard_map/ppermute | solution.py:1009
  50.6 3.2 %collective-permute-done.6.other = f32[4,32,128]{2,1,0:T(8,128)S(1)} collective-permute-done((f32[4,32,128]{2,1,0:T(8,128)S(1)}, f32[4,32,128]{2,1,0:T(8,128)S(1)}, u32[]{:S(2)}, u32[]{:S(2)}) %collective-permute-start.6) | collective-permute-done | bytes 65568 | tf_op jit(solution)/shard_map/ppermute | solution.py:1009
  53.8 0.0 collective-permute-done.9.near_two
  53.8 0.5 parts.1
  54.3 0.1 collective-permute-start.10
  54.4 0.6 collective-permute-start.11
  55.0 3.4 %collective-permute-done.11.rest_5_ = f32[2,32,128]{2,1,0:T(8,128)S(1)} collective-permute-done((f32[2,32,128]{2,1,0:T(8,128)S(1)}, f32[2,32,128]{2,1,0:T(8,128)S(1)}, u32[]{:S(2)}, u32[]{:S(2)}) %collective-permute-start.11) | collective-permute-done | bytes 32800 | tf_op jit(solution)/shard_map/ppermute | solution.py:1009
  58.4 3.0 %sides.1 = (f32[2,32,128]{2,1,0:T(8,128)S(1)}, f32[2,1024,128]{2,1,0:T(8,128)S(1)}) custom-call(f32[1024,128]{1,0:T(8,128)S(1)} %copy-done.1, f32[1024,128]{1,0:T(8,128)S(1)} %copy-done.2, f32[8,128]{1,0:T(8,128)S(1)} %copy-done.8, f32[32]{0:T(128)S(1)} %copy-done.10, f32[32]{0:T(128)S(1)} %copy-done.9, f32[32]{0:T(128)S(1)} %copy-done.11, ...), custom_call_target="tpu_custom_call" | custom-call | bytes 11070000 | tf_op jit(solution)/shard_map/sides/pallas_call | solution.py:980
  61.3 0.0 collective-permute-done.10.got
  61.4 0.0 copy-done.4
  61.4 5.3 %backward.1 = f32[4096,128]{1,0:T(8,128)} custom-call(f32[4,1024,128]{2,1,0:T(8,128)S(1)} %copy-done, f32[2,512,128]{2,1,0:T(8,128)S(1)} %get-tuple-element.58.own, f32[2,512,128]{2,1,0:T(8,128)S(1)} %collective-permute-done.10.got, f32[2,1024,128]{2,1,0:T(8,128)S(1)} %get-tuple-element.61.extra, f32[2,32,128]{2,1,0:T(8,128)S(1)} %get-tuple-element.62.sources, ...), custom_call_target="tpu_custom_call" | custom-call | bytes 25830000 | tf_op jit(solution)/shard_map/backward/pallas_call | solution.py:980
  (10 shorter events, 0.1 us)
Async XLA Ops:
  0.0 6.2 %copy-start.8 = (f32[8,128]{1,0:T(8,128)S(1)}, f32[8,128]{1,0:T(8,128)}, u32[]{:S(2)}) copy-start(f32[8,128]{1,0:T(8,128)} %constant.22.clone.mu) | copy-start | bytes 12292
  0.0 6.2 %copy-start.1 = (f32[1024,128]{1,0:T(8,128)S(1)}, f32[1024,128]{1,0:T(8,128)}, u32[]{:S(2)}) copy-start(f32[1024,128]{1,0:T(8,128)} %constant.20.clone.lam) | copy-start | bytes 1572868
  0.0 6.2 %copy-start.9 = (f32[32]{0:T(128)S(1)}, f32[32]{0:T(128)}, u32[]{:S(2)}) copy-start(f32[32]{0:T(128)} %rest_1_.10) | copy-start | bytes 388
  0.0 6.2 %copy-start.12 = (f32[32]{0:T(128)S(1)}, f32[32]{0:T(128)}, u32[]{:S(2)}) copy-start(f32[32]{0:T(128)} %rest_3_.13) | copy-start | bytes 388
  0.0 6.2 %copy-start.11 = (f32[32]{0:T(128)S(1)}, f32[32]{0:T(128)}, u32[]{:S(2)}) copy-start(f32[32]{0:T(128)} %rest_2_.13) | copy-start | bytes 388
  0.0 6.2 %copy-start.10 = (f32[32]{0:T(128)S(1)}, f32[32]{0:T(128)}, u32[]{:S(2)}) copy-start(f32[32]{0:T(128)} %rest_0_.13) | copy-start | bytes 388
  5.6 2.3 %copy-start.3 = (f32[2,512,128]{2,1,0:T(8,128)S(1)}, f32[2,512,128]{2,1,0:T(8,128)}, u32[]{:S(2)}) copy-start(f32[2,512,128]{2,1,0:T(8,128)} %get-tuple-element.35.keep) | copy-start | bytes 1572868
  5.6 2.3 %collective-permute-start = (f32[2,512,128]{2,1,0:T(8,128)}, f32[2,512,128]{2,1,0:T(8,128)S(1)}, u32[]{:S(2)}, u32[]{:S(2)}) collective-permute-start(f32[2,512,128]{2,1,0:T(8,128)} %get-tuple-element.36), channel_id=1, source_target_pairs={{0,1},{1,0},{2,3},{3,2},{4,5},{5,4},{6,7},{7,6},{8,9},{9,8},{10,11... | collective-permute-start | bytes 1572872 | tf_op jit(solution)/shard_map/ppermute | solution.py:999
  7.8 5.5 %copy-start.5 = (f32[640,128]{1,0:T(8,128)S(1)}, f32[640,128]{1,0:T(8,128)}, u32[]{:S(2)}) copy-start(f32[640,128]{1,0:T(8,128)} %constant.24.clone.lam) | copy-start | bytes 983044
  7.9 8.5 %copy-start.6 = (f32[256,128]{1,0:T(8,128)S(1)}, f32[256,128]{1,0:T(8,128)}, u32[]{:S(2)}) copy-start(f32[256,128]{1,0:T(8,128)} %constant.27.clone.weight) | copy-start | bytes 393220
  7.9 8.5 %copy-start.7 = (f32[256,128]{1,0:T(8,128)S(1)}, f32[256,128]{1,0:T(8,128)}, u32[]{:S(2)}) copy-start(f32[256,128]{1,0:T(8,128)} %constant.26.clone.lam) | copy-start | bytes 393220
  7.9 8.5 %copy-start.13 = (f32[4,128]{1,0:T(4,128)S(1)}, f32[4,128]{1,0:T(4,128)}, u32[]{:S(2)}) copy-start(f32[4,128]{1,0:T(4,128)} %constant.25.clone.mu) | copy-start | bytes 6148
  7.9 12.6 %copy-start = (f32[4,1024,128]{2,1,0:T(8,128)S(1)}, f32[4,1024,128]{2,1,0:T(8,128)}, u32[]{:S(2)}) copy-start(f32[4,1024,128]{2,1,0:T(8,128)} %get-tuple-element.34.spectrum) | copy-start | bytes 6291460
  7.9 12.6 %copy-start.2 = (f32[1024,128]{1,0:T(8,128)S(1)}, f32[1024,128]{1,0:T(8,128)}, u32[]{:S(2)}) copy-start(f32[1024,128]{1,0:T(8,128)} %constant.21.clone.ends) | copy-start | bytes 1572868
  8.2 21.0 %collective-permute-start.7 = (f32[512,128]{1,0:T(8,128)S(1)}, f32[512,128]{1,0:T(8,128)S(1)}, u32[]{:S(2)}, u32[]{:S(2)}) collective-permute-start(f32[512,128]{1,0:T(8,128)S(1)} %get-tuple-element.53), channel_id=1, source_target_pairs={{0,2},{1,3},{6,4},{7,5},{8,10},{9,11},{14,12},{15,13},{16,18},{17,... | collective-permute-start | bytes 786440 | tf_op jit(solution)/shard_map/ppermute | solution.py:1004
  23.8 4.3 %collective-permute-start.1 = (f32[4,32,128]{2,1,0:T(8,128)S(1)}, f32[4,32,128]{2,1,0:T(8,128)S(1)}, u32[]{:S(2)}, u32[]{:S(2)}) collective-permute-start(f32[4,32,128]{2,1,0:T(8,128)S(1)} %ends.4.own), channel_id=1, source_target_pairs={{0,2},{1,3},{2,0},{3,1},{4,6},{5,7},{6,4},{7,5},{8,10},{9,11},{10,... | collective-permute-start | bytes 196616 | tf_op jit(solution)/shard_map/ppermute | solution.py:1009
  28.1 6.7 %collective-permute-start.2 = (f32[6,32,128]{2,1,0:T(8,128)S(1)}, f32[6,32,128]{2,1,0:T(8,128)S(1)}, u32[]{:S(2)}, u32[]{:S(2)}) collective-permute-start(f32[6,32,128]{2,1,0:T(8,128)S(1)} %join.5.own), channel_id=1, source_target_pairs={{0,4},{1,5},{2,6},{3,7},{4,0},{5,1},{6,2},{7,3},{8,12},{9,13},{10,... | collective-permute-start | bytes 294920 | tf_op jit(solution)/shard_map/ppermute | solution.py:1009
  29.4 12.5 %collective-permute-start.8 = (f32[512,128]{1,0:T(8,128)S(1)}, f32[512,128]{1,0:T(8,128)S(1)}, u32[]{:S(2)}, u32[]{:S(2)}) collective-permute-start(f32[512,128]{1,0:T(8,128)S(1)} %inward.1.own), channel_id=1, source_target_pairs={{2,4},{3,5},{4,2},{5,3},{10,12},{11,13},{12,10},{13,11},{18,20},{1... | collective-permute-start | bytes 786440 | tf_op jit(solution)/shard_map/ppermute | solution.py:1004
  34.9 1.5 %collective-permute-start.3 = (f32[10,32,128]{2,1,0:T(8,128)S(1)}, f32[10,32,128]{2,1,0:T(8,128)S(1)}, u32[]{:S(2)}, u32[]{:S(2)}) collective-permute-start(f32[10,32,128]{2,1,0:T(8,128)S(1)} %join.6.own), channel_id=1, source_target_pairs={{0,1},{1,0},{2,3},{3,2},{4,5},{5,4},{6,7},{7,6},{8,9},{9,8},{10,11... | collective-permute-start | bytes 491528 | tf_op jit(solution)/shard_map/ppermute | solution.py:1009
  36.4 5.6 %collective-permute-start.4 = (f32[2,32,128]{2,1,0:T(8,128)S(1)}, f32[2,32,128]{2,1,0:T(8,128)S(1)}, u32[]{:S(2)}, u32[]{:S(2)}) collective-permute-start(f32[2,32,128]{2,1,0:T(8,128)S(1)} %slice.4.own), channel_id=1, source_target_pairs={{0,8},{8,0},{16,24},{24,16},{1,9},{9,1},{17,25},{25,17},{2,10},{10... | collective-permute-start | bytes 98312 | tf_op jit(solution)/shard_map/ppermute | solution.py:1009
  42.2 11.6 %collective-permute-start.9 = (f32[512,128]{1,0:T(8,128)S(1)}, f32[512,128]{1,0:T(8,128)S(1)}, u32[]{:S(2)}, u32[]{:S(2)}) collective-permute-start(f32[512,128]{1,0:T(8,128)S(1)} %get-tuple-element.57), channel_id=1, source_target_pairs={{2,0},{3,1},{4,6},{5,7},{10,8},{11,9},{12,14},{13,15},{18,16},{19,... | collective-permute-start | bytes 786440 | tf_op jit(solution)/shard_map/ppermute | solution.py:1004
  43.5 4.7 %collective-permute-start.5 = (f32[4,32,128]{2,1,0:T(8,128)S(1)}, f32[4,32,128]{2,1,0:T(8,128)S(1)}, u32[]{:S(2)}, u32[]{:S(2)}) collective-permute-start(f32[4,32,128]{2,1,0:T(8,128)S(1)} %join.8.own), channel_id=1, source_target_pairs={{0,16},{8,24},{16,0},{24,8},{1,17},{9,25},{17,1},{25,9},{2,18},{10... | collective-permute-start | bytes 196616 | tf_op jit(solution)/shard_map/ppermute | solution.py:1009
  49.5 4.3 %collective-permute-start.6 = (f32[4,32,128]{2,1,0:T(8,128)S(1)}, f32[4,32,128]{2,1,0:T(8,128)S(1)}, u32[]{:S(2)}, u32[]{:S(2)}) collective-permute-start(f32[4,32,128]{2,1,0:T(8,128)S(1)} %get-tuple-element.50), channel_id=1, source_target_pairs={{0,16},{8,24},{16,0},{24,8},{1,17},{9,25},{17,1},{25,9},{2,18},{10... | collective-permute-start | bytes 196616 | tf_op jit(solution)/shard_map/ppermute | solution.py:1009
  54.3 7.1 %collective-permute-start.10 = (f32[2,512,128]{2,1,0:T(8,128)S(1)}, f32[2,512,128]{2,1,0:T(8,128)S(1)}, u32[]{:S(2)}, u32[]{:S(2)}) collective-permute-start(f32[2,512,128]{2,1,0:T(8,128)S(1)} %get-tuple-element.59), channel_id=1, source_target_pairs={{0,1},{1,0},{2,3},{3,2},{4,5},{5,4},{6,7},{7,6},{8,9},{9,8},{10,11... | collective-permute-start | bytes 1572872 | tf_op jit(solution)/shard_map/ppermute | solution.py:999
  54.4 4.0 %collective-permute-start.11 = (f32[2,32,128]{2,1,0:T(8,128)S(1)}, f32[2,32,128]{2,1,0:T(8,128)S(1)}, u32[]{:S(2)}, u32[]{:S(2)}) collective-permute-start(f32[2,32,128]{2,1,0:T(8,128)S(1)} %get-tuple-element.51), channel_id=1, source_target_pairs={{0,8},{8,0},{16,24},{24,16},{1,9},{9,1},{17,25},{25,17},{2,10},{10... | collective-permute-start | bytes 98312 | tf_op jit(solution)/shard_map/ppermute | solution.py:1009
  58.4 3.0 %copy-start.4 = (bf16[2304,256]{1,0:T(8,128)(2,1)S(1)}, bf16[2304,256]{1,0:T(8,128)(2,1)}, u32[]{:S(2)}) copy-start(bf16[2304,256]{1,0:T(8,128)(2,1)} %constant.29.clone.stages) | copy-start | bytes 3538948

commit v4 on v3

--- a/solution.py
+++ b/solution.py
@@ -532,21 +532,13 @@
     chunk = spectrum.shape[1] // 8
     sums[...] = jnp.zeros_like(sums)
 
-    def step(index, _):
-        kind = lax.rem(index, 2)
+    def start(kind, index, view, left, right):
         rows = pl.ds(pl.multiple_of(index * chunk, chunk), chunk)
-        values = lam[rows, :]
-        if kept:
-            view = stored_view(store, index, chunk)
-            left, right = outside(view, first, total)
-        else:
-            view = store
-            left, right = ratios(radial, first, values, level, store, store)
         weight = 2.0 * ends[rows, :]
         answer = solve_block(
             radial,
             first,
-            values,
+            lam[rows, :],
             level,
             [weight * spectrum[cell, rows, :] for cell in range(CELLS)],
             radial.previous(first) * left,
@@ -554,24 +546,48 @@
         )
         for place in range(CELLS):
             sums[kind, first + place] += fold_rows(answer[place])
-
-        def outward_left(move, value):
-            cell = first - 1 - move
-            value = view[cell] * value
-            sums[kind, cell] += fold_rows(value)
-            return value
-
-        def outward_right(move, value):
-            cell = first + CELLS + move
-            value = view[cell] * value
-            sums[kind, cell] += fold_rows(value)
-            return value
-
-        by_blocks(first, outward_left, answer[0])
-        by_blocks(total - CELLS - first, outward_right, answer[-1])
-        return 0
-
-    lax.fori_loop(0, 8, step, 0)
+        return answer
+
+    def spread_out(kinds, views, answers):
+        def onward(cell, values):
+            values = [view[cell] * value for view, value in zip(views, values)]
+            for kind, value in zip(kinds, values):
+                sums[kind, cell] += fold_rows(value)
+            return tuple(values)
+
+        by_blocks(
+            first,
+            lambda move, values: onward(first - 1 - move, values),
+            tuple(answer[0] for answer in answers),
+        )
+        by_blocks(
+            total - CELLS - first,
+            lambda move, values: onward(first + CELLS + move, values),
+            tuple(answer[-1] for answer in answers),
+        )
+
+    if kept:
+
+        def step(slot, _):
+            views = [stored_view(store, 2 * slot + kind, chunk) for kind in range(2)]
+            answers = [
+                start(kind, 2 * slot + kind, views[kind], *outside(views[kind], first, total))
+                for kind in range(2)
+            ]
+            spread_out((0, 1), views, answers)
+            return 0
+
+        lax.fori_loop(0, 4, step, 0)
+    else:
+
+        def step(index, _):
+            kind = lax.rem(index, 2)
+            rows = pl.ds(pl.multiple_of(index * chunk, chunk), chunk)
+            left, right = ratios(radial, first, lam[rows, :], level, store, store)
+            spread_out((kind,), (store,), [start(kind, index, store, left, right)])
+            return 0
+
+        lax.fori_loop(0, 8, step, 0)
     for kind in range(2):
         for cell in range(total):
             out[kind, cell : cell + 1, :] = jnp.sum(sums[kind, cell], axis=0, keepdims=True)
@@ -718,7 +734,7 @@
                     corners[row] = jnp.where(spot, 0.0, corners[row]) - factor * corner
                 lines[place], corners[place] = line, corner
 
-        batch = 16
+        batch = 32
 
         def update(index, _):
             for matrix, (lines, _corners) in zip(matrices, state):
@@ -867,39 +883,57 @@
     first = lax.axis_index("rad") * CELLS
     level = mu[...][:1]
     chunk = lam.shape[0] // 8
-
-    def step(index, _):
-        kind = lax.rem(index, 2)
-        rows = pl.ds(pl.multiple_of(index * chunk, chunk), chunk)
-        values = lam[rows, :]
-        if kept:
-            view = stored_view(store, index, chunk)
-            left, right = outside(view, first, total)
-        else:
-            view = store
-            left, right = ratios(radial, first, values, level, store, store)
-        zero = jnp.zeros((chunk, LANES), F32)
-
-        def passed(cell, value):
-            return view[cell] * (sources[kind, pl.ds(cell, 1), :] + value)
-
-        from_left = by_blocks(first, passed, zero)
+    entry, leave = radial.previous(first), radial.coupling(first + CELLS - 1)
+
+    def inflow(kinds, views):
+        zeros = tuple(jnp.zeros((chunk, LANES), F32) for _ in kinds)
+
+        def passed(cell, values):
+            return tuple(
+                view[cell] * (sources[kind, pl.ds(cell, 1), :] + value)
+                for kind, view, value in zip(kinds, views, values)
+            )
+
+        from_left = by_blocks(first, passed, zeros)
         from_right = by_blocks(
             total - CELLS - first,
-            lambda move, value: passed(total - 1 - move, value),
-            zero,
+            lambda move, values: passed(total - 1 - move, values),
+            zeros,
         )
-        entry, leave = radial.previous(first), radial.coupling(first + CELLS - 1)
+        return from_left, from_right
+
+    def finish(kind, index, left, right, from_left, from_right):
+        rows = pl.ds(pl.multiple_of(index * chunk, chunk), chunk)
         own = [sources[kind, pl.ds(first + place, 1), :] for place in range(CELLS)]
         own[0] = own[0] + from_left
         own[-1] = own[-1] + from_right
-        answer = solve_block(radial, first, values, level, own, entry * left, leave * right)
+        answer = solve_block(radial, first, lam[rows, :], level, own, entry * left, leave * right)
         weight = ends[rows, :]
         out[0, rows, :] = weight * (from_left + entry * left * answer[0])
         out[1, rows, :] = weight * (from_right + leave * right * answer[-1])
-        return 0
-
-    lax.fori_loop(0, 8, step, 0)
+
+    if kept:
+
+        def step(slot, _):
+            views = [stored_view(store, 2 * slot + kind, chunk) for kind in range(2)]
+            from_left, from_right = inflow((0, 1), views)
+            for kind, view in enumerate(views):
+                left, right = outside(view, first, total)
+                finish(kind, 2 * slot + kind, left, right, from_left[kind], from_right[kind])
+            return 0
+
+        lax.fori_loop(0, 4, step, 0)
+    else:
+
+        def step(index, _):
+            kind = lax.rem(index, 2)
+            rows = pl.ds(pl.multiple_of(index * chunk, chunk), chunk)
+            left, right = ratios(radial, first, lam[rows, :], level, store, store)
+            from_left, from_right = inflow((kind,), (store,))
+            finish(kind, index, left, right, from_left[0], from_right[0])
+            return 0
+
+        lax.fori_loop(0, 8, step, 0)
 
 
 def backward_kernel(total, spectrum, own, got, extra, sources, stages, lam, ends, mu, *rest):
@@ -910,7 +944,7 @@
     core = lax.rem(lax.axis_index("rad"), 2)
     first = lax.axis_index("rad") * CELLS
     level = mu[...][:1]
-    chunk = min(64, quarter)
+    chunk = min(128, quarter)
     entry, leave = radial.previous(first), radial.coupling(first + CELLS - 1)
 
     for slot in range(4):
@@ -976,7 +1010,14 @@
     for place in range(len(args)):
         space = pltpu.SMEM if place in scalars else pltpu.HBM if place in held else pltpu.VMEM
         specs.append(pl.BlockSpec(memory_space=space))
-    outs = [jax.ShapeDtypeStruct(shape, F32) for shape in out_shapes]
+    outs = [
+        (pltpu.HBM if place in out_held else jax.ShapeDtypeStruct)(shape, F32)
+        for place, shape in enumerate(out_shapes)
+    ]
+    args = [
+        pltpu.with_memory_space_constraint(arg, pltpu.HBM) if place in held else arg
+        for place, arg in enumerate(args)
+    ]
     return pl.pallas_call(
         kernel,
         out_shape=outs,
@@ -1074,7 +1115,7 @@
         cost=8,
         held=tuple(range(7)),
         out_held=(0,),
-        room=57,
+        room=room,
         name="forward",
     )
     got = other_core(send)

time: 66.8 us -> 63.9 us (0.957)
  Pallas kernels: 35.8 us -> 32.3 us
    pallas_call x21, Pallas kernels: 35.8 us -> 32.3 us  [call(): pl.pallas_call(kernel, out_shape=outs, in_specs=specs, out_specs=[pl.Bloc...]
  transfers between devices with their start and end apart: 12 -> 12, of which waited for: 6 -> 6; matrix products, arithmetic and copies ran while one was open for 0% -> 0% of each run, Pallas kernels for 36% -> 34%
where the time goes in v4:
time: 63.9 us; the launch traced here: 63.8 us
  Pallas kernels  32.3 us (51%)
  waiting for transfers between devices  17.2 us (27%)
  starting transfers between devices  13.8 us (22%)
    pallas_call x21, Pallas kernels, call(): pl.pallas_call(kernel, out_shape=outs, in_specs=specs, out_specs=[pl.Bloc...  32.3 us
    ppermute x7, waiting for transfers between devices, hop(): lax.ppermute(values, axis, [(index, index ^ 1 << bit) for index in range(...  17.2 us
    ppermute x3, starting transfers between devices, between_chips(): return lax.ppermute(values, 'rad', route)  6.81 us
    ppermute x7, starting transfers between devices, hop(): lax.ppermute(values, axis, [(index, index ^ 1 << bit) for index in range(...  6.39 us
  transfers between devices with their start and end apart: 12, of which 6 were waited for; matrix products, arithmetic and copies ran while one was open for 0% of the time, Pallas kernels for 34%

profile of v4, /device:TPU:0, one launch (start us, length us, event | category | flops | bytes accessed | tf_op | source)
XLA Modules:
  0.0 63.8 jit_solution(3154171804909797693)
XLA Ops:
  0.0 0.0 copy-start.7
  0.0 0.0 copy-start.1
  0.0 0.0 copy-start.8
  0.0 0.0 copy-start.10
  0.0 0.0 copy-start.9
  0.0 4.6 %forward.1 = (f32[4,1024,128]{2,1,0:T(8,128)}, f32[2,512,128]{2,1,0:T(8,128)S(1)}, f32[2,512,128]{2,1,0:T(8,128)S(1)}) custom-call(f32[8,512,128]{2,1,0:T(8,128)} %bitcast.2, f32[1032,128]{1,0:T(8,128)} %constant.23.clone.tables_in, bf16[2304,256]{1,0:T(8,128)(2,1)} %constant.28.clone.stages_in, f32[32]{0:T(128)} %rest_0_.13, f32[32]{0:T(128)} %rest_1_.10, ...), custom_call_target="tpu_custom_call" | custom-call | bytes 29520000 | tf_op jit(solution)/shard_map/forward/pallas_call | solution.py:1021
  4.6 0.5 collective-permute-start
  5.2 0.0 copy-done.7
  5.2 0.0 copy-done.1
  5.2 0.0 copy-done.8
  5.2 0.0 copy-done.11
  5.2 0.0 copy-done.10
  5.2 0.0 copy-done.9
  5.2 1.6 %pair_ports.1.ports = f32[11,512,128]{2,1,0:T(8,128)S(1)} custom-call(f32[1024,128]{1,0:T(8,128)S(1)} %copy-done.1, f32[8,128]{1,0:T(8,128)S(1)} %copy-done.7, f32[32]{0:T(128)S(1)} %copy-done.9, f32[32]{0:T(128)S(1)} %copy-done.8, f32[32]{0:T(128)S(1)} %copy-done.10, f32[32]{0:T(128)S(1)} %copy-done.11), custom_call_target="tpu_custom_call" | custom-call | bytes 7380000 | tf_op jit(solution)/shard_map/pair_ports/pallas_call | solution.py:1021
  6.8 0.0 copy-start.4
  6.8 0.0 collective-permute-done.got
  6.8 0.0 copy-start.5
  6.8 0.0 copy-start.6
  6.8 0.0 copy-start.12
  6.9 0.0 copy-start
  6.9 0.0 copy-start.2
  6.9 0.3 merge.1
  7.2 4.8 %collective-permute-start.7 = (f32[512,128]{1,0:T(8,128)S(1)}, f32[512,128]{1,0:T(8,128)S(1)}, u32[]{:S(2)}, u32[]{:S(2)}) collective-permute-start(f32[512,128]{1,0:T(8,128)S(1)} %get-tuple-element.53), channel_id=1, source_target_pairs={{0,2},{1,3},{6,4},{7,5},{8,10},{9,11},{14,12},{15,13},{16,18},{17,... | collective-permute-start | bytes 786440 | tf_op jit(solution)/shard_map/ppermute | solution.py:1045
  12.0 0.0 copy-done.4
  12.0 3.1 %ratios.1 = (f32[2,640,128]{2,1,0:T(8,128)S(1)}, f32[32,640,128]{2,1,0:T(8,128)S(1)}) custom-call(f32[640,128]{1,0:T(8,128)S(1)} %copy-done.4, f32[8,128]{1,0:T(8,128)S(1)} %copy-done.7, f32[32]{0:T(128)S(1)} %copy-done.9, f32[32]{0:T(128)S(1)} %copy-done.8, f32[32]{0:T(128)S(1)} %copy-done.10, f32[32]{0:T(128)S(1)} %copy-done.11), custom_call_target="tpu_custom_call" | custom-call | bytes 18450000 | tf_op jit(solution)/shard_map/ratios/pallas_call | solution.py:1021
  15.2 0.0 copy-done.5
  15.2 0.0 copy-done.6
  15.2 0.0 copy-done.12
  15.2 4.1 %response.1 = f32[2,32,128]{2,1,0:T(8,128)S(1)} custom-call(f32[256,128]{1,0:T(8,128)S(1)} %copy-done.6, f32[256,128]{1,0:T(8,128)S(1)} %copy-done.5, f32[4,128]{1,0:T(4,128)S(1)} %copy-done.12, f32[32]{0:T(128)S(1)} %copy-done.9, f32[32]{0:T(128)S(1)} %copy-done.8, f32[32]{0:T(128)S(1)} %copy-done.10, f32[32]{0:T(128)S(1)} %copy-done.11), custom_call_target="tpu_custom_call" | custom-call | bytes 18450000 | tf_op jit(solution)/shard_map/response/pallas_call | solution.py:1021
  19.3 0.0 copy-done
  19.3 0.0 copy-done.2
  19.3 3.0 %ends.4.own = f32[4,32,128]{2,1,0:T(8,128)S(1)} custom-call(f32[2,32,128]{2,1,0:T(8,128)S(1)} %response.1, f32[4,1024,128]{2,1,0:T(8,128)S(1)} %copy-done, f32[1024,128]{1,0:T(8,128)S(1)} %copy-done.1, f32[1024,128]{1,0:T(8,128)S(1)} %copy-done.2, f32[8,128]{1,0:T(8,128)S(1)} %copy-done.7, f32[32]{0:T(128)S(1)} %copy-done.9, f32[32]{0:T(128)S(1)} %copy-done.8, ...), custom_call_target="tpu_custom_call" | custom-call | bytes 11070000 | tf_op jit(solution)/shard_map/ends/pallas_call | solution.py:1021
  22.3 0.1 collective-permute-start.1
  22.3 4.3 %collective-permute-done.1.other = f32[4,32,128]{2,1,0:T(8,128)S(1)} collective-permute-done((f32[4,32,128]{2,1,0:T(8,128)S(1)}, f32[4,32,128]{2,1,0:T(8,128)S(1)}, u32[]{:S(2)}, u32[]{:S(2)}) %collective-permute-start.1) | collective-permute-done | bytes 65568 | tf_op jit(solution)/shard_map/ppermute | solution.py:1050
  26.6 0.7 %collective-permute-start.2 = (f32[6,32,128]{2,1,0:T(8,128)S(1)}, f32[6,32,128]{2,1,0:T(8,128)S(1)}, u32[]{:S(2)}, u32[]{:S(2)}) collective-permute-start(f32[6,32,128]{2,1,0:T(8,128)S(1)} %join.5.own), channel_id=1, source_target_pairs={{0,4},{1,5},{2,6},{3,7},{4,0},{5,1},{6,2},{7,3},{8,12},{9,13},{10,... | collective-permute-start | bytes 294920 | tf_op jit(solution)/shard_map/ppermute | solution.py:1050
  27.3 0.3 links.1
  27.6 0.0 collective-permute-done.7.incoming
  27.6 0.2 inward.1.own
  27.8 0.7 %collective-permute-start.8 = (f32[512,128]{1,0:T(8,128)S(1)}, f32[512,128]{1,0:T(8,128)S(1)}, u32[]{:S(2)}, u32[]{:S(2)}) collective-permute-start(f32[512,128]{1,0:T(8,128)S(1)} %inward.1.own), channel_id=1, source_target_pairs={{2,4},{3,5},{4,2},{5,3},{10,12},{11,13},{12,10},{13,11},{18,20},{1... | collective-permute-start | bytes 786440 | tf_op jit(solution)/shard_map/ppermute | solution.py:1045
  28.5 5.0 %collective-permute-done.2.other = f32[6,32,128]{2,1,0:T(8,128)S(1)} collective-permute-done((f32[6,32,128]{2,1,0:T(8,128)S(1)}, f32[6,32,128]{2,1,0:T(8,128)S(1)}, u32[]{:S(2)}, u32[]{:S(2)}) %collective-permute-start.2) | collective-permute-done | bytes 98336 | tf_op jit(solution)/shard_map/ppermute | solution.py:1050
  33.5 0.1 collective-permute-start.3
  33.6 1.4 %collective-permute-done.3.other = f32[10,32,128]{2,1,0:T(8,128)S(1)} collective-permute-done((f32[10,32,128]{2,1,0:T(8,128)S(1)}, f32[10,32,128]{2,1,0:T(8,128)S(1)}, u32[]{:S(2)}, u32[]{:S(2)}) %collective-permute-start.3) | collective-permute-done | bytes 163872 | tf_op jit(solution)/shard_map/ppermute | solution.py:1050
  35.1 1.5 %collective-permute-start.4 = (f32[2,32,128]{2,1,0:T(8,128)S(1)}, f32[2,32,128]{2,1,0:T(8,128)S(1)}, u32[]{:S(2)}, u32[]{:S(2)}) collective-permute-start(f32[2,32,128]{2,1,0:T(8,128)S(1)} %slice.4.own), channel_id=1, source_target_pairs={{0,8},{8,0},{16,24},{24,16},{1,9},{9,1},{17,25},{25,17},{2,10},{10... | collective-permute-start | bytes 98312 | tf_op jit(solution)/shard_map/ppermute | solution.py:1050
  36.6 3.1 %capacity.1 = (f32[32,8,128]{2,1,0:T(8,128)S(1)}, f32[32,8,128]{2,1,0:T(8,128)S(1)}, f32[32,8,128]{2,1,0:T(8,128)S(1)}) custom-call(f32[32]{0:T(128)S(1)} %copy-done.8, f32[18,32,128]{2,1,0:T(8,128)S(1)} %join.7.responses), custom_call_target="tpu_custom_call" | custom-call | bytes 14760000 | tf_op jit(solution)/shard_map/capacity/pallas_call | solution.py:1021
  39.7 0.0 collective-permute-done.4.other
  39.8 0.0 collective-permute-done.8.other
  39.8 0.2 middle.1
  40.0 1.3 %collective-permute-start.9 = (f32[512,128]{1,0:T(8,128)S(1)}, f32[512,128]{1,0:T(8,128)S(1)}, u32[]{:S(2)}, u32[]{:S(2)}) collective-permute-start(f32[512,128]{1,0:T(8,128)S(1)} %get-tuple-element.57), channel_id=1, source_target_pairs={{2,0},{3,1},{4,6},{5,7},{10,8},{11,9},{12,14},{13,15},{18,16},{19,... | collective-permute-start | bytes 786440 | tf_op jit(solution)/shard_map/ppermute | solution.py:1045
  41.3 1.6 %collective-permute-start.5 = (f32[4,32,128]{2,1,0:T(8,128)S(1)}, f32[4,32,128]{2,1,0:T(8,128)S(1)}, u32[]{:S(2)}, u32[]{:S(2)}) collective-permute-start(f32[4,32,128]{2,1,0:T(8,128)S(1)} %join.8.own), channel_id=1, source_target_pairs={{0,16},{8,24},{16,0},{24,8},{1,17},{9,25},{17,1},{25,9},{2,18},{10... | collective-permute-start | bytes 196616 | tf_op jit(solution)/shard_map/ppermute | solution.py:1050
  42.9 2.1 %pair.1.pair_matrix = f32[32,8,128]{2,1,0:T(8,128)S(1)} custom-call(f32[32]{0:T(128)S(1)} %copy-done.8, f32[32,8,128]{2,1,0:T(8,128)S(1)} %get-tuple-element.43.minus_matrix, f32[32,8,128]{2,1,0:T(8,128)S(1)} %get-tuple-element.47.plus_matrix), custom_call_target="tpu_custom_call" | custom-call | bytes 11070000 | tf_op jit(solution)/shard_map/pair/pallas_call | solution.py:1021
  45.0 0.6 collective-permute-done.5.other
  45.6 1.2 %slabs.1 = (f32[4,32,128]{2,1,0:T(8,128)S(1)}, f32[4,32,128]{2,1,0:T(8,128)S(1)}) custom-call(f32[32]{0:T(128)S(1)} %copy-done.8, f32[32,8,128]{2,1,0:T(8,128)S(1)} %get-tuple-element.43.minus_matrix, f32[32,8,128]{2,1,0:T(8,128)S(1)} %get-tuple-element.44.alternate_matrix, f32[32,8,128]{2,1,0:T(8,128)S(1)} %pair.1.pair_matrix, f32[8,32,128]{2,1,0:T(8,128)S(1)} %join.9.rest_0_), custom_call_target="tpu_custom_call" | custom-call | bytes 7380000 | tf_op jit(solution)/shard_map/slabs/pallas_call | solution.py:1021
  46.9 1.6 %collective-permute-start.6 = (f32[4,32,128]{2,1,0:T(8,128)S(1)}, f32[4,32,128]{2,1,0:T(8,128)S(1)}, u32[]{:S(2)}, u32[]{:S(2)}) collective-permute-start(f32[4,32,128]{2,1,0:T(8,128)S(1)} %get-tuple-element.50), channel_id=1, source_target_pairs={{0,16},{8,24},{16,0},{24,8},{1,17},{9,25},{17,1},{25,9},{2,18},{10... | collective-permute-start | bytes 196616 | tf_op jit(solution)/shard_map/ppermute | solution.py:1050
  48.5 2.7 %collective-permute-done.6.other = f32[4,32,128]{2,1,0:T(8,128)S(1)} collective-permute-done((f32[4,32,128]{2,1,0:T(8,128)S(1)}, f32[4,32,128]{2,1,0:T(8,128)S(1)}, u32[]{:S(2)}, u32[]{:S(2)}) %collective-permute-start.6) | collective-permute-done | bytes 65568 | tf_op jit(solution)/shard_map/ppermute | solution.py:1050
  51.2 0.0 collective-permute-done.9.near_two
  51.2 0.5 parts.1
  51.7 0.1 collective-permute-start.10
  51.8 0.8 %collective-permute-start.11 = (f32[2,32,128]{2,1,0:T(8,128)S(1)}, f32[2,32,128]{2,1,0:T(8,128)S(1)}, u32[]{:S(2)}, u32[]{:S(2)}) collective-permute-start(f32[2,32,128]{2,1,0:T(8,128)S(1)} %get-tuple-element.51), channel_id=1, source_target_pairs={{0,8},{8,0},{16,24},{24,16},{1,9},{9,1},{17,25},{25,17},{2,10},{10... | collective-permute-start | bytes 98312 | tf_op jit(solution)/shard_map/ppermute | solution.py:1050
  52.6 3.2 %collective-permute-done.11.rest_5_ = f32[2,32,128]{2,1,0:T(8,128)S(1)} collective-permute-done((f32[2,32,128]{2,1,0:T(8,128)S(1)}, f32[2,32,128]{2,1,0:T(8,128)S(1)}, u32[]{:S(2)}, u32[]{:S(2)}) %collective-permute-start.11) | collective-permute-done | bytes 32800 | tf_op jit(solution)/shard_map/ppermute | solution.py:1050
  55.7 0.0 copy-start.3
  55.7 2.9 %sides.1 = (f32[2,32,128]{2,1,0:T(8,128)S(1)}, f32[2,1024,128]{2,1,0:T(8,128)S(1)}) custom-call(f32[1024,128]{1,0:T(8,128)S(1)} %copy-done.1, f32[1024,128]{1,0:T(8,128)S(1)} %copy-done.2, f32[8,128]{1,0:T(8,128)S(1)} %copy-done.7, f32[32]{0:T(128)S(1)} %copy-done.9, f32[32]{0:T(128)S(1)} %copy-done.8, f32[32]{0:T(128)S(1)} %copy-done.10, f32[32]{0:T(128)S(1)} %copy-done.11, ...), custom_call_target="tpu_custom_call" | custom-call | bytes 11070000 | tf_op jit(solution)/shard_map/sides/pallas_call | solution.py:1021
  58.6 0.0 collective-permute-done.10.got
  58.7 0.0 copy-done.3
  58.7 5.1 %backward.1 = f32[4096,128]{1,0:T(8,128)} custom-call(f32[4,1024,128]{2,1,0:T(8,128)S(1)} %copy-done, f32[2,512,128]{2,1,0:T(8,128)S(1)} %get-tuple-element.58.own, f32[2,512,128]{2,1,0:T(8,128)S(1)} %collective-permute-done.10.got, f32[2,1024,128]{2,1,0:T(8,128)S(1)} %get-tuple-element.61.extra, f32[2,32,128]{2,1,0:T(8,128)S(1)} %get-tuple-element.62.sources, ...), custom_call_target="tpu_custom_call" | custom-call | bytes 25830000 | tf_op jit(solution)/shard_map/backward/pallas_call | solution.py:1021
  (8 shorter events, 0.1 us)
Async XLA Ops:
  0.0 5.2 %copy-start.7 = (f32[8,128]{1,0:T(8,128)S(1)}, f32[8,128]{1,0:T(8,128)}, u32[]{:S(2)}) copy-start(f32[8,128]{1,0:T(8,128)} %constant.22.clone.mu) | copy-start | bytes 12292
  0.0 5.2 %copy-start.1 = (f32[1024,128]{1,0:T(8,128)S(1)}, f32[1024,128]{1,0:T(8,128)}, u32[]{:S(2)}) copy-start(f32[1024,128]{1,0:T(8,128)} %constant.20.clone.lam) | copy-start | bytes 1572868
  0.0 5.2 %copy-start.8 = (f32[32]{0:T(128)S(1)}, f32[32]{0:T(128)}, u32[]{:S(2)}) copy-start(f32[32]{0:T(128)} %rest_1_.10) | copy-start | bytes 388
  0.0 5.2 %copy-start.11 = (f32[32]{0:T(128)S(1)}, f32[32]{0:T(128)}, u32[]{:S(2)}) copy-start(f32[32]{0:T(128)} %rest_3_.13) | copy-start | bytes 388
  0.0 5.2 %copy-start.10 = (f32[32]{0:T(128)S(1)}, f32[32]{0:T(128)}, u32[]{:S(2)}) copy-start(f32[32]{0:T(128)} %rest_2_.13) | copy-start | bytes 388
  0.0 5.2 %copy-start.9 = (f32[32]{0:T(128)S(1)}, f32[32]{0:T(128)}, u32[]{:S(2)}) copy-start(f32[32]{0:T(128)} %rest_0_.13) | copy-start | bytes 388
  4.6 2.2 %collective-permute-start = (f32[2,512,128]{2,1,0:T(8,128)S(1)}, f32[2,512,128]{2,1,0:T(8,128)S(1)}, u32[]{:S(2)}, u32[]{:S(2)}) collective-permute-start(f32[2,512,128]{2,1,0:T(8,128)S(1)} %get-tuple-element.36), channel_id=1, source_target_pairs={{0,1},{1,0},{2,3},{3,2},{4,5},{5,4},{6,7},{7,6},{8,9},{9,8},{10,11... | collective-permute-start | bytes 1572872 | tf_op jit(solution)/shard_map/ppermute | solution.py:1040
  6.8 5.2 %copy-start.4 = (f32[640,128]{1,0:T(8,128)S(1)}, f32[640,128]{1,0:T(8,128)}, u32[]{:S(2)}) copy-start(f32[640,128]{1,0:T(8,128)} %constant.24.clone.lam) | copy-start | bytes 983044
  6.8 8.4 %copy-start.5 = (f32[256,128]{1,0:T(8,128)S(1)}, f32[256,128]{1,0:T(8,128)}, u32[]{:S(2)}) copy-start(f32[256,128]{1,0:T(8,128)} %constant.27.clone.weight) | copy-start | bytes 393220
  6.8 8.4 %copy-start.6 = (f32[256,128]{1,0:T(8,128)S(1)}, f32[256,128]{1,0:T(8,128)}, u32[]{:S(2)}) copy-start(f32[256,128]{1,0:T(8,128)} %constant.26.clone.lam) | copy-start | bytes 393220
  6.8 8.4 %copy-start.12 = (f32[4,128]{1,0:T(4,128)S(1)}, f32[4,128]{1,0:T(4,128)}, u32[]{:S(2)}) copy-start(f32[4,128]{1,0:T(4,128)} %constant.25.clone.mu) | copy-start | bytes 6148
  6.9 12.4 %copy-start = (f32[4,1024,128]{2,1,0:T(8,128)S(1)}, f32[4,1024,128]{2,1,0:T(8,128)}, u32[]{:S(2)}) copy-start(f32[4,1024,128]{2,1,0:T(8,128)} %get-tuple-element.34.spectrum) | copy-start | bytes 6291460
  6.9 12.4 %copy-start.2 = (f32[1024,128]{1,0:T(8,128)S(1)}, f32[1024,128]{1,0:T(8,128)}, u32[]{:S(2)}) copy-start(f32[1024,128]{1,0:T(8,128)} %constant.21.clone.ends) | copy-start | bytes 1572868
  7.2 20.4 %collective-permute-start.7 = (f32[512,128]{1,0:T(8,128)S(1)}, f32[512,128]{1,0:T(8,128)S(1)}, u32[]{:S(2)}, u32[]{:S(2)}) collective-permute-start(f32[512,128]{1,0:T(8,128)S(1)} %get-tuple-element.53), channel_id=1, source_target_pairs={{0,2},{1,3},{6,4},{7,5},{8,10},{9,11},{14,12},{15,13},{16,18},{17,... | collective-permute-start | bytes 786440 | tf_op jit(solution)/shard_map/ppermute | solution.py:1045
  22.3 4.3 %collective-permute-start.1 = (f32[4,32,128]{2,1,0:T(8,128)S(1)}, f32[4,32,128]{2,1,0:T(8,128)S(1)}, u32[]{:S(2)}, u32[]{:S(2)}) collective-permute-start(f32[4,32,128]{2,1,0:T(8,128)S(1)} %ends.4.own), channel_id=1, source_target_pairs={{0,2},{1,3},{2,0},{3,1},{4,6},{5,7},{6,4},{7,5},{8,10},{9,11},{10,... | collective-permute-start | bytes 196616 | tf_op jit(solution)/shard_map/ppermute | solution.py:1050
  26.6 6.9 %collective-permute-start.2 = (f32[6,32,128]{2,1,0:T(8,128)S(1)}, f32[6,32,128]{2,1,0:T(8,128)S(1)}, u32[]{:S(2)}, u32[]{:S(2)}) collective-permute-start(f32[6,32,128]{2,1,0:T(8,128)S(1)} %join.5.own), channel_id=1, source_target_pairs={{0,4},{1,5},{2,6},{3,7},{4,0},{5,1},{6,2},{7,3},{8,12},{9,13},{10,... | collective-permute-start | bytes 294920 | tf_op jit(solution)/shard_map/ppermute | solution.py:1050
  27.8 11.9 %collective-permute-start.8 = (f32[512,128]{1,0:T(8,128)S(1)}, f32[512,128]{1,0:T(8,128)S(1)}, u32[]{:S(2)}, u32[]{:S(2)}) collective-permute-start(f32[512,128]{1,0:T(8,128)S(1)} %inward.1.own), channel_id=1, source_target_pairs={{2,4},{3,5},{4,2},{5,3},{10,12},{11,13},{12,10},{13,11},{18,20},{1... | collective-permute-start | bytes 786440 | tf_op jit(solution)/shard_map/ppermute | solution.py:1045
  33.5 1.5 %collective-permute-start.3 = (f32[10,32,128]{2,1,0:T(8,128)S(1)}, f32[10,32,128]{2,1,0:T(8,128)S(1)}, u32[]{:S(2)}, u32[]{:S(2)}) collective-permute-start(f32[10,32,128]{2,1,0:T(8,128)S(1)} %join.6.own), channel_id=1, source_target_pairs={{0,1},{1,0},{2,3},{3,2},{4,5},{5,4},{6,7},{7,6},{8,9},{9,8},{10,11... | collective-permute-start | bytes 491528 | tf_op jit(solution)/shard_map/ppermute | solution.py:1050
  35.1 4.7 %collective-permute-start.4 = (f32[2,32,128]{2,1,0:T(8,128)S(1)}, f32[2,32,128]{2,1,0:T(8,128)S(1)}, u32[]{:S(2)}, u32[]{:S(2)}) collective-permute-start(f32[2,32,128]{2,1,0:T(8,128)S(1)} %slice.4.own), channel_id=1, source_target_pairs={{0,8},{8,0},{16,24},{24,16},{1,9},{9,1},{17,25},{25,17},{2,10},{10... | collective-permute-start | bytes 98312 | tf_op jit(solution)/shard_map/ppermute | solution.py:1050
  40.0 11.2 %collective-permute-start.9 = (f32[512,128]{1,0:T(8,128)S(1)}, f32[512,128]{1,0:T(8,128)S(1)}, u32[]{:S(2)}, u32[]{:S(2)}) collective-permute-start(f32[512,128]{1,0:T(8,128)S(1)} %get-tuple-element.57), channel_id=1, source_target_pairs={{2,0},{3,1},{4,6},{5,7},{10,8},{11,9},{12,14},{13,15},{18,16},{19,... | collective-permute-start | bytes 786440 | tf_op jit(solution)/shard_map/ppermute | solution.py:1045
  41.3 4.3 %collective-permute-start.5 = (f32[4,32,128]{2,1,0:T(8,128)S(1)}, f32[4,32,128]{2,1,0:T(8,128)S(1)}, u32[]{:S(2)}, u32[]{:S(2)}) collective-permute-start(f32[4,32,128]{2,1,0:T(8,128)S(1)} %join.8.own), channel_id=1, source_target_pairs={{0,16},{8,24},{16,0},{24,8},{1,17},{9,25},{17,1},{25,9},{2,18},{10... | collective-permute-start | bytes 196616 | tf_op jit(solution)/shard_map/ppermute | solution.py:1050
  46.9 4.3 %collective-permute-start.6 = (f32[4,32,128]{2,1,0:T(8,128)S(1)}, f32[4,32,128]{2,1,0:T(8,128)S(1)}, u32[]{:S(2)}, u32[]{:S(2)}) collective-permute-start(f32[4,32,128]{2,1,0:T(8,128)S(1)} %get-tuple-element.50), channel_id=1, source_target_pairs={{0,16},{8,24},{16,0},{24,8},{1,17},{9,25},{17,1},{25,9},{2,18},{10... | collective-permute-start | bytes 196616 | tf_op jit(solution)/shard_map/ppermute | solution.py:1050
  51.7 7.0 %collective-permute-start.10 = (f32[2,512,128]{2,1,0:T(8,128)S(1)}, f32[2,512,128]{2,1,0:T(8,128)S(1)}, u32[]{:S(2)}, u32[]{:S(2)}) collective-permute-start(f32[2,512,128]{2,1,0:T(8,128)S(1)} %get-tuple-element.59), channel_id=1, source_target_pairs={{0,1},{1,0},{2,3},{3,2},{4,5},{5,4},{6,7},{7,6},{8,9},{9,8},{10,11... | collective-permute-start | bytes 1572872 | tf_op jit(solution)/shard_map/ppermute | solution.py:1040
  51.8 4.0 %collective-permute-start.11 = (f32[2,32,128]{2,1,0:T(8,128)S(1)}, f32[2,32,128]{2,1,0:T(8,128)S(1)}, u32[]{:S(2)}, u32[]{:S(2)}) collective-permute-start(f32[2,32,128]{2,1,0:T(8,128)S(1)} %get-tuple-element.51), channel_id=1, source_target_pairs={{0,8},{8,0},{16,24},{24,16},{1,9},{9,1},{17,25},{25,17},{2,10},{10... | collective-permute-start | bytes 98312 | tf_op jit(solution)/shard_map/ppermute | solution.py:1050
  55.7 2.9 %copy-start.3 = (bf16[2304,256]{1,0:T(8,128)(2,1)S(1)}, bf16[2304,256]{1,0:T(8,128)(2,1)}, u32[]{:S(2)}) copy-start(bf16[2304,256]{1,0:T(8,128)(2,1)} %constant.29.clone.stages) | copy-start | bytes 3538948

commit v5 on v4

--- a/solution.py
+++ b/solution.py
@@ -275,17 +275,18 @@
     def step(index, _):
         ends = []
         for part in range(2):
-            rows = pl.ds(pl.multiple_of(part * half + index * chunk, chunk), chunk)
+            rows = pl.ds(part * half + index * chunk, chunk)
             right = [spectrum[cell, rows, :] for cell in range(CELLS)]
             answer = solve_block(radial, first, tables[rows, :], level, right)
             ends.append((answer[0], answer[-1]))
-        rows = pl.ds(pl.multiple_of(index * chunk, chunk), chunk)
+        rows = pl.ds(index * chunk, chunk)
         for place in range(2):
             keep[place, rows, :] = jnp.where(core == 0, ends[0][place], ends[1][place])
             send[place, rows, :] = jnp.where(core == 0, ends[1][place], ends[0][place])
         return 0
 
-    lax.fori_loop(0, half // chunk, step, 0)
+    for index in range(half // chunk):
+        step(index, 0)
     for copy in leaving:
         copy.wait()
 
@@ -944,16 +945,16 @@
     core = lax.rem(lax.axis_index("rad"), 2)
     first = lax.axis_index("rad") * CELLS
     level = mu[...][:1]
-    chunk = min(128, quarter)
+    chunk = min(64, quarter)
     entry, leave = radial.previous(first), radial.coupling(first + CELLS - 1)
 
     for slot in range(4):
 
         def step(index, _):
             kind = index // (quarter // chunk)
-            spot = pl.ds(pl.multiple_of(index * chunk, chunk), chunk)
-            rows = pl.ds(pl.multiple_of(slot * 2 * quarter + index * chunk, chunk), chunk)
-            near = pl.ds(pl.multiple_of(slot % 2 * 2 * quarter + index * chunk, chunk), chunk)
+            spot = pl.ds(index * chunk, chunk)
+            rows = pl.ds(slot * 2 * quarter + index * chunk, chunk)
+            near = pl.ds(slot % 2 * 2 * quarter + index * chunk, chunk)
             mine = core == slot // 2
             side = [jnp.where(mine, own[place, near, :], got[place, near, :]) for place in range(2)]
             weight = ends[rows, :]
@@ -971,7 +972,8 @@
                 low[slot, spot, columns] = two
             return 0
 
-        lax.fori_loop(0, 2 * quarter // chunk, step, 0)
+        for index in range(2 * quarter // chunk):
+            step(index, 0)
         upper = stages[slot * 2 * quarter : (slot + 1) * 2 * quarter, :]
         lower = stages[(4 + slot) * 2 * quarter : (5 + slot) * 2 * quarter, :]
         middle[slot] = dot(upper, high[slot]) + dot(upper, low[slot]) + dot(lower, high[slot])

time: 63.9 us -> 63.3 us (level)
    pallas_call x21, Pallas kernels: 32.3 us -> 31.7 us  [call(): pl.pallas_call(kernel, out_shape=outs, in_specs=specs, out_specs=[pl.Bloc...]
where the time goes in v5:
time: 63.3 us; the launch traced here: 63.1 us
  Pallas kernels  31.7 us (50%)
  waiting for transfers between devices  17.2 us (27%)
  starting transfers between devices  13.8 us (22%)
    pallas_call x21, Pallas kernels, call(): pl.pallas_call(kernel, out_shape=outs, in_specs=specs, out_specs=[pl.Bloc...  31.7 us
    ppermute x7, waiting for transfers between devices, hop(): lax.ppermute(values, axis, [(index, index ^ 1 << bit) for index in range(...  17.2 us
    ppermute x3, starting transfers between devices, between_chips(): return lax.ppermute(values, 'rad', route)  6.81 us
    ppermute x7, starting transfers between devices, hop(): lax.ppermute(values, axis, [(index, index ^ 1 << bit) for index in range(...  6.39 us
  transfers between devices with their start and end apart: 12, of which 6 were waited for; matrix products, arithmetic and copies ran while one was open for 0% of the time, Pallas kernels for 34%

profile of v5, /device:TPU:0, one launch (start us, length us, event | category | flops | bytes accessed | tf_op | source)
XLA Modules:
  0.0 63.1 jit_solution(13697816680926851378)
XLA Ops:
  0.0 0.0 copy-start.7
  0.0 0.0 copy-start.1
  0.0 0.0 copy-start.8
  0.0 0.0 copy-start.11
  0.0 0.0 copy-start.10
  0.0 0.0 copy-start.9
  0.0 4.5 %forward.1 = (f32[4,1024,128]{2,1,0:T(8,128)}, f32[2,512,128]{2,1,0:T(8,128)S(1)}, f32[2,512,128]{2,1,0:T(8,128)S(1)}) custom-call(f32[8,512,128]{2,1,0:T(8,128)} %bitcast.2, f32[1032,128]{1,0:T(8,128)} %constant.23.clone.tables_in, bf16[2304,256]{1,0:T(8,128)(2,1)} %constant.28.clone.stages_in, f32[32]{0:T(128)} %rest_0_.13, f32[32]{0:T(128)} %rest_1_.10, ...), custom_call_target="tpu_custom_call" | custom-call | bytes 29520000 | tf_op jit(solution)/shard_map/forward/pallas_call | solution.py:1023
  4.5 0.5 collective-permute-start
  5.0 0.0 copy-done.7
  5.0 0.0 copy-done.1
  5.0 0.0 copy-done.8
  5.0 0.0 copy-done.11
  5.1 0.0 copy-done.10
  5.1 0.0 copy-done.9
  5.1 1.6 %pair_ports.1.ports = f32[11,512,128]{2,1,0:T(8,128)S(1)} custom-call(f32[1024,128]{1,0:T(8,128)S(1)} %copy-done.1, f32[8,128]{1,0:T(8,128)S(1)} %copy-done.7, f32[32]{0:T(128)S(1)} %copy-done.9, f32[32]{0:T(128)S(1)} %copy-done.8, f32[32]{0:T(128)S(1)} %copy-done.10, f32[32]{0:T(128)S(1)} %copy-done.11), custom_call_target="tpu_custom_call" | custom-call | bytes 7380000 | tf_op jit(solution)/shard_map/pair_ports/pallas_call | solution.py:1023
  6.7 0.0 copy-start.4
  6.7 0.0 collective-permute-done.got
  6.7 0.0 copy-start.5
  6.7 0.0 copy-start.6
  6.7 0.0 copy-start.12
  6.7 0.0 copy-start
  6.7 0.0 copy-start.2
  6.8 0.3 merge.1
  7.1 4.8 %collective-permute-start.7 = (f32[512,128]{1,0:T(8,128)S(1)}, f32[512,128]{1,0:T(8,128)S(1)}, u32[]{:S(2)}, u32[]{:S(2)}) collective-permute-start(f32[512,128]{1,0:T(8,128)S(1)} %get-tuple-element.53), channel_id=1, source_target_pairs={{0,2},{1,3},{6,4},{7,5},{8,10},{9,11},{14,12},{15,13},{16,18},{17,... | collective-permute-start | bytes 786440 | tf_op jit(solution)/shard_map/ppermute | solution.py:1047
  11.9 0.0 copy-done.4
  11.9 3.1 %ratios.1 = (f32[2,640,128]{2,1,0:T(8,128)S(1)}, f32[32,640,128]{2,1,0:T(8,128)S(1)}) custom-call(f32[640,128]{1,0:T(8,128)S(1)} %copy-done.4, f32[8,128]{1,0:T(8,128)S(1)} %copy-done.7, f32[32]{0:T(128)S(1)} %copy-done.9, f32[32]{0:T(128)S(1)} %copy-done.8, f32[32]{0:T(128)S(1)} %copy-done.10, f32[32]{0:T(128)S(1)} %copy-done.11), custom_call_target="tpu_custom_call" | custom-call | bytes 18450000 | tf_op jit(solution)/shard_map/ratios/pallas_call | solution.py:1023
  15.1 0.0 copy-done.5
  15.1 0.0 copy-done.6
  15.1 0.0 copy-done.12
  15.1 4.1 %response.1 = f32[2,32,128]{2,1,0:T(8,128)S(1)} custom-call(f32[256,128]{1,0:T(8,128)S(1)} %copy-done.6, f32[256,128]{1,0:T(8,128)S(1)} %copy-done.5, f32[4,128]{1,0:T(4,128)S(1)} %copy-done.12, f32[32]{0:T(128)S(1)} %copy-done.9, f32[32]{0:T(128)S(1)} %copy-done.8, f32[32]{0:T(128)S(1)} %copy-done.10, f32[32]{0:T(128)S(1)} %copy-done.11), custom_call_target="tpu_custom_call" | custom-call | bytes 18450000 | tf_op jit(solution)/shard_map/response/pallas_call | solution.py:1023
  19.1 0.0 copy-done
  19.2 0.0 copy-done.2
  19.2 3.0 %ends.4.own = f32[4,32,128]{2,1,0:T(8,128)S(1)} custom-call(f32[2,32,128]{2,1,0:T(8,128)S(1)} %response.1, f32[4,1024,128]{2,1,0:T(8,128)S(1)} %copy-done, f32[1024,128]{1,0:T(8,128)S(1)} %copy-done.1, f32[1024,128]{1,0:T(8,128)S(1)} %copy-done.2, f32[8,128]{1,0:T(8,128)S(1)} %copy-done.7, f32[32]{0:T(128)S(1)} %copy-done.9, f32[32]{0:T(128)S(1)} %copy-done.8, ...), custom_call_target="tpu_custom_call" | custom-call | bytes 11070000 | tf_op jit(solution)/shard_map/ends/pallas_call | solution.py:1023
  22.1 0.1 collective-permute-start.1
  22.2 4.3 %collective-permute-done.1.other = f32[4,32,128]{2,1,0:T(8,128)S(1)} collective-permute-done((f32[4,32,128]{2,1,0:T(8,128)S(1)}, f32[4,32,128]{2,1,0:T(8,128)S(1)}, u32[]{:S(2)}, u32[]{:S(2)}) %collective-permute-start.1) | collective-permute-done | bytes 65568 | tf_op jit(solution)/shard_map/ppermute | solution.py:1052
  26.5 0.7 %collective-permute-start.2 = (f32[6,32,128]{2,1,0:T(8,128)S(1)}, f32[6,32,128]{2,1,0:T(8,128)S(1)}, u32[]{:S(2)}, u32[]{:S(2)}) collective-permute-start(f32[6,32,128]{2,1,0:T(8,128)S(1)} %join.5.own), channel_id=1, source_target_pairs={{0,4},{1,5},{2,6},{3,7},{4,0},{5,1},{6,2},{7,3},{8,12},{9,13},{10,... | collective-permute-start | bytes 294920 | tf_op jit(solution)/shard_map/ppermute | solution.py:1052
  27.2 0.3 links.1
  27.5 0.0 collective-permute-done.7.incoming
  27.5 0.2 inward.1.own
  27.7 0.7 %collective-permute-start.8 = (f32[512,128]{1,0:T(8,128)S(1)}, f32[512,128]{1,0:T(8,128)S(1)}, u32[]{:S(2)}, u32[]{:S(2)}) collective-permute-start(f32[512,128]{1,0:T(8,128)S(1)} %inward.1.own), channel_id=1, source_target_pairs={{2,4},{3,5},{4,2},{5,3},{10,12},{11,13},{12,10},{13,11},{18,20},{1... | collective-permute-start | bytes 786440 | tf_op jit(solution)/shard_map/ppermute | solution.py:1047
  28.4 5.0 %collective-permute-done.2.other = f32[6,32,128]{2,1,0:T(8,128)S(1)} collective-permute-done((f32[6,32,128]{2,1,0:T(8,128)S(1)}, f32[6,32,128]{2,1,0:T(8,128)S(1)}, u32[]{:S(2)}, u32[]{:S(2)}) %collective-permute-start.2) | collective-permute-done | bytes 98336 | tf_op jit(solution)/shard_map/ppermute | solution.py:1052
  33.4 0.1 collective-permute-start.3
  33.5 1.4 %collective-permute-done.3.other = f32[10,32,128]{2,1,0:T(8,128)S(1)} collective-permute-done((f32[10,32,128]{2,1,0:T(8,128)S(1)}, f32[10,32,128]{2,1,0:T(8,128)S(1)}, u32[]{:S(2)}, u32[]{:S(2)}) %collective-permute-start.3) | collective-permute-done | bytes 163872 | tf_op jit(solution)/shard_map/ppermute | solution.py:1052
  34.9 1.5 %collective-permute-start.4 = (f32[2,32,128]{2,1,0:T(8,128)S(1)}, f32[2,32,128]{2,1,0:T(8,128)S(1)}, u32[]{:S(2)}, u32[]{:S(2)}) collective-permute-start(f32[2,32,128]{2,1,0:T(8,128)S(1)} %slice.4.own), channel_id=1, source_target_pairs={{0,8},{8,0},{16,24},{24,16},{1,9},{9,1},{17,25},{25,17},{2,10},{10... | collective-permute-start | bytes 98312 | tf_op jit(solution)/shard_map/ppermute | solution.py:1052
  36.5 3.1 %capacity.1 = (f32[32,8,128]{2,1,0:T(8,128)S(1)}, f32[32,8,128]{2,1,0:T(8,128)S(1)}, f32[32,8,128]{2,1,0:T(8,128)S(1)}) custom-call(f32[32]{0:T(128)S(1)} %copy-done.8, f32[18,32,128]{2,1,0:T(8,128)S(1)} %join.7.responses), custom_call_target="tpu_custom_call" | custom-call | bytes 14760000 | tf_op jit(solution)/shard_map/capacity/pallas_call | solution.py:1023
  39.6 0.0 collective-permute-done.4.other
  39.6 0.0 collective-permute-done.8.other
  39.7 0.2 middle.1
  39.9 1.3 %collective-permute-start.9 = (f32[512,128]{1,0:T(8,128)S(1)}, f32[512,128]{1,0:T(8,128)S(1)}, u32[]{:S(2)}, u32[]{:S(2)}) collective-permute-start(f32[512,128]{1,0:T(8,128)S(1)} %get-tuple-element.57), channel_id=1, source_target_pairs={{2,0},{3,1},{4,6},{5,7},{10,8},{11,9},{12,14},{13,15},{18,16},{19,... | collective-permute-start | bytes 786440 | tf_op jit(solution)/shard_map/ppermute | solution.py:1047
  41.2 1.6 %collective-permute-start.5 = (f32[4,32,128]{2,1,0:T(8,128)S(1)}, f32[4,32,128]{2,1,0:T(8,128)S(1)}, u32[]{:S(2)}, u32[]{:S(2)}) collective-permute-start(f32[4,32,128]{2,1,0:T(8,128)S(1)} %join.8.own), channel_id=1, source_target_pairs={{0,16},{8,24},{16,0},{24,8},{1,17},{9,25},{17,1},{25,9},{2,18},{10... | collective-permute-start | bytes 196616 | tf_op jit(solution)/shard_map/ppermute | solution.py:1052
  42.8 2.1 %pair.1.pair_matrix = f32[32,8,128]{2,1,0:T(8,128)S(1)} custom-call(f32[32]{0:T(128)S(1)} %copy-done.8, f32[32,8,128]{2,1,0:T(8,128)S(1)} %get-tuple-element.43.minus_matrix, f32[32,8,128]{2,1,0:T(8,128)S(1)} %get-tuple-element.47.plus_matrix), custom_call_target="tpu_custom_call" | custom-call | bytes 11070000 | tf_op jit(solution)/shard_map/pair/pallas_call | solution.py:1023
  44.9 0.6 %collective-permute-done.5.other = f32[4,32,128]{2,1,0:T(8,128)S(1)} collective-permute-done((f32[4,32,128]{2,1,0:T(8,128)S(1)}, f32[4,32,128]{2,1,0:T(8,128)S(1)}, u32[]{:S(2)}, u32[]{:S(2)}) %collective-permute-start.5) | collective-permute-done | bytes 65568 | tf_op jit(solution)/shard_map/ppermute | solution.py:1052
  45.5 1.2 %slabs.1 = (f32[4,32,128]{2,1,0:T(8,128)S(1)}, f32[4,32,128]{2,1,0:T(8,128)S(1)}) custom-call(f32[32]{0:T(128)S(1)} %copy-done.8, f32[32,8,128]{2,1,0:T(8,128)S(1)} %get-tuple-element.43.minus_matrix, f32[32,8,128]{2,1,0:T(8,128)S(1)} %get-tuple-element.44.alternate_matrix, f32[32,8,128]{2,1,0:T(8,128)S(1)} %pair.1.pair_matrix, f32[8,32,128]{2,1,0:T(8,128)S(1)} %join.9.rest_0_), custom_call_target="tpu_custom_call" | custom-call | bytes 7380000 | tf_op jit(solution)/shard_map/slabs/pallas_call | solution.py:1023
  46.7 1.6 %collective-permute-start.6 = (f32[4,32,128]{2,1,0:T(8,128)S(1)}, f32[4,32,128]{2,1,0:T(8,128)S(1)}, u32[]{:S(2)}, u32[]{:S(2)}) collective-permute-start(f32[4,32,128]{2,1,0:T(8,128)S(1)} %get-tuple-element.50), channel_id=1, source_target_pairs={{0,16},{8,24},{16,0},{24,8},{1,17},{9,25},{17,1},{25,9},{2,18},{10... | collective-permute-start | bytes 196616 | tf_op jit(solution)/shard_map/ppermute | solution.py:1052
  48.3 2.7 %collective-permute-done.6.other = f32[4,32,128]{2,1,0:T(8,128)S(1)} collective-permute-done((f32[4,32,128]{2,1,0:T(8,128)S(1)}, f32[4,32,128]{2,1,0:T(8,128)S(1)}, u32[]{:S(2)}, u32[]{:S(2)}) %collective-permute-start.6) | collective-permute-done | bytes 65568 | tf_op jit(solution)/shard_map/ppermute | solution.py:1052
  51.1 0.0 collective-permute-done.9.near_two
  51.1 0.5 parts.1
  51.6 0.1 collective-permute-start.10
  51.6 0.8 %collective-permute-start.11 = (f32[2,32,128]{2,1,0:T(8,128)S(1)}, f32[2,32,128]{2,1,0:T(8,128)S(1)}, u32[]{:S(2)}, u32[]{:S(2)}) collective-permute-start(f32[2,32,128]{2,1,0:T(8,128)S(1)} %get-tuple-element.51), channel_id=1, source_target_pairs={{0,8},{8,0},{16,24},{24,16},{1,9},{9,1},{17,25},{25,17},{2,10},{10... | collective-permute-start | bytes 98312 | tf_op jit(solution)/shard_map/ppermute | solution.py:1052
  52.4 3.2 %collective-permute-done.11.rest_5_ = f32[2,32,128]{2,1,0:T(8,128)S(1)} collective-permute-done((f32[2,32,128]{2,1,0:T(8,128)S(1)}, f32[2,32,128]{2,1,0:T(8,128)S(1)}, u32[]{:S(2)}, u32[]{:S(2)}) %collective-permute-start.11) | collective-permute-done | bytes 32800 | tf_op jit(solution)/shard_map/ppermute | solution.py:1052
  55.6 2.9 %sides.1 = (f32[2,32,128]{2,1,0:T(8,128)S(1)}, f32[2,1024,128]{2,1,0:T(8,128)S(1)}) custom-call(f32[1024,128]{1,0:T(8,128)S(1)} %copy-done.1, f32[1024,128]{1,0:T(8,128)S(1)} %copy-done.2, f32[8,128]{1,0:T(8,128)S(1)} %copy-done.7, f32[32]{0:T(128)S(1)} %copy-done.9, f32[32]{0:T(128)S(1)} %copy-done.8, f32[32]{0:T(128)S(1)} %copy-done.10, f32[32]{0:T(128)S(1)} %copy-done.11, ...), custom_call_target="tpu_custom_call" | custom-call | bytes 11070000 | tf_op jit(solution)/shard_map/sides/pallas_call | solution.py:1023
  58.5 0.0 collective-permute-done.10.got
  58.5 0.0 copy-done.3
  58.5 4.6 %backward.1 = f32[4096,128]{1,0:T(8,128)} custom-call(f32[4,1024,128]{2,1,0:T(8,128)S(1)} %copy-done, f32[2,512,128]{2,1,0:T(8,128)S(1)} %get-tuple-element.58.own, f32[2,512,128]{2,1,0:T(8,128)S(1)} %collective-permute-done.10.got, f32[2,1024,128]{2,1,0:T(8,128)S(1)} %get-tuple-element.61.extra, f32[2,32,128]{2,1,0:T(8,128)S(1)} %get-tuple-element.62.sources, ...), custom_call_target="tpu_custom_call" | custom-call | bytes 25830000 | tf_op jit(solution)/shard_map/backward/pallas_call | solution.py:1023
  (8 shorter events, 0.1 us)
Async XLA Ops:
  0.0 5.0 %copy-start.7 = (f32[8,128]{1,0:T(8,128)S(1)}, f32[8,128]{1,0:T(8,128)}, u32[]{:S(2)}) copy-start(f32[8,128]{1,0:T(8,128)} %constant.22.clone.mu) | copy-start | bytes 12292
  0.0 5.0 %copy-start.1 = (f32[1024,128]{1,0:T(8,128)S(1)}, f32[1024,128]{1,0:T(8,128)}, u32[]{:S(2)}) copy-start(f32[1024,128]{1,0:T(8,128)} %constant.20.clone.lam) | copy-start | bytes 1572868
  0.0 5.0 %copy-start.8 = (f32[32]{0:T(128)S(1)}, f32[32]{0:T(128)}, u32[]{:S(2)}) copy-start(f32[32]{0:T(128)} %rest_1_.10) | copy-start | bytes 388
  0.0 5.0 %copy-start.11 = (f32[32]{0:T(128)S(1)}, f32[32]{0:T(128)}, u32[]{:S(2)}) copy-start(f32[32]{0:T(128)} %rest_3_.13) | copy-start | bytes 388
  0.0 5.0 %copy-start.10 = (f32[32]{0:T(128)S(1)}, f32[32]{0:T(128)}, u32[]{:S(2)}) copy-start(f32[32]{0:T(128)} %rest_2_.13) | copy-start | bytes 388
  0.0 5.1 %copy-start.9 = (f32[32]{0:T(128)S(1)}, f32[32]{0:T(128)}, u32[]{:S(2)}) copy-start(f32[32]{0:T(128)} %rest_0_.13) | copy-start | bytes 388
  4.5 2.2 %collective-permute-start = (f32[2,512,128]{2,1,0:T(8,128)S(1)}, f32[2,512,128]{2,1,0:T(8,128)S(1)}, u32[]{:S(2)}, u32[]{:S(2)}) collective-permute-start(f32[2,512,128]{2,1,0:T(8,128)S(1)} %get-tuple-element.36), channel_id=1, source_target_pairs={{0,1},{1,0},{2,3},{3,2},{4,5},{5,4},{6,7},{7,6},{8,9},{9,8},{10,11... | collective-permute-start | bytes 1572872 | tf_op jit(solution)/shard_map/ppermute | solution.py:1042
  6.7 5.2 %copy-start.4 = (f32[640,128]{1,0:T(8,128)S(1)}, f32[640,128]{1,0:T(8,128)}, u32[]{:S(2)}) copy-start(f32[640,128]{1,0:T(8,128)} %constant.24.clone.lam) | copy-start | bytes 983044
  6.7 8.4 %copy-start.5 = (f32[256,128]{1,0:T(8,128)S(1)}, f32[256,128]{1,0:T(8,128)}, u32[]{:S(2)}) copy-start(f32[256,128]{1,0:T(8,128)} %constant.27.clone.weight) | copy-start | bytes 393220
  6.7 8.4 %copy-start.6 = (f32[256,128]{1,0:T(8,128)S(1)}, f32[256,128]{1,0:T(8,128)}, u32[]{:S(2)}) copy-start(f32[256,128]{1,0:T(8,128)} %constant.26.clone.lam) | copy-start | bytes 393220
  6.7 8.4 %copy-start.12 = (f32[4,128]{1,0:T(4,128)S(1)}, f32[4,128]{1,0:T(4,128)}, u32[]{:S(2)}) copy-start(f32[4,128]{1,0:T(4,128)} %constant.25.clone.mu) | copy-start | bytes 6148
  6.7 12.4 %copy-start = (f32[4,1024,128]{2,1,0:T(8,128)S(1)}, f32[4,1024,128]{2,1,0:T(8,128)}, u32[]{:S(2)}) copy-start(f32[4,1024,128]{2,1,0:T(8,128)} %get-tuple-element.34.spectrum) | copy-start | bytes 6291460
  6.7 12.4 %copy-start.2 = (f32[1024,128]{1,0:T(8,128)S(1)}, f32[1024,128]{1,0:T(8,128)}, u32[]{:S(2)}) copy-start(f32[1024,128]{1,0:T(8,128)} %constant.21.clone.ends) | copy-start | bytes 1572868
  7.1 20.4 %collective-permute-start.7 = (f32[512,128]{1,0:T(8,128)S(1)}, f32[512,128]{1,0:T(8,128)S(1)}, u32[]{:S(2)}, u32[]{:S(2)}) collective-permute-start(f32[512,128]{1,0:T(8,128)S(1)} %get-tuple-element.53), channel_id=1, source_target_pairs={{0,2},{1,3},{6,4},{7,5},{8,10},{9,11},{14,12},{15,13},{16,18},{17,... | collective-permute-start | bytes 786440 | tf_op jit(solution)/shard_map/ppermute | solution.py:1047
  22.1 4.3 %collective-permute-start.1 = (f32[4,32,128]{2,1,0:T(8,128)S(1)}, f32[4,32,128]{2,1,0:T(8,128)S(1)}, u32[]{:S(2)}, u32[]{:S(2)}) collective-permute-start(f32[4,32,128]{2,1,0:T(8,128)S(1)} %ends.4.own), channel_id=1, source_target_pairs={{0,2},{1,3},{2,0},{3,1},{4,6},{5,7},{6,4},{7,5},{8,10},{9,11},{10,... | collective-permute-start | bytes 196616 | tf_op jit(solution)/shard_map/ppermute | solution.py:1052
  26.5 6.9 %collective-permute-start.2 = (f32[6,32,128]{2,1,0:T(8,128)S(1)}, f32[6,32,128]{2,1,0:T(8,128)S(1)}, u32[]{:S(2)}, u32[]{:S(2)}) collective-permute-start(f32[6,32,128]{2,1,0:T(8,128)S(1)} %join.5.own), channel_id=1, source_target_pairs={{0,4},{1,5},{2,6},{3,7},{4,0},{5,1},{6,2},{7,3},{8,12},{9,13},{10,... | collective-permute-start | bytes 294920 | tf_op jit(solution)/shard_map/ppermute | solution.py:1052
  27.7 11.9 %collective-permute-start.8 = (f32[512,128]{1,0:T(8,128)S(1)}, f32[512,128]{1,0:T(8,128)S(1)}, u32[]{:S(2)}, u32[]{:S(2)}) collective-permute-start(f32[512,128]{1,0:T(8,128)S(1)} %inward.1.own), channel_id=1, source_target_pairs={{2,4},{3,5},{4,2},{5,3},{10,12},{11,13},{12,10},{13,11},{18,20},{1... | collective-permute-start | bytes 786440 | tf_op jit(solution)/shard_map/ppermute | solution.py:1047
  33.4 1.5 %collective-permute-start.3 = (f32[10,32,128]{2,1,0:T(8,128)S(1)}, f32[10,32,128]{2,1,0:T(8,128)S(1)}, u32[]{:S(2)}, u32[]{:S(2)}) collective-permute-start(f32[10,32,128]{2,1,0:T(8,128)S(1)} %join.6.own), channel_id=1, source_target_pairs={{0,1},{1,0},{2,3},{3,2},{4,5},{5,4},{6,7},{7,6},{8,9},{9,8},{10,11... | collective-permute-start | bytes 491528 | tf_op jit(solution)/shard_map/ppermute | solution.py:1052
  34.9 4.7 %collective-permute-start.4 = (f32[2,32,128]{2,1,0:T(8,128)S(1)}, f32[2,32,128]{2,1,0:T(8,128)S(1)}, u32[]{:S(2)}, u32[]{:S(2)}) collective-permute-start(f32[2,32,128]{2,1,0:T(8,128)S(1)} %slice.4.own), channel_id=1, source_target_pairs={{0,8},{8,0},{16,24},{24,16},{1,9},{9,1},{17,25},{25,17},{2,10},{10... | collective-permute-start | bytes 98312 | tf_op jit(solution)/shard_map/ppermute | solution.py:1052
  39.9 11.2 %collective-permute-start.9 = (f32[512,128]{1,0:T(8,128)S(1)}, f32[512,128]{1,0:T(8,128)S(1)}, u32[]{:S(2)}, u32[]{:S(2)}) collective-permute-start(f32[512,128]{1,0:T(8,128)S(1)} %get-tuple-element.57), channel_id=1, source_target_pairs={{2,0},{3,1},{4,6},{5,7},{10,8},{11,9},{12,14},{13,15},{18,16},{19,... | collective-permute-start | bytes 786440 | tf_op jit(solution)/shard_map/ppermute | solution.py:1047
  41.2 4.3 %collective-permute-start.5 = (f32[4,32,128]{2,1,0:T(8,128)S(1)}, f32[4,32,128]{2,1,0:T(8,128)S(1)}, u32[]{:S(2)}, u32[]{:S(2)}) collective-permute-start(f32[4,32,128]{2,1,0:T(8,128)S(1)} %join.8.own), channel_id=1, source_target_pairs={{0,16},{8,24},{16,0},{24,8},{1,17},{9,25},{17,1},{25,9},{2,18},{10... | collective-permute-start | bytes 196616 | tf_op jit(solution)/shard_map/ppermute | solution.py:1052
  46.7 4.3 %collective-permute-start.6 = (f32[4,32,128]{2,1,0:T(8,128)S(1)}, f32[4,32,128]{2,1,0:T(8,128)S(1)}, u32[]{:S(2)}, u32[]{:S(2)}) collective-permute-start(f32[4,32,128]{2,1,0:T(8,128)S(1)} %get-tuple-element.50), channel_id=1, source_target_pairs={{0,16},{8,24},{16,0},{24,8},{1,17},{9,25},{17,1},{25,9},{2,18},{10... | collective-permute-start | bytes 196616 | tf_op jit(solution)/shard_map/ppermute | solution.py:1052
  51.6 7.0 %collective-permute-start.10 = (f32[2,512,128]{2,1,0:T(8,128)S(1)}, f32[2,512,128]{2,1,0:T(8,128)S(1)}, u32[]{:S(2)}, u32[]{:S(2)}) collective-permute-start(f32[2,512,128]{2,1,0:T(8,128)S(1)} %get-tuple-element.59), channel_id=1, source_target_pairs={{0,1},{1,0},{2,3},{3,2},{4,5},{5,4},{6,7},{7,6},{8,9},{9,8},{10,11... | collective-permute-start | bytes 1572872 | tf_op jit(solution)/shard_map/ppermute | solution.py:1042
  51.6 4.0 %collective-permute-start.11 = (f32[2,32,128]{2,1,0:T(8,128)S(1)}, f32[2,32,128]{2,1,0:T(8,128)S(1)}, u32[]{:S(2)}, u32[]{:S(2)}) collective-permute-start(f32[2,32,128]{2,1,0:T(8,128)S(1)} %get-tuple-element.51), channel_id=1, source_target_pairs={{0,8},{8,0},{16,24},{24,16},{1,9},{9,1},{17,25},{25,17},{2,10},{10... | collective-permute-start | bytes 98312 | tf_op jit(solution)/shard_map/ppermute | solution.py:1052
  55.6 2.9 %copy-start.3 = (bf16[2304,256]{1,0:T(8,128)(2,1)S(1)}, bf16[2304,256]{1,0:T(8,128)(2,1)}, u32[]{:S(2)}) copy-start(bf16[2304,256]{1,0:T(8,128)(2,1)} %constant.29.clone.stages) | copy-start | bytes 3538948
